TPU v7x, 1024 devices: a whole 4x4x32 slice. The times are simulated.
1024 devices in a mesh: pp: 32 (over y, z_lo), ep: 32 (over x, z_hi, core).
Axes of the slice: x: 4, y: 4, z: 32 (z_hi: 4, z_lo: 8; z = z_hi * 8 + z_lo), core: 2. Of those that a mesh axis runs over, the one named last changes fastest.
Arguments:
- fwd_in: bfloat16 [32, 2048, 3584], P('pp', 'ep'), may hold values from -6 to 6
- fwd_route: int32 [32, 2048, 1], P('pp', 'ep'), may hold values from 0 to 8, as said below
- fwd_gate: float32 [32, 2048, 1], P('pp', 'ep'), may hold values from 0.25 to 1.5
- bwd_cot: bfloat16 [32, 2048, 3584], P('pp', 'ep'), may hold values from -6 to 6
- bwd_route: int32 [32, 2048, 1], P('pp', 'ep'), may hold values from 0 to 8, as said below
- bwd_gate: float32 [32, 2048, 1], P('pp', 'ep'), may hold values from 0.25 to 1.5
- saved_pre: bfloat16 [32, 32, 128, 512], P('pp', 'ep'), may hold values from -6 to 6
- w_gate_up: bfloat16 [32, 3584, 512], P('ep'), may hold values from -0.09375 to 0.09375
- w_down: bfloat16 [32, 256, 3584], P('ep'), may hold values from -0.1875 to 0.1875
Outputs:
- fwd_next: bfloat16 [32, 2048, 3584], P('pp', 'ep')
- bwd_prev: bfloat16 [32, 2048, 3584], P('pp', 'ep')
Inputs may be any that keep to these rules, and one draw needn't show every extreme that they name: `fwd_route`: in each section, among the 64 tokens of one index of ep, every expert is named by 1 to 4 tokens and one expert by exactly 4; the other tokens hold 8. `bwd_route`: in each section, among the 64 tokens of one index of ep, every expert is named by 1 to 4 tokens and one expert by exactly 4; the other tokens hold 8.
All inputs are finite; a program needn't handle non-finite values.
Results may differ from a plain program's by a relative error of at most 0.008.
Values may be sent and summed in bfloat16 or wider, within the bound.
No kernel may reach another device: no remote copies, remote signals or barrier semaphores. Data moves between devices by JAX's collectives and lax.ppermute only.
A program may use at most 32 MiB of HBM per device.

v0:
```python
import jax
import jax.numpy as jnp
from jax import lax
from jax.sharding import PartitionSpec as P

FFW = 1024


def from_behind(block, axis, distance):
    devices = range(lax.axis_size(axis))
    route = [((i - distance) % len(devices), i) for i in devices]
    return lax.ppermute(block, axis, route)


def placement_of(route, experts, capacity):
    onehot = (route[:, None] == jnp.arange(experts, dtype=jnp.int32)[None, :]).astype(jnp.int32)
    before = jnp.cumsum(onehot, axis=0) - onehot
    slot = jnp.sum(before * onehot, axis=1)
    routed = route < experts
    index = jnp.where(routed, route * capacity + slot, experts * capacity)
    table = (index[:, None] == jnp.arange(experts * capacity, dtype=jnp.int32)[None, :]).astype(
        jnp.bfloat16
    )
    return (index, routed, table)


def dispatch(rows, table, experts, capacity, split):
    tokens, width = rows.shape
    packed = lax.dot_general(
        table, rows, (((0,), (0,)), ((), ())), preferred_element_type=jnp.float32
    ).astype(jnp.bfloat16)
    packed = jnp.repeat(packed.reshape(experts, capacity, width), split, axis=0)
    arrived = lax.all_to_all(packed, "ep", split_axis=0, concat_axis=0, tiled=True)
    return arrived.reshape(1, -1, width)


def combine(partial_value, index, routed, experts, capacity, split):
    width = partial_value.shape[1]
    arrived = lax.all_to_all(
        partial_value.reshape(experts * split, capacity, width),
        "ep",
        split_axis=0,
        concat_axis=0,
        tiled=True,
    )
    summed = jnp.sum(arrived.reshape(experts, split, capacity, width).astype(jnp.float32), axis=1)
    safe = jnp.minimum(index, experts * capacity - 1)
    picked = jnp.take(summed.reshape(experts * capacity, width), safe, axis=0)
    return jnp.where(routed[:, None], picked, 0.0)


def shards(fwd_in, fwd_route, fwd_gate, bwd_cot, bwd_route, bwd_gate, saved_pre, w_gate_up, w_down):
    ep_count = lax.axis_size("ep")
    hid = w_down.shape[1]
    split = FFW // hid
    experts = ep_count // split
    capacity = saved_pre.shape[2] // ep_count
    weight_gu = w_gate_up[0]
    weight_dn = w_down[0]
    width = weight_gu.shape[0]
    x_rows = fwd_in[0]
    index_f, routed_f, table_f = placement_of(fwd_route[0, :, 0], experts, capacity)
    arrived_x = dispatch(x_rows, table_f, experts, capacity, split)
    parts = arrived_x.shape[0]
    pre = jnp.einsum(
        "jrk,jkh->rh",
        arrived_x,
        weight_gu.reshape(parts, width // parts, 2 * hid),
        preferred_element_type=jnp.float32,
    )
    hidden = (jax.nn.silu(pre[:, :hid]) * pre[:, hid:]).astype(jnp.bfloat16)
    partial_value = jnp.dot(hidden, weight_dn, preferred_element_type=jnp.float32).astype(
        jnp.bfloat16
    )
    expert_out = combine(partial_value, index_f, routed_f, experts, capacity, split)
    out_rows = (x_rows.astype(jnp.float32) + fwd_gate[0] * expert_out).astype(jnp.bfloat16)
    fwd_next = from_behind(out_rows[None], "pp", 1)
    cot = bwd_cot[0]
    index_b, routed_b, table_b = placement_of(bwd_route[0, :, 0], experts, capacity)
    scaled = (bwd_gate[0] * cot.astype(jnp.float32)).astype(jnp.bfloat16)
    arrived_u = dispatch(scaled, table_b, experts, capacity, split)
    dh = jnp.einsum(
        "jrk,hjk->rh",
        arrived_u,
        weight_dn.reshape(hid, parts, width // parts),
        preferred_element_type=jnp.float32,
    )
    saved = saved_pre[0, 0].astype(jnp.float32)
    act = saved[:, :hid]
    lin = saved[:, hid:]
    sig = jax.nn.sigmoid(act)
    d_act = (dh * lin * sig * (1.0 + act * (1.0 - sig))).astype(jnp.bfloat16)
    d_lin = (dh * act * sig).astype(jnp.bfloat16)
    grads = jnp.concatenate([d_act, d_lin], axis=1)
    back = lax.dot_general(
        grads, weight_gu, (((1,), (1,)), ((), ())), preferred_element_type=jnp.float32
    ).astype(jnp.bfloat16)
    grad_rows = (
        cot.astype(jnp.float32) + combine(back, index_b, routed_b, experts, capacity, split)
    ).astype(jnp.bfloat16)
    bwd_prev = from_behind(grad_rows[None], "pp", -1)
    return (fwd_next, bwd_prev)


def solution(mesh):
    placed = (
        P("pp", "ep", None),
        P("pp", "ep", None),
        P("pp", "ep", None),
        P("pp", "ep", None),
        P("pp", "ep", None),
        P("pp", "ep", None),
        P("pp", "ep", None, None),
        P("ep", None, None),
        P("ep", None, None),
    )
    return jax.shard_map(
        shards,
        mesh=mesh,
        in_specs=placed,
        out_specs=(P("pp", "ep", None), P("pp", "ep", None)),
        check_vma=False,
    )
```

profile of v0, /device:TPU:70, one launch (start us, length us, event | category | flops | bytes accessed | tf_op | source)
XLA Modules:
  0.0 457.2 jit_solution(13138944397101807397)
XLA Ops:
  0.6 0.0 copy-start
  0.6 0.9 fusion.26
  1.5 0.1 reduce_window_sum.18
  1.6 0.8 select_reduce_fusion
  2.4 0.7 compare_and_fusion
  3.1 1.4 convolution_convert_fusion.2
  4.5 0.0 copy-start.3
  4.5 0.0 copy-start.1
  4.5 0.1 reshape.100
  4.6 1.2 broadcast_in_dim.58
  5.7 29.7 %all-to-all-start.2 = ((bf16[32,4,3584]{2,1,0:T(4,128)(2,1)}), bf16[32,4,3584]{2,1,0:T(4,128)(2,1)S(1)}, u32[]{:S(2)}, u32[]{:S(2)}) async-start(bf16[32,4,3584]{2,1,0:T(4,128)(2,1)} %bitcast.50), calls=%async_computation.2 | async-start | bytes 1835008 | tf_op jit(solution)/shard_map/all_to_all | solution.py:33
  35.4 0.0 copy-done.3
  35.4 0.1 fusion.27
  35.5 0.1 reduce_window_sum.17
  35.6 0.2 select_reduce_fusion.1
  35.8 0.0 copy-done.1
  35.8 0.3 convolution_convert_fusion.3
  36.1 0.0 copy-start.2
  36.2 0.1 reshape.94
  36.2 80.0 %all-to-all-done.2 = bf16[32,4,3584]{2,1,0:T(4,128)(2,1)S(1)} async-done(((bf16[32,4,3584]{2,1,0:T(4,128)(2,1)}), bf16[32,4,3584]{2,1,0:T(4,128)(2,1)S(1)}, u32[]{:S(2)}, u32[]{:S(2)}) %all-to-all-start.2) | async-done | bytes 917536 | tf_op jit(solution)/shard_map/all_to_all | solution.py:33
  116.3 1.2 broadcast_in_dim.54
  117.5 22.5 %all-to-all-start = ((bf16[32,4,3584]{2,1,0:T(4,128)(2,1)}), bf16[32,4,3584]{2,1,0:T(4,128)(2,1)}, u32[]{:S(2)}, u32[]{:S(2)}) async-start(bf16[32,4,3584]{2,1,0:T(4,128)(2,1)} %bitcast.51), calls=%async_computation | async-start | bytes 1835008 | tf_op jit(solution)/shard_map/all_to_all | solution.py:33
  139.9 0.0 copy-done.2
  140.0 1.1 reshape.102
  141.1 0.0 copy-done
  141.1 1.9 fusion.19
  143.0 3.3 convolution_convert_fusion
  146.4 1.1 reshape.103
  147.5 65.5 %all-to-all-done = bf16[32,4,3584]{2,1,0:T(4,128)(2,1)} async-done(((bf16[32,4,3584]{2,1,0:T(4,128)(2,1)}), bf16[32,4,3584]{2,1,0:T(4,128)(2,1)}, u32[]{:S(2)}, u32[]{:S(2)}) %all-to-all-start) | async-done | bytes 917536 | tf_op jit(solution)/shard_map/all_to_all | solution.py:33
  213.0 99.9 %all-to-all-start.3 = ((bf16[32,4,3584]{2,1,0:T(4,128)(2,1)}), bf16[32,4,3584]{2,1,0:T(4,128)(2,1)}, u32[]{:S(2)}, u32[]{:S(2)}) async-start(bf16[32,4,3584]{2,1,0:T(4,128)(2,1)} %reshape.103), calls=%async_computation.3 | async-start | bytes 1835008 | tf_op jit(solution)/shard_map/all_to_all | solution.py:39
  312.9 1.7 reshape.96
  314.6 2.7 fusion.1
  317.3 0.4 convolution_convert_fusion.1
  317.7 1.1 reshape.98
  318.8 59.8 %all-to-all-done.3 = bf16[32,4,3584]{2,1,0:T(4,128)(2,1)} async-done(((bf16[32,4,3584]{2,1,0:T(4,128)(2,1)}), bf16[32,4,3584]{2,1,0:T(4,128)(2,1)}, u32[]{:S(2)}, u32[]{:S(2)}) %all-to-all-start.3) | async-done | bytes 917536 | tf_op jit(solution)/shard_map/all_to_all | solution.py:39
  378.7 18.6 %all-to-all-start.1 = ((bf16[32,4,3584]{2,1,0:T(4,128)(2,1)}), bf16[32,4,3584]{2,1,0:T(4,128)(2,1)}, u32[]{:S(2)}, u32[]{:S(2)}) async-start(bf16[32,4,3584]{2,1,0:T(4,128)(2,1)} %reshape.98), calls=%async_computation.1 | async-start | bytes 1835008 | tf_op jit(solution)/shard_map/all_to_all | solution.py:39
  397.3 1.7 convert_reduce_fusion
  399.0 0.2 reshape.104
  399.2 0.9 gather_fusion.1
  400.1 2.0 fusion.12
  402.1 1.9 collective-permute-start.1
  404.0 31.7 %all-to-all-done.1 = bf16[32,4,3584]{2,1,0:T(4,128)(2,1)} async-done(((bf16[32,4,3584]{2,1,0:T(4,128)(2,1)}), bf16[32,4,3584]{2,1,0:T(4,128)(2,1)}, u32[]{:S(2)}, u32[]{:S(2)}) %all-to-all-start.1) | async-done | bytes 917536 | tf_op jit(solution)/shard_map/all_to_all | solution.py:39
  435.7 1.7 convert_reduce_fusion.1
  437.4 0.2 reshape.99
  437.6 0.0 copy-start.4
  437.6 0.9 gather_fusion
  438.5 0.0 copy-done.4
  438.5 1.3 fusion.11
  439.7 2.1 collective-permute-start
  441.9 0.0 collective-permute-done.1
  441.9 12.7 %collective-permute-done = bf16[1,64,3584]{2,1,0:T(8,128)(2,1)S(1)} collective-permute-done((bf16[1,64,3584]{2,1,0:T(8,128)(2,1)S(1)}, bf16[1,64,3584]{2,1,0:T(8,128)(2,1)S(1)}, u32[]{:S(2)}, u32[]{:S(2)}) %collective-permute-start) | collective-permute-done | bytes 458784 | tf_op jit(solution)/shard_map/ppermute | solution.py:12
  454.6 0.8 copy.13
  455.3 1.8 copy.14
  (4 shorter events, 0.0 us)
Async XLA Ops:
  0.6 140.5 %copy-start = (bf16[1,256,3584]{2,1,0:T(8,128)(2,1)S(1)}, bf16[1,256,3584]{2,1,0:T(8,128)(2,1)}, u32[]{:S(2)}) copy-start(bf16[1,256,3584]{2,1,0:T(8,128)(2,1)} %param.19) | copy-start | bytes 5505028
  4.5 30.9 %copy-start.3 = (s32[1,64,1]{1,2,0:T(1,128)S(1)}, s32[1,64,1]{1,2,0:T(1,128)}, u32[]{:S(2)}) copy-start(s32[1,64,1]{1,2,0:T(1,128)} %param.12) | copy-start | bytes 772
  4.5 31.3 %copy-start.1 = (bf16[1,64,3584]{2,1,0:T(8,128)(2,1)S(1)}, bf16[1,64,3584]{2,1,0:T(8,128)(2,1)}, u32[]{:S(2)}) copy-start(bf16[1,64,3584]{2,1,0:T(8,128)(2,1)} %param.11) | copy-start | bytes 1376260
  5.7 110.5 %all-to-all-start.2 = ((bf16[32,4,3584]{2,1,0:T(4,128)(2,1)}), bf16[32,4,3584]{2,1,0:T(4,128)(2,1)S(1)}, u32[]{:S(2)}, u32[]{:S(2)}) async-start(bf16[32,4,3584]{2,1,0:T(4,128)(2,1)} %bitcast.50), calls=%async_computation.2 | async-start | bytes 1835008 | tf_op jit(solution)/shard_map/all_to_all | solution.py:33
  36.1 103.8 %copy-start.2 = (bf16[1,1,128,512]{3,2,1,0:T(8,128)(2,1)S(1)}, bf16[1,1,128,512]{3,2,1,0:T(8,128)(2,1)}, u32[]{:S(2)}) copy-start(bf16[1,1,128,512]{3,2,1,0:T(8,128)(2,1)} %param.17) | copy-start | bytes 393220
  117.5 95.5 %all-to-all-start = ((bf16[32,4,3584]{2,1,0:T(4,128)(2,1)}), bf16[32,4,3584]{2,1,0:T(4,128)(2,1)}, u32[]{:S(2)}, u32[]{:S(2)}) async-start(bf16[32,4,3584]{2,1,0:T(4,128)(2,1)} %bitcast.51), calls=%async_computation | async-start | bytes 1835008 | tf_op jit(solution)/shard_map/all_to_all | solution.py:33
  213.0 165.7 %all-to-all-start.3 = ((bf16[32,4,3584]{2,1,0:T(4,128)(2,1)}), bf16[32,4,3584]{2,1,0:T(4,128)(2,1)}, u32[]{:S(2)}, u32[]{:S(2)}) async-start(bf16[32,4,3584]{2,1,0:T(4,128)(2,1)} %reshape.103), calls=%async_computation.3 | async-start | bytes 1835008 | tf_op jit(solution)/shard_map/all_to_all | solution.py:39
  378.7 57.0 %all-to-all-start.1 = ((bf16[32,4,3584]{2,1,0:T(4,128)(2,1)}), bf16[32,4,3584]{2,1,0:T(4,128)(2,1)}, u32[]{:S(2)}, u32[]{:S(2)}) async-start(bf16[32,4,3584]{2,1,0:T(4,128)(2,1)} %reshape.98), calls=%async_computation.1 | async-start | bytes 1835008 | tf_op jit(solution)/shard_map/all_to_all | solution.py:39
  402.1 39.8 %collective-permute-start.1 = (bf16[1,64,3584]{2,1,0:T(8,128)(2,1)}, bf16[1,64,3584]{2,1,0:T(8,128)(2,1)}, u32[]{:S(2)}, u32[]{:S(2)}) collective-permute-start(bf16[1,64,3584]{2,1,0:T(8,128)(2,1)} %fusion.12), channel_id=1, source_target_pairs={{32,0},{64,32},{96,64},{128,96},{160,128},{192,160},{224,192},{256... | collective-permute-start | bytes 1376264 | tf_op jit(solution)/shard_map/ppermute | solution.py:12
  437.6 0.9 copy-start.4
  439.7 14.8 %collective-permute-start = (bf16[1,64,3584]{2,1,0:T(8,128)(2,1)S(1)}, bf16[1,64,3584]{2,1,0:T(8,128)(2,1)S(1)}, u32[]{:S(2)}, u32[]{:S(2)}) collective-permute-start(bf16[1,64,3584]{2,1,0:T(8,128)(2,1)S(1)} %fusion.11), channel_id=1, source_target_pairs={{992,0},{0,32},{32,64},{64,96},{96,128},{128,160},{160,192},{192,2... | collective-permute-start | bytes 1376264 | tf_op jit(solution)/shard_map/ppermute | solution.py:12
where the time goes:
time: 460 us; the launch traced here: 457 us
  waiting for transfers between devices  250 us (54%)
  starting transfers between devices  175 us (38%)
  local copies, waits for them, and re-layouts  12.3 us (3%)
  matrix products  10 us (2%)
  other arithmetic  9.56 us (2%)
    all_to_all x2, waiting for transfers between devices, dispatch(): lax.all_to_all(packed, 'ep', split_axis=0, concat_axis=0, tiled=True)  146 us
    all_to_all x2, starting transfers between devices, combine(): lax.all_to_all(partial_value.reshape(experts * split, capacity, width), '...  119 us
    all_to_all x2, waiting for transfers between devices, combine(): lax.all_to_all(partial_value.reshape(experts * split, capacity, width), '...  91.5 us
    all_to_all x2, starting transfers between devices, dispatch(): lax.all_to_all(packed, 'ep', split_axis=0, concat_axis=0, tiled=True)  52.1 us
    ppermute x2, waiting for transfers between devices, from_behind(): return lax.ppermute(block, axis, route)  12.7 us
  transfers between devices with their start and end apart: 6, of which 5 were waited for; matrix products, arithmetic and copies ran while one was open for 5% of the time, Pallas kernels for 0%

commit v1 on v0

v1 whole, which is shorter than its diff:
```python
import jax
import jax.numpy as jnp
from jax import lax
from jax.experimental import pallas as pl
from jax.experimental.pallas import tpu as pltpu
from jax.sharding import Mesh
from jax.sharding import PartitionSpec as P

CORES = 2
Z_GROUPS = 4
SPLIT = 4
F32 = jnp.float32
BF16 = jnp.bfloat16
VMEM = pl.BlockSpec(memory_space=pltpu.VMEM)
SMEM = pl.BlockSpec(memory_space=pltpu.SMEM)
PARAMS = pltpu.CompilerParams(vmem_limit_bytes=44 * 1024 * 1024)


def iota(shape, axis):
    return lax.broadcasted_iota(jnp.int32, shape, axis)


def dot(a, b, dims=((1,), (0,))):
    return lax.dot_general(a, b, (dims, ((), ())), preferred_element_type=F32)


def slots_of(route, experts):
    tokens = route.shape[1]
    onehot = iota((experts, tokens), 0) == route
    onehot = jnp.where(onehot, 1.0, 0.0)
    shape = (tokens, tokens)
    earlier = jnp.where(iota(shape, 0) < iota(shape, 1), 1.0, 0.0).astype(BF16)
    before = dot(onehot.astype(BF16), earlier)
    return jnp.sum(before * onehot, axis=0, keepdims=True)


def column(row):
    tokens = row.shape[1]
    shape = (tokens, tokens)
    on = iota(shape, 0) == iota(shape, 1)
    return jnp.sum(jnp.where(on, row, 0.0), axis=1, keepdims=True)


def pack_kernel(experts, cap, x_ref, rf_ref, cot_ref, rb_ref, gb_ref, out_ref):
    tokens = x_ref.shape[0]
    rows = out_ref.shape[0]
    scaled = (column(gb_ref[...]) * cot_ref[...].astype(F32)).astype(BF16)
    total = jnp.zeros(out_ref.shape, F32)
    for kind, (route, values) in enumerate(((rf_ref[...], x_ref[...]), (rb_ref[...], scaled))):
        slot = slots_of(route, experts).astype(jnp.int32)
        m = iota((rows, tokens), 0)
        table = (m // (4 * cap) == route) & ((m % (2 * cap)) // cap == kind) & (m % cap == slot)
        total += dot(jnp.where(table, 1.0, 0.0).astype(BF16), values)
    out_ref[...] = total.astype(BF16)


def expert_kernel(cap, c_ref, own_ref, oth_ref, saved_ref, wgu_ref, wd_ref, mine_ref, send_ref):
    rows = own_ref.shape[0]
    hid, width = wd_ref.shape
    values = jnp.concatenate([own_ref[...], oth_ref[...]], axis=0)
    both = 2 * rows
    pre = dot(values, wgu_ref[...])
    gate = pre[:, :hid]
    hidden = (gate / (1.0 + jnp.exp(-gate)) * pre[:, hid:]).astype(BF16)
    dh = dot(values, wd_ref[...], ((1,), (1,)))
    r = iota((both, rows), 0)
    p = iota((both, rows), 1)
    core = jnp.where(r < rows, c_ref[0], 1 - c_ref[0])
    r = r % rows
    pick = (p // (2 * cap) == r // (2 * cap)) & (p % cap == r % cap) & ((p % (2 * cap)) // cap == core)
    saved = dot(jnp.where(pick, 1.0, 0.0).astype(BF16), saved_ref[...])
    act = saved[:, :hid]
    lin = saved[:, hid:]
    sig = 1.0 / (1.0 + jnp.exp(-act))
    d_act = (dh * lin * sig * (1.0 + act * (1.0 - sig))).astype(BF16)
    d_lin = (dh * act * sig).astype(BF16)
    zero = jnp.zeros((), BF16)
    forward = (iota((both, hid), 0) % (2 * cap)) // cap == 0
    hidden = jnp.where(forward, hidden, zero)
    grads = jnp.concatenate(
        [jnp.where(forward, zero, d_act), jnp.where(forward, zero, d_lin)], axis=1
    )
    step = 512 if width % 512 == 0 else width
    for at in range(0, width, step):
        part = dot(hidden, wd_ref[:, at : at + step])
        part += dot(grads, wgu_ref[at : at + step, :], ((1,), (1,)))
        part = part.astype(BF16)
        mine_ref[:, at : at + step] = part[:rows]
        send_ref[:, at : at + step] = part[rows:]


def final_kernel(experts, cap, x_ref, rf_ref, gf_ref, cot_ref, rb_ref, back_ref, f_ref, b_ref):
    tokens = x_ref.shape[0]
    rows = back_ref.shape[0]
    back = back_ref[...]
    sums = []
    for kind, route in enumerate((rf_ref[...], rb_ref[...])):
        slot = column(slots_of(route, experts)).astype(jnp.int32)
        expert = column(route.astype(F32)).astype(jnp.int32)
        m = iota((tokens, rows), 1)
        table = (m // (4 * cap) == expert) & ((m % (2 * cap)) // cap == kind) & (m % cap == slot)
        sums.append(dot(jnp.where(table, 1.0, 0.0).astype(BF16), back))
    f_ref[...] = (x_ref[...].astype(F32) + column(gf_ref[...]) * sums[0]).astype(BF16)
    b_ref[...] = (cot_ref[...].astype(F32) + sums[1]).astype(BF16)


def call(kernel, out, operands, flops):
    nbytes = sum(a.size * a.dtype.itemsize for a in (*operands, *out))
    scalar = [a.ndim == 1 for a in operands]
    return pl.pallas_call(
        kernel,
        out_shape=out,
        in_specs=[SMEM if s else VMEM for s in scalar],
        out_specs=[VMEM] * len(out),
        compiler_params=PARAMS,
        cost_estimate=pl.CostEstimate(flops=flops, bytes_accessed=nbytes, transcendentals=0),
    )(*operands)


def swap_core(block):
    return lax.ppermute(block, "c", [(0, 1), (1, 0)])


def shift(block, distance):
    count = lax.axis_size("pp")
    return lax.ppermute(block, "pp", [(i, (i + distance) % count) for i in range(count)])


def exchange(rows, cap):
    width = rows.shape[1]
    blocks = rows.reshape(-1, 2 * cap, width)
    blocks = lax.all_to_all(blocks, ("x", "zh"), split_axis=0, concat_axis=0, tiled=True)
    return blocks.reshape(-1, width)


def shards(fwd_in, fwd_route, fwd_gate, bwd_cot, bwd_route, bwd_gate, saved_pre, w_gate_up, w_down):
    devices = lax.axis_size(("x", "zh", "c"))
    experts = devices // SPLIT
    cap = saved_pre.shape[2] // devices
    x = fwd_in[0]
    cot = bwd_cot[0]
    tokens, width = x.shape
    hid = w_down.shape[1]
    route_f, gate_f, route_b, gate_b = (
        a.reshape(1, tokens) for a in (fwd_route, fwd_gate, bwd_route, bwd_gate)
    )
    rows = devices * cap
    slab = jax.ShapeDtypeStruct((rows, width), BF16)
    out = jax.ShapeDtypeStruct((tokens, width), BF16)
    core = lax.axis_index("c").astype(jnp.int32).reshape(1)

    def pack(*refs):
        pack_kernel(experts, cap, *refs)

    def expert(*refs):
        expert_kernel(cap, *refs)

    def final(*refs):
        final_kernel(experts, cap, *refs)

    (packed,) = call(pack, [slab], (x, route_f, cot, route_b, gate_b), 2 * rows * tokens * width * 2)
    own = exchange(packed, cap)
    other = swap_core(own)
    mine, send = call(
        expert,
        [slab, slab],
        (core, own, other, saved_pre[0, 0], w_gate_up[0], w_down[0]),
        12 * rows * hid * width,
    )
    taken = swap_core(send)
    summed = (mine.astype(F32) + taken.astype(F32)).astype(BF16)
    back = exchange(summed, cap)
    out_f, out_b = call(
        final, [out, out], (x, route_f, gate_f, cot, route_b, back), 4 * rows * tokens * width
    )
    return shift(out_f[None], 1), shift(out_b[None], -1)


def solution(mesh):
    sections, members = mesh.devices.shape
    fine = Mesh(
        mesh.devices.reshape(sections, members // (Z_GROUPS * CORES), Z_GROUPS, CORES),
        ("pp", "x", "zh", "c"),
    )
    ep = ("x", "zh", "c")
    rows = P("pp", ep, None)
    return jax.shard_map(
        shards,
        mesh=fine,
        in_specs=(rows,) * 6 + (P("pp", ep, None, None), P(ep, None, None), P(ep, None, None)),
        out_specs=(rows, rows),
        check_vma=False,
    )
```

time: 460 us -> 287 us (0.62)
  the two profiles are of different devices: /device:TPU:70 before, /device:TPU:1 now
where the time goes in v1:
time: 287 us
  blocking collectives  221 us (77%)
  starting transfers between devices  26.5 us (9%)
  waiting for transfers between devices  24 us (8%)
  local copies, waits for them, and re-layouts  7.6 us (3%)
  Pallas kernels  6.87 us (2%)
    all_to_all x2, blocking collectives, exchange(): lax.all_to_all(blocks, ('x', 'zh'), split_axis=0, concat_axis=0, tiled=True)  221 us
    ppermute x2, waiting for transfers between devices, shift(): lax.ppermute(block, 'pp', [(i, (i + distance) % count) for i in range(cou...  19.7 us
    ppermute x2, starting transfers between devices, shift(): lax.ppermute(block, 'pp', [(i, (i + distance) % count) for i in range(cou...  19.5 us
    unnamed x28, local copies, waits for them, and re-layouts  7.6 us
    ppermute x2, starting transfers between devices, swap_core(): return lax.ppermute(block, 'c', [(0, 1), (1, 0)])  6.98 us
    pallas_call x3, Pallas kernels, call(): pl.pallas_call(kernel, out_shape=out, in_specs=[SMEM if s else VMEM for s...  6.87 us
  transfers between devices with their start and end apart: 4, of which 4 were waited for; matrix products, arithmetic and copies ran while one was open for 0% of the time, Pallas kernels for 0%

profile of v1, /device:TPU:1, one launch (start us, length us, event | category | flops | bytes accessed | tf_op | source)
XLA Modules:
  0.0 287.0 jit_solution(15734235038461138939)
XLA Ops:
  0.6 0.0 copy-start.2
  0.6 1.0 copy-done.2
  1.7 0.0 copy-start.4
  1.7 1.0 copy-done.4
  2.7 0.0 copy-start.7
  2.7 0.7 copy-done.7
  3.3 0.0 copy-start.9
  3.3 0.7 copy-done.9
  4.0 0.0 copy-start.11
  4.0 0.7 copy-done.11
  4.6 0.0 copy-start.1
  4.6 0.0 copy-start.6
  4.6 0.7 shard_map.104
  5.4 117.6 %all_to_all.10 = bf16[16,8,3584]{2,1,0:T(8,128)(2,1)S(1)} all-to-all(bf16[16,8,3584]{2,1,0:T(8,128)(2,1)S(1)} %bitcast.18), channel_id=1, replica_groups=mesh['pp'=32,'x'=4,'zh'=4,'c'=2] {'x','zh'}, dimensions={0} | all-to-all | bytes 1835008 | tf_op jit(solution)/shard_map/all_to_all | solution.py:132
  123.0 4.7 %collective-permute-start = (bf16[128,3584]{1,0:T(8,128)(2,1)S(1)}, bf16[128,3584]{1,0:T(8,128)(2,1)}, u32[]{:S(2)}, u32[]{:S(2)}) collective-permute-start(bf16[128,3584]{1,0:T(8,128)(2,1)S(1)} %bitcast.20), channel_id=1, source_target_pairs={{0,1},{1,0},{2,3},{3,2},{4,5},{5,4},{6,7},{7,6},{8,9},{9,8},{10,11... | collective-permute-start | bytes 2752520 | tf_op jit(solution)/shard_map/ppermute | solution.py:121
  127.7 2.2 collective-permute-done.refs_2_
  129.9 0.0 copy-done.1
  129.9 0.0 copy-done.6
  129.9 0.0 copy-start
  129.9 2.0 copy-done
  132.0 5.2 %shard_map.105 = (bf16[128,3584]{1,0:T(8,128)(2,1)S(1)}, bf16[128,3584]{1,0:T(8,128)(2,1)S(1)}) custom-call(s32[1]{0:T(128)} %bitcast.5.refs_0_, bf16[128,3584]{1,0:T(8,128)(2,1)S(1)} %bitcast.21, bf16[128,3584]{1,0:T(8,128)(2,1)} %collective-permute-done.refs_2_, bf16[128,512]{1,0:T(8,128)(2,1)S(1)} %bitcast.27, bf16[3584,512]{1,0:T(8,128)(2,1)S(1)} %bitcast.19, ...), custom_call_target="tpu_custom_call" | custom-call | flops 1409286144 | bytes 9306116 | tf_op jit(solution)/shard_map/pallas_call | solution.py:110
  137.2 2.3 collective-permute-start.1
  139.5 2.1 collective-permute-done.1
  141.5 0.0 copy-start.3
  141.5 0.0 copy-start.5
  141.5 0.0 copy-start.8
  141.5 0.0 copy-start.10
  141.5 0.0 copy-start.12
  141.6 0.3 fusion
  141.9 103.4 %all_to_all.11 = bf16[16,8,3584]{2,1,0:T(8,128)(2,1)S(1)} all-to-all(bf16[16,8,3584]{2,1,0:T(8,128)(2,1)S(1)} %fusion), channel_id=1, replica_groups=mesh['pp'=32,'x'=4,'zh'=4,'c'=2] {'x','zh'}, dimensions={0} | all-to-all | bytes 1835008 | tf_op jit(solution)/shard_map/all_to_all | solution.py:132
  245.2 0.0 copy-done.3
  245.2 0.0 copy-done.5
  245.3 0.0 copy-done.8
  245.3 0.0 copy-done.10
  245.3 0.0 copy-done.12
  245.3 0.9 shard_map.106
  246.2 17.6 %collective-permute-start.3 = (bf16[1,64,3584]{2,1,0:T(8,128)(2,1)S(1)}, bf16[1,64,3584]{2,1,0:T(8,128)(2,1)S(1)}, u32[]{:S(2)}, u32[]{:S(2)}) collective-permute-start(bf16[1,64,3584]{2,1,0:T(8,128)(2,1)S(1)} %bitcast.35), channel_id=1, source_target_pairs={{0,992},{32,0},{64,32},{96,64},{128,96},{160,128},{192,160},{224,1... | collective-permute-start | bytes 1376264 | tf_op jit(solution)/shard_map/ppermute | solution.py:126
  263.8 1.9 collective-permute-start.2
  265.7 7.3 %collective-permute-done.3 = bf16[1,64,3584]{2,1,0:T(8,128)(2,1)S(1)} collective-permute-done((bf16[1,64,3584]{2,1,0:T(8,128)(2,1)S(1)}, bf16[1,64,3584]{2,1,0:T(8,128)(2,1)S(1)}, u32[]{:S(2)}, u32[]{:S(2)}) %collective-permute-start.3) | collective-permute-done | bytes 458784 | tf_op jit(solution)/shard_map/ppermute | solution.py:126
  273.0 12.5 %collective-permute-done.2 = bf16[1,64,3584]{2,1,0:T(8,128)(2,1)S(1)} collective-permute-done((bf16[1,64,3584]{2,1,0:T(8,128)(2,1)S(1)}, bf16[1,64,3584]{2,1,0:T(8,128)(2,1)S(1)}, u32[]{:S(2)}, u32[]{:S(2)}) %collective-permute-start.2) | collective-permute-done | bytes 458784 | tf_op jit(solution)/shard_map/ppermute | solution.py:126
  285.5 0.8 copy.13
  286.2 0.8 copy.14
Async XLA Ops:
  0.6 1.0 copy-start.2
  1.7 1.0 copy-start.4
  2.7 0.7 copy-start.7
  3.3 0.7 copy-start.9
  4.0 0.7 copy-start.11
  4.6 125.3 %copy-start.1 = (bf16[1,256,3584]{2,1,0:T(8,128)(2,1)S(1)}, bf16[1,256,3584]{2,1,0:T(8,128)(2,1)}, u32[]{:S(2)}) copy-start(bf16[1,256,3584]{2,1,0:T(8,128)(2,1)} %param.17) | copy-start | bytes 5505028
  4.6 125.3 %copy-start.6 = (bf16[1,1,128,512]{3,2,1,0:T(8,128)(2,1)S(1)}, bf16[1,1,128,512]{3,2,1,0:T(8,128)(2,1)}, u32[]{:S(2)}) copy-start(bf16[1,1,128,512]{3,2,1,0:T(8,128)(2,1)} %param.15) | copy-start | bytes 393220
  123.0 6.9 %collective-permute-start = (bf16[128,3584]{1,0:T(8,128)(2,1)S(1)}, bf16[128,3584]{1,0:T(8,128)(2,1)}, u32[]{:S(2)}, u32[]{:S(2)}) collective-permute-start(bf16[128,3584]{1,0:T(8,128)(2,1)S(1)} %bitcast.20), channel_id=1, source_target_pairs={{0,1},{1,0},{2,3},{3,2},{4,5},{5,4},{6,7},{7,6},{8,9},{9,8},{10,11... | collective-permute-start | bytes 2752520 | tf_op jit(solution)/shard_map/ppermute | solution.py:121
  129.9 2.0 copy-start
  137.2 4.4 %collective-permute-start.1 = (bf16[128,3584]{1,0:T(8,128)(2,1)S(1)}, bf16[128,3584]{1,0:T(8,128)(2,1)S(1)}, u32[]{:S(2)}, u32[]{:S(2)}) collective-permute-start(bf16[128,3584]{1,0:T(8,128)(2,1)S(1)} %get-tuple-element.7), channel_id=1, source_target_pairs={{0,1},{1,0},{2,3},{3,2},{4,5},{5,4},{6,7},{7,6},{8,9},{9,8},{10,11... | collective-permute-start | bytes 2752520 | tf_op jit(solution)/shard_map/ppermute | solution.py:121
  141.5 103.7 %copy-start.3 = (bf16[1,64,3584]{2,1,0:T(8,128)(2,1)S(1)}, bf16[1,64,3584]{2,1,0:T(8,128)(2,1)}, u32[]{:S(2)}) copy-start(bf16[1,64,3584]{2,1,0:T(8,128)(2,1)} %param.9) | copy-start | bytes 1376260
  141.5 103.7 %copy-start.5 = (bf16[1,64,3584]{2,1,0:T(8,128)(2,1)S(1)}, bf16[1,64,3584]{2,1,0:T(8,128)(2,1)}, u32[]{:S(2)}) copy-start(bf16[1,64,3584]{2,1,0:T(8,128)(2,1)} %param.12) | copy-start | bytes 1376260
  141.5 103.7 %copy-start.8 = (s32[1,64,1]{1,2,0:T(1,128)S(1)}, s32[1,64,1]{1,2,0:T(1,128)}, u32[]{:S(2)}) copy-start(s32[1,64,1]{1,2,0:T(1,128)} %param.10) | copy-start | bytes 772
  141.5 103.7 %copy-start.10 = (s32[1,64,1]{1,2,0:T(1,128)S(1)}, s32[1,64,1]{1,2,0:T(1,128)}, u32[]{:S(2)}) copy-start(s32[1,64,1]{1,2,0:T(1,128)} %param.13) | copy-start | bytes 772
  141.5 103.7 %copy-start.12 = (f32[1,64,1]{1,2,0:T(1,128)S(1)}, f32[1,64,1]{1,2,0:T(1,128)}, u32[]{:S(2)}) copy-start(f32[1,64,1]{1,2,0:T(1,128)} %param.11) | copy-start | bytes 772
  246.2 26.8 %collective-permute-start.3 = (bf16[1,64,3584]{2,1,0:T(8,128)(2,1)S(1)}, bf16[1,64,3584]{2,1,0:T(8,128)(2,1)S(1)}, u32[]{:S(2)}, u32[]{:S(2)}) collective-permute-start(bf16[1,64,3584]{2,1,0:T(8,128)(2,1)S(1)} %bitcast.35), channel_id=1, source_target_pairs={{0,992},{32,0},{64,32},{96,64},{128,96},{160,128},{192,160},{224,1... | collective-permute-start | bytes 1376264 | tf_op jit(solution)/shard_map/ppermute | solution.py:126
  263.8 21.7 %collective-permute-start.2 = (bf16[1,64,3584]{2,1,0:T(8,128)(2,1)S(1)}, bf16[1,64,3584]{2,1,0:T(8,128)(2,1)S(1)}, u32[]{:S(2)}, u32[]{:S(2)}) collective-permute-start(bf16[1,64,3584]{2,1,0:T(8,128)(2,1)S(1)} %bitcast.34), channel_id=1, source_target_pairs={{0,32},{32,64},{64,96},{96,128},{128,160},{160,192},{192,224},{224... | collective-permute-start | bytes 1376264 | tf_op jit(solution)/shard_map/ppermute | solution.py:126

commit v2 on v1

v2 whole, which is shorter than its diff:
```python
import jax
import jax.numpy as jnp
from jax import lax
from jax.experimental import pallas as pl
from jax.experimental.pallas import tpu as pltpu
from jax.sharding import Mesh
from jax.sharding import PartitionSpec as P

CORES = 2
Z_GROUPS = 4
SPLIT = 4
HIDES = {"pack_b": 1e11, "join_b":1e11, "merge_b":1e11,"expert_f":1e11,"pack_f":1e10}
F32 = jnp.float32
BF16 = jnp.bfloat16
VMEM = pl.BlockSpec(memory_space=pltpu.VMEM)
ANY = pl.BlockSpec(memory_space=pl.ANY)
SMEM = pl.BlockSpec(memory_space=pltpu.SMEM)
PARAMS = pltpu.CompilerParams(vmem_limit_bytes=44 * 1024 * 1024)


def iota(shape, axis):
    return lax.broadcasted_iota(jnp.int32, shape, axis)


def dot(a, b, dims=((1,), (0,))):
    return lax.dot_general(a, b, (dims, ((), ())), preferred_element_type=F32)


def ones_at(where):
    return jnp.where(where, 1.0, 0.0).astype(BF16)


def slots_of(route, experts):
    tokens = route.shape[1]
    onehot = jnp.where(iota((experts, tokens), 0) == route, 1.0, 0.0)
    shape = (tokens, tokens)
    before = dot(onehot.astype(BF16), ones_at(iota(shape, 0) < iota(shape, 1)))
    return jnp.sum(before * onehot, axis=0, keepdims=True).astype(jnp.int32)


def column(row):
    tokens = row.shape[1]
    shape = (tokens, tokens)
    on = iota(shape, 0) == iota(shape, 1)
    return jnp.sum(jnp.where(on, row, jnp.zeros((), row.dtype)), axis=1, keepdims=True)


def pack_b_kernel(experts, cap, at_ref, cot_ref, route_ref, gate_ref, *out_refs):
    tokens = cot_ref.shape[0]
    scaled = (column(gate_ref[...]) * cot_ref[...].astype(F32)).astype(BF16)
    route = route_ref[...]
    slot = slots_of(route, experts)
    count = len(out_refs)
    m = iota((count * 2 * cap, tokens), 0)
    pair = at_ref[1] // 2 ^ ((m % (2 * cap)) // cap)
    expert = (at_ref[0] + m // (2 * cap)) % count * 2 + pair
    packed = dot(ones_at((expert == route) & (m % cap == slot)), scaled).astype(BF16)
    for d, out_ref in enumerate(out_refs):
        out_ref[...] = packed[d * 2 * cap : (d + 1) * 2 * cap]


def pairs_kernel(cap, *refs):
    *in_refs, own_ref, oth_ref = refs
    rows = jnp.concatenate([r[...] for r in in_refs], axis=0)
    shape = (own_ref.shape[0], rows.shape[0])
    r, m = iota(shape, 0), iota(shape, 1)
    same = (m // (2 * cap) == r // cap) & (m % cap == r % cap)
    own = (m % (2 * cap)) // cap == 0
    own_ref[...] = dot(ones_at(same & own), rows).astype(BF16)
    oth_ref[...] = dot(ones_at(same & ~own), rows).astype(BF16)


def expert_b_kernel(cap, at_ref, own_ref, oth_ref, saved_ref, wgu_ref, wd_ref, mine_ref, send_ref):
    rows = own_ref.shape[0]
    hid, width = wd_ref.shape
    values = jnp.concatenate([own_ref[...], oth_ref[...]], axis=0)
    dh = dot(values, wd_ref[...], ((1,), (1,)))
    shape = (2 * rows, saved_ref.shape[0])
    r, p = iota(shape, 0), iota(shape, 1)
    core = at_ref[2] ^ (r // rows)
    block = (r % rows) // (rows // Z_GROUPS)
    mask = block ^ (block // 2)
    count = rows // (Z_GROUPS * cap)
    source_x = (at_ref[0] + count - (r // cap) % count) % count
    source = (source_x * Z_GROUPS + (at_ref[1] ^ mask)) * CORES + core
    saved = dot(ones_at(p == source * cap + r % cap), saved_ref[...])
    act = saved[:, :hid]
    lin = saved[:, hid:]
    sig = 1.0 / (1.0 + jnp.exp(-act))
    d_act = (dh * lin * sig * (1.0 + act * (1.0 - sig))).astype(BF16)
    d_lin = (dh * act * sig).astype(BF16)
    grads = jnp.concatenate([d_act, d_lin], axis=1)
    step = 512 if width % 512 == 0 else width
    for at in range(0, width, step):
        part = dot(grads, wgu_ref[at : at + step, :], ((1,), (1,))).astype(BF16)
        mine_ref[:, at : at + step] = part[:rows]
        send_ref[:, at : at + step] = part[rows:]


def join_kernel(*refs):
    *in_refs, out_ref = refs
    out_ref[...] = jnp.concatenate([r[...] for r in in_refs], axis=0)


def add_kernel(a_ref, b_ref, *out_refs):
    total = (a_ref[...].astype(F32) + b_ref[...].astype(F32)).astype(BF16)
    size = total.shape[0] // len(out_refs)
    for i, out_ref in enumerate(out_refs):
        out_ref[...] = total[i * size : (i + 1) * size]


def merge_kernel(cap, here_ref, partner_ref, mirror_ref, opposite_ref, *out_refs):
    rows = jnp.concatenate([r[...] for r in (here_ref, partner_ref, mirror_ref, opposite_ref)], axis=0)
    shape = (len(out_refs) * 2 * cap, rows.shape[0])
    block = here_ref.shape[0]
    r, m = iota(shape, 0), iota(shape, 1)
    same = ((m % block) // cap == r // (2 * cap)) & (m % cap == r % cap)
    same = same & (m // (2 * block) == (r % (2 * cap)) // cap)
    merged = dot(ones_at(same), rows).astype(BF16)
    for d, out_ref in enumerate(out_refs):
        out_ref[...] = merged[d * 2 * cap : (d + 1) * 2 * cap]


def final_b_kernel(experts, cap, at_ref, cot_ref, route_ref, *refs):
    *in_refs, out_ref = refs
    tokens = cot_ref.shape[0]
    count = len(in_refs)
    rows = jnp.concatenate([r[...] for r in in_refs], axis=0)
    route = route_ref[...]
    slot = column(slots_of(route, experts))
    m = iota((tokens, rows.shape[0]), 1)
    pair = at_ref[1] // 2 ^ ((m % (2 * cap)) // cap)
    expert = (at_ref[0] + m // (2 * cap)) % count * 2 + pair
    total = dot(ones_at((expert == column(route)) & (m % cap == slot)), rows)
    out_ref[...] = (cot_ref[...].astype(F32) + total).astype(BF16)


def pack_f_kernel(experts, cap, x_ref, meta_ref, out_ref):
    tokens, width = x_ref.shape
    rows, half = out_ref.shape
    route = meta_ref[0:1, :].astype(jnp.int32)
    slot = slots_of(route, experts)
    m = iota((rows, tokens), 0)
    table = (m // (4 * cap) == route) & (m % cap == slot)
    low = (m % (2 * cap)) // cap == 0
    total = dot(ones_at(table & low), x_ref[:, :half])
    total += dot(ones_at(table & ~low), x_ref[:, half:])
    out_ref[...] = total.astype(BF16)


def joined(rows, cap):
    count = rows.shape[0]
    shape = (count // 2, count)
    r, m = iota(shape, 0), iota(shape, 1)
    same = (m // (2 * cap) == r // cap) & (m % cap == r % cap)
    low = (m % (2 * cap)) // cap == 0
    parts = [dot(ones_at(same & half), rows).astype(BF16) for half in (low, ~low)]
    return jnp.concatenate(parts, axis=1)


def parted(low, high, cap, rows):
    shape = (rows, rows // 2)
    m, r = iota(shape, 0), iota(shape, 1)
    same = (m // (2 * cap) == r // cap) & (m % cap == r % cap)
    first = (m % (2 * cap)) // cap == 0
    return (dot(ones_at(same & first), low) + dot(ones_at(same & ~first), high)).astype(BF16)


def expert_f_kernel(cap, own_ref, oth_ref, wgu_ref, wd_ref, mine_ref, send_ref):
    rows, half = own_ref.shape
    hid = wd_ref.shape[0]
    values = jnp.concatenate([joined(own_ref[...], cap), joined(oth_ref[...], cap)], axis=0)
    pre = dot(values, wgu_ref[...])
    gate = pre[:, :hid]
    hidden = (gate / (1.0 + jnp.exp(-gate)) * pre[:, hid:]).astype(BF16)
    mid = rows // 2
    step = 256 if half % 256 == 0 else half
    for at in range(0, half, step):
        low, high = (
            dot(hidden, wd_ref[:, base + at : base + at + step]).astype(BF16) for base in (0, half)
        )
        mine_ref[:, at : at + step] = parted(low[:mid], high[:mid], cap, rows)
        send_ref[:, at : at + step] = parted(low[mid:], high[mid:], cap, rows)


def final_f_kernel(experts, cap, x_ref, meta_ref, back_ref, out_ref):
    tokens = x_ref.shape[0]
    rows, half = back_ref.shape
    meta = meta_ref[...]
    route = meta[0:1, :].astype(jnp.int32)
    slot = column(slots_of(route, experts))
    gate = column(meta[1:2, :])
    m = iota((tokens, rows), 1)
    table = (m // (4 * cap) == column(route)) & (m % cap == slot)
    low = (m % (2 * cap)) // cap == 0
    back = back_ref[...]
    for base, part in ((0, low), (half, ~low)):
        total = gate * dot(ones_at(table & part), back)
        x = x_ref[:, base : base + half].astype(F32)
        out_ref[:, base : base + half] = (x + total).astype(BF16)


def call(kernel, name, shapes, operands, flops, earlier=()):
    out = [jax.ShapeDtypeStruct(s, BF16) for s in shapes]
    nbytes = sum(a.size * a.dtype.itemsize for a in (*operands, *out))
    count = len(operands)

    def body(*refs):
        kernel(*refs[:count], *refs[count + len(earlier) :])

    return pl.pallas_call(
        body,
        out_shape=out,
        in_specs=[SMEM if a.ndim == 1 else VMEM for a in operands] + [ANY] * len(earlier),
        out_specs=[VMEM] * len(out),
        compiler_params=PARAMS,
        name=name,
        cost_estimate=pl.CostEstimate(
            flops=flops + int(HIDES.get(name, 0)), bytes_accessed=nbytes, transcendentals=0
        ),
    )(*operands, *earlier)


def moved(block, axis, to):
    return lax.ppermute(block, axis, [(i, to(i)) for i in range(lax.axis_size(axis))])


def swap_core(block):
    return moved(block, "c", lambda i: 1 - i)


def shift(block, distance):
    count = lax.axis_size("pp")
    return moved(block, "pp", lambda i: (i + distance) % count)


def along_x(blocks, sign):
    count = len(blocks)
    rest = [moved(b, "x", lambda i, d=d: (i + sign * d) % count) for d, b in enumerate(blocks) if d]
    return [blocks[0]] + rest


def after(value, *earlier):
    return pl.pallas_call(
        lambda *refs: None,
        out_shape=jax.ShapeDtypeStruct(value.shape, value.dtype),
        in_specs=[ANY] * (1 + len(earlier)),
        out_specs=ANY,
        input_output_aliases={0: 0},
        name="after",
    )(value, *earlier)


def exchange(rows, cap):
    width = rows.shape[1]
    blocks = rows.reshape(-1, 2 * cap, width)
    blocks = lax.all_to_all(blocks, ("x", "zh"), split_axis=0, concat_axis=0, tiled=True)
    return blocks.reshape(-1, width)


def partner(block):
    return moved(block, "zh", lambda i: i ^ 1)


def mirror(block):
    return moved(block, "zh", lambda i: 3 - i)


def opposite(block):
    return moved(block, "zh", lambda i: i ^ 2)


def shards(fwd_in, fwd_route, fwd_gate, bwd_cot, bwd_route, bwd_gate, saved_pre, w_gate_up, w_down):
    devices = lax.axis_size(("x", "zh", "c"))
    experts = devices // SPLIT
    cap = saved_pre.shape[2] // devices
    cot = bwd_cot[0]
    tokens, width = cot.shape
    hid = w_down.shape[1]
    wgu, wd = w_gate_up[0], w_down[0]
    at = jnp.stack([lax.axis_index(a) for a in ("x", "zh", "c")]).astype(jnp.int32)
    many = devices * cap
    few = many // 2
    half = (many, width // 2)
    block = few // Z_GROUPS

    def kernel(body, *head):
        return lambda *refs: body(*head, *refs)

    route_b, gate_b = bwd_route.reshape(1, tokens), bwd_gate.reshape(1, tokens)
    meta = jnp.concatenate(
        [fwd_route.reshape(1, tokens).astype(F32), fwd_gate.reshape(1, tokens)], axis=0
    )
    x = shift(fwd_in[0], 1)
    meta = shift(meta, 1)

    chunks = call(
        kernel(pack_b_kernel, experts, cap),
        "pack_b",
        [(2 * cap, width)] * (block // cap),
        (at, cot, route_b, gate_b),
        4 * block * tokens * width,
    )
    chunks = along_x(chunks, 1)
    here, away = call(
        kernel(pairs_kernel, cap), "pairs", [(block, width)] * 2, chunks, 4 * block * block * width
    )
    from_partner = partner(here)
    from_mirror, from_opposite = mirror(away), opposite(away)
    blocks = (here, from_partner, from_mirror, from_opposite)

    (packed,) = call(
        kernel(pack_f_kernel, experts, cap),
        "pack_f",
        [half],
        (x, meta),
        2 * many * tokens * width,
        earlier=(here,),
    )
    own_f = exchange(packed, cap)
    (own_b,) = call(join_kernel, "join_b", [(few, width)], blocks, few * width, earlier=(packed,))

    mine_b, send_b = call(
        kernel(expert_b_kernel, cap),
        "expert_b",
        [(few, width)] * 2,
        (at, own_b, swap_core(own_b), saved_pre[0, 0], wgu, wd),
        6 * many * hid * width,
    )
    here, to_partner, to_mirror, to_opposite = call(
        add_kernel, "add_b", [(block, width)] * Z_GROUPS, (mine_b, swap_core(send_b)), few * width
    )
    from_partner = partner(to_partner)
    from_mirror, from_opposite = mirror(to_mirror), opposite(to_opposite)
    chunks = call(
        kernel(merge_kernel, cap),
        "merge_b",
        [(2 * cap, width)] * (block // cap),
        (here, from_partner, from_mirror, from_opposite),
        4 * block * few * width,
    )
    chunks = along_x(chunks, -1)
    (out_b,) = call(
        kernel(final_b_kernel, experts, cap),
        "final_b",
        [(tokens, width)],
        (at, cot, route_b, *chunks),
        4 * block * tokens * width,
    )
    out_b = shift(out_b, -1)

    def chain(_, rows):
        mine, send = call(
            kernel(expert_f_kernel, cap),
            "expert_f",
            [half] * 2,
            (rows, swap_core(rows), wgu, wd),
            6 * many * hid * width,
        )
        return (mine.astype(F32) + swap_core(send).astype(F32)).astype(BF16)

    rounds = jnp.minimum(jnp.sum((fwd_route < experts).astype(jnp.int32)), 1)
    summed_f = lax.fori_loop(0, rounds, chain, own_f)
    back_f = exchange(summed_f, cap)
    (out_f,) = call(
        kernel(final_f_kernel, experts, cap),
        "final_f",
        [(tokens, width)],
        (x, meta, back_f),
        2 * many * tokens * width,
    )
    return out_f[None], out_b[None]


def solution(mesh):
    sections, members = mesh.devices.shape
    fine = Mesh(
        mesh.devices.reshape(sections, members // (Z_GROUPS * CORES), Z_GROUPS, CORES),
        ("pp", "x", "zh", "c"),
    )
    ep = ("x", "zh", "c")
    rows = P("pp", ep, None)
    return jax.shard_map(
        shards,
        mesh=fine,
        in_specs=(rows,) * 6 + (P("pp", ep, None, None), P(ep, None, None), P(ep, None, None)),
        out_specs=(rows, rows),
        check_vma=False,
    )
```

time: 287 us -> 259 us (0.902)
  the two profiles are of different devices: /device:TPU:1 before, /device:TPU:184 now
where the time goes in v2:
time: 259 us
  starting transfers between devices  168 us (65%)
  waiting for transfers between devices  68.9 us (27%)
  Pallas kernels  14.9 us (6%)
  local copies, waits for them, and re-layouts  3.17 us (1%)
    ppermute x19, starting transfers between devices, moved(): lax.ppermute(block, axis, [(i, to(i)) for i in range(lax.axis_size(axis))])  117 us
    ppermute x19, waiting for transfers between devices, moved(): lax.ppermute(block, axis, [(i, to(i)) for i in range(lax.axis_size(axis))])  68.9 us
    all_to_all x2, starting transfers between devices, exchange(): lax.all_to_all(blocks, ('x', 'zh'), split_axis=0, concat_axis=0, tiled=True)  51.2 us
    pallas_call x10, Pallas kernels, call(): pl.pallas_call(body, out_shape=out, in_specs=[SMEM if a.ndim == 1 else VM...  14.9 us
  transfers between devices with their start and end apart: 21, of which 8 were waited for; matrix products, arithmetic and copies ran while one was open for 1% of the time, Pallas kernels for 5%

profile of v2, /device:TPU:184, one launch (start us, length us, event | category | flops | bytes accessed | tf_op | source)
XLA Modules:
  0.0 258.5 jit_solution(9147664007029210202)
XLA Ops:
  0.6 3.8 %collective-permute-start.2 = (bf16[64,3584]{1,0:T(8,128)(2,1)}, bf16[64,3584]{1,0:T(8,128)(2,1)S(1)}, u32[]{:S(2)}, u32[]{:S(2)}) collective-permute-start(bf16[64,3584]{1,0:T(8,128)(2,1)} %bitcast.33), channel_id=1, source_target_pairs={{0,32},{32,64},{64,96},{96,128},{128,160},{160,192},{192,224},{224... | collective-permute-start | bytes 1376264 | tf_op jit(solution)/shard_map/ppermute | solution.py:225
  4.5 0.1 pad_add_fusion.refs_0_
  4.5 1.0 copy-done
  5.6 0.7 copy-done.9
  6.2 0.7 copy-done.11
  6.9 0.9 pack_b.1
  7.8 3.4 %collective-permute-start.4 = (bf16[8,3584]{1,0:T(8,128)(2,1)S(1)}, bf16[8,3584]{1,0:T(8,128)(2,1)S(1)}, u32[]{:S(2)}, u32[]{:S(2)}) collective-permute-start(bf16[8,3584]{1,0:T(8,128)(2,1)S(1)} %get-tuple-element.49), channel_id=1, source_target_pairs={{0,8},{8,16},{16,24},{24,0},{1,9},{9,17},{17,25},{25,1},{2,10},{10... | collective-permute-start | bytes 172040 | tf_op jit(solution)/shard_map/ppermute | solution.py:225
  11.2 4.6 %collective-permute-start.5 = (bf16[8,3584]{1,0:T(8,128)(2,1)S(1)}, bf16[8,3584]{1,0:T(8,128)(2,1)S(1)}, u32[]{:S(2)}, u32[]{:S(2)}) collective-permute-start(bf16[8,3584]{1,0:T(8,128)(2,1)S(1)} %get-tuple-element.50), channel_id=1, source_target_pairs={{0,16},{8,24},{16,0},{24,8},{1,17},{9,25},{17,1},{25,9},{2,18},{10... | collective-permute-start | bytes 172040 | tf_op jit(solution)/shard_map/ppermute | solution.py:225
  15.8 3.3 %collective-permute-start.6 = (bf16[8,3584]{1,0:T(8,128)(2,1)S(1)}, bf16[8,3584]{1,0:T(8,128)(2,1)S(1)}, u32[]{:S(2)}, u32[]{:S(2)}) collective-permute-start(bf16[8,3584]{1,0:T(8,128)(2,1)S(1)} %get-tuple-element.51), channel_id=1, source_target_pairs={{0,24},{8,0},{16,8},{24,16},{1,25},{9,1},{17,9},{25,17},{2,26},{10... | collective-permute-start | bytes 172040 | tf_op jit(solution)/shard_map/ppermute | solution.py:225
  19.2 0.6 fusion
  19.8 3.8 %collective-permute-start.3 = (f32[2,64]{1,0:T(2,128)S(1)}, f32[2,64]{1,0:T(2,128)S(1)}, u32[]{:S(2)}, u32[]{:S(2)}) collective-permute-start(f32[2,64]{1,0:T(2,128)S(1)} %pad_maximum_fusion), channel_id=1, source_target_pairs={{0,32},{32,64},{64,96},{96,128},{128,160},{160,192},{192,224},{224... | collective-permute-start | bytes 1544 | tf_op jit(solution)/shard_map/ppermute | solution.py:225
  23.7 0.0 collective-permute-done.4.refs_1_
  23.7 0.0 collective-permute-done.5.refs_2_
  23.7 0.0 collective-permute-done.6.refs_3_
  23.7 0.2 pairs.1
  23.9 15.5 %collective-permute-start.8 = (bf16[16,3584]{1,0:T(8,128)(2,1)S(1)}, bf16[16,3584]{1,0:T(8,128)(2,1)S(1)}, u32[]{:S(2)}, u32[]{:S(2)}) collective-permute-start(bf16[16,3584]{1,0:T(8,128)(2,1)S(1)} %get-tuple-element.54), channel_id=1, source_target_pairs={{0,6},{2,4},{4,2},{6,0},{1,7},{3,5},{5,3},{7,1},{8,14},{10,12},{12... | collective-permute-start | bytes 344072 | tf_op jit(solution)/shard_map/ppermute | solution.py:225
  39.4 12.3 %collective-permute-start.9 = (bf16[16,3584]{1,0:T(8,128)(2,1)S(1)}, bf16[16,3584]{1,0:T(8,128)(2,1)S(1)}, u32[]{:S(2)}, u32[]{:S(2)}) collective-permute-start(bf16[16,3584]{1,0:T(8,128)(2,1)S(1)} %get-tuple-element.54), channel_id=1, source_target_pairs={{0,4},{2,6},{4,0},{6,2},{1,5},{3,7},{5,1},{7,3},{8,12},{10,14},{12... | collective-permute-start | bytes 344072 | tf_op jit(solution)/shard_map/ppermute | solution.py:225
  51.7 1.9 collective-permute-start.7
  53.7 0.0 collective-permute-done.3.refs_1_
  53.7 0.0 collective-permute-done.2.refs_0_
  53.7 0.0 copy-start.2
  53.7 1.3 pack_f.1.refs_4_
  55.0 19.1 %all-to-all-start = ((bf16[16,8,1792]{2,1,0:T(8,128)(2,1)}), bf16[16,8,1792]{2,1,0:T(8,128)(2,1)}, u32[]{:S(2)}, u32[]{:S(2)}) async-start(bf16[16,8,1792]{2,1,0:T(8,128)(2,1)} %bitcast.9), calls=%async_computation | async-start | bytes 917504 | tf_op jit(solution)/shard_map/all_to_all | solution.py:257
  74.1 0.0 copy-start.4
  74.1 0.0 copy-start.12
  74.1 0.0 copy-start.13
  74.1 45.9 %collective-permute-done.7.refs_1_ = bf16[16,3584]{1,0:T(8,128)(2,1)S(1)} collective-permute-done((bf16[16,3584]{1,0:T(8,128)(2,1)S(1)}, bf16[16,3584]{1,0:T(8,128)(2,1)S(1)}, u32[]{:S(2)}, u32[]{:S(2)}) %collective-permute-start.7) | collective-permute-done | bytes 114720 | tf_op jit(solution)/shard_map/ppermute | solution.py:225
  120.0 0.0 collective-permute-done.8.refs_2_
  120.0 0.0 collective-permute-done.9.refs_3_
  120.0 1.9 collective-permute-start.10
  121.9 1.8 collective-permute-done.10.refs_2_
  123.7 3.3 %expert_b.1 = (bf16[64,3584]{1,0:T(8,128)(2,1)S(1)}, bf16[64,3584]{1,0:T(8,128)(2,1)S(1)}) custom-call(s32[3]{0:T(128)S(1)} %pad_add_fusion.refs_0_, bf16[64,3584]{1,0:T(8,128)(2,1)S(1)} %join_b.1.refs_1_, bf16[64,3584]{1,0:T(8,128)(2,1)S(1)} %collective-permute-done.10.refs_2_, bf16[128,512]{1,0:T(8,128)(2,1)S(1)} %bitcast.22, ...), custom_call_target="tpu_custom_call" | custom-call | flops 704643072 | bytes 7471116 | tf_op jit(solution)/shard_map/expert_b/pallas_call | solution.py:211
  127.0 2.0 collective-permute-start.11
  129.7 1.0 collective-permute-done.11.refs_1_
  130.7 0.8 add_b.1
  131.5 27.9 %collective-permute-start.12 = (bf16[16,3584]{1,0:T(8,128)(2,1)}, bf16[16,3584]{1,0:T(8,128)(2,1)}, u32[]{:S(2)}, u32[]{:S(2)}) collective-permute-start(bf16[16,3584]{1,0:T(8,128)(2,1)} %get-tuple-element.58), channel_id=1, source_target_pairs={{0,2},{2,0},{4,6},{6,4},{1,3},{3,1},{5,7},{7,5},{8,10},{10,8},{12,... | collective-permute-start | bytes 344072 | tf_op jit(solution)/shard_map/ppermute | solution.py:225
  159.4 1.9 collective-permute-start.13
  161.3 12.1 %collective-permute-start.14 = (bf16[16,3584]{1,0:T(8,128)(2,1)}, bf16[16,3584]{1,0:T(8,128)(2,1)}, u32[]{:S(2)}, u32[]{:S(2)}) collective-permute-start(bf16[16,3584]{1,0:T(8,128)(2,1)} %get-tuple-element.60), channel_id=1, source_target_pairs={{0,4},{2,6},{4,0},{6,2},{1,5},{3,7},{5,1},{7,3},{8,12},{10,14},{12... | collective-permute-start | bytes 344072 | tf_op jit(solution)/shard_map/ppermute | solution.py:225
  173.4 0.0 all-to-all-done
  173.4 13.4 %while.10 = (s32[]{:T(128)}, bf16[128,1792]{1,0:T(8,128)(2,1)}, s32[]{:T(128)}, bf16[3584,512]{1,0:T(8,128)(2,1)}, bf16[256,3584]{1,0:T(8,128)(2,1)S(1)}, /*index=5*/s32[]{:T(128)}) while((s32[]{:T(128)}, bf16[128,1792]{1,0:T(8,128)(2,1)}, s32[]{:T(128)}, bf16[3584,512]{1,0:T(8,128)(2,1)}, bf16[256,3584]{1,0:T(8,128)(2,1)S(1)}, ...), condition=%wide.region_2.0_spmd, body=%wide.region_1.0_spmd.sunk | while | flops 100705558528 | bytes 12386453 | solution.py:363
  173.4 1.9 collective-permute-start
  175.4 2.0 collective-permute-done.refs_1_
  177.4 4.8 %expert_f.1 = (bf16[128,1792]{1,0:T(8,128)(2,1)S(1)}, bf16[128,1792]{1,0:T(8,128)(2,1)S(1)}) custom-call(bf16[128,1792]{1,0:T(8,128)(2,1)} %get-tuple-element.120.refs_0_, bf16[128,1792]{1,0:T(8,128)(2,1)S(1)} %collective-permute-done.refs_1_, bf16[3584,512]{1,0:T(8,128)(2,1)} %get-tuple-element.128.refs_2_, bf16[256,3584]{1,0:T(8,128)(2,1)S(1)} %get-tuple-element.129.refs_3_), custom_call_target="tpu_custom_call" | custom-call | flops 100704641024 | bytes 7340032 | tf_op jit(solution)/shard_map/while/body/expert_f/pallas_call | solution.py:211
  182.2 2.0 collective-permute-start.1
  184.3 1.7 collective-permute-done.1
  185.9 0.9 add_convert_fusion.2
  186.8 32.1 %all-to-all-start.1 = ((bf16[16,8,1792]{2,1,0:T(8,128)(2,1)}), bf16[16,8,1792]{2,1,0:T(8,128)(2,1)S(1)}, u32[]{:S(2)}, u32[]{:S(2)}) async-start(bf16[16,8,1792]{2,1,0:T(8,128)(2,1)} %bitcast.13), calls=%async_computation.1 | async-start | bytes 917504 | tf_op jit(solution)/shard_map/all_to_all | solution.py:257
  218.9 0.0 collective-permute-done.12.refs_1_
  218.9 0.0 collective-permute-done.13.refs_2_
  218.9 0.0 collective-permute-done.14.refs_3_
  218.9 0.0 copy-start.1
  218.9 0.0 copy-start.10
  218.9 0.0 copy-start.3
  219.0 1.3 merge_b.1
  220.3 12.0 %collective-permute-start.15 = (bf16[8,3584]{1,0:T(8,128)(2,1)S(1)}, bf16[8,3584]{1,0:T(8,128)(2,1)S(1)}, u32[]{:S(2)}, u32[]{:S(2)}) collective-permute-start(bf16[8,3584]{1,0:T(8,128)(2,1)S(1)} %get-tuple-element.62), channel_id=1, source_target_pairs={{0,24},{8,0},{16,8},{24,16},{1,25},{9,1},{17,9},{25,17},{2,26},{10... | collective-permute-start | bytes 172040 | tf_op jit(solution)/shard_map/ppermute | solution.py:225
  232.2 1.9 collective-permute-start.16
  234.2 2.8 %collective-permute-start.17 = (bf16[8,3584]{1,0:T(8,128)(2,1)S(1)}, bf16[8,3584]{1,0:T(8,128)(2,1)S(1)}, u32[]{:S(2)}, u32[]{:S(2)}) collective-permute-start(bf16[8,3584]{1,0:T(8,128)(2,1)S(1)} %get-tuple-element.64), channel_id=1, source_target_pairs={{0,8},{8,16},{16,24},{24,0},{1,9},{9,17},{17,25},{25,1},{2,10},{10... | collective-permute-start | bytes 172040 | tf_op jit(solution)/shard_map/ppermute | solution.py:225
  236.9 3.1 %collective-permute-done.16.refs_5_ = bf16[8,3584]{1,0:T(8,128)(2,1)S(1)} collective-permute-done((bf16[8,3584]{1,0:T(8,128)(2,1)S(1)}, bf16[8,3584]{1,0:T(8,128)(2,1)S(1)}, u32[]{:S(2)}, u32[]{:S(2)}) %collective-permute-start.16) | collective-permute-done | bytes 57376 | tf_op jit(solution)/shard_map/ppermute | solution.py:225
  240.0 1.4 collective-permute-done.17.refs_6_
  241.5 1.0 final_b.1
  242.5 1.9 collective-permute-start.18
  244.4 12.1 %collective-permute-done.18 = bf16[64,3584]{1,0:T(8,128)(2,1)S(1)} collective-permute-done((bf16[64,3584]{1,0:T(8,128)(2,1)S(1)}, bf16[64,3584]{1,0:T(8,128)(2,1)S(1)}, u32[]{:S(2)}, u32[]{:S(2)}) %collective-permute-start.18) | collective-permute-done | bytes 458784 | tf_op jit(solution)/shard_map/ppermute | solution.py:225
  256.5 1.3 final_f.1
  257.7 0.8 copy.20
  (26 shorter events, 0.1 us)
Async XLA Ops:
  0.6 53.1 %collective-permute-start.2 = (bf16[64,3584]{1,0:T(8,128)(2,1)}, bf16[64,3584]{1,0:T(8,128)(2,1)S(1)}, u32[]{:S(2)}, u32[]{:S(2)}) collective-permute-start(bf16[64,3584]{1,0:T(8,128)(2,1)} %bitcast.33), channel_id=1, source_target_pairs={{0,32},{32,64},{64,96},{96,128},{128,160},{160,192},{192,224},{224... | collective-permute-start | bytes 1376264 | tf_op jit(solution)/shard_map/ppermute | solution.py:225
  4.5 119.2 %copy-start.5 = (s32[3]{0:T(128)}, s32[3]{0:T(128)S(1)}, u32[]{:S(2)}) copy-start(s32[3]{0:T(128)S(1)} %pad_add_fusion.refs_0_) | copy-start | bytes 40
  4.5 1.0 copy-start
  5.6 0.7 copy-start.9
  6.2 0.7 copy-start.11
  6.9 12.3 %copy-start.15 = (s32[1,64,1]{1,2,0:T(1,128)S(1)}, s32[1,64,1]{1,2,0:T(1,128)}, u32[]{:S(2)}) copy-start(s32[1,64,1]{1,2,0:T(1,128)} %param.12) | copy-start | bytes 772
  6.9 12.9 %copy-start.14 = (f32[1,64,1]{1,2,0:T(1,128)S(1)}, f32[1,64,1]{1,2,0:T(1,128)}, u32[]{:S(2)}) copy-start(f32[1,64,1]{1,2,0:T(1,128)} %param.13) | copy-start | bytes 772
  7.8 15.9 %collective-permute-start.4 = (bf16[8,3584]{1,0:T(8,128)(2,1)S(1)}, bf16[8,3584]{1,0:T(8,128)(2,1)S(1)}, u32[]{:S(2)}, u32[]{:S(2)}) collective-permute-start(bf16[8,3584]{1,0:T(8,128)(2,1)S(1)} %get-tuple-element.49), channel_id=1, source_target_pairs={{0,8},{8,16},{16,24},{24,0},{1,9},{9,17},{17,25},{25,1},{2,10},{10... | collective-permute-start | bytes 172040 | tf_op jit(solution)/shard_map/ppermute | solution.py:225
  11.2 12.5 %collective-permute-start.5 = (bf16[8,3584]{1,0:T(8,128)(2,1)S(1)}, bf16[8,3584]{1,0:T(8,128)(2,1)S(1)}, u32[]{:S(2)}, u32[]{:S(2)}) collective-permute-start(bf16[8,3584]{1,0:T(8,128)(2,1)S(1)} %get-tuple-element.50), channel_id=1, source_target_pairs={{0,16},{8,24},{16,0},{24,8},{1,17},{9,25},{17,1},{25,9},{2,18},{10... | collective-permute-start | bytes 172040 | tf_op jit(solution)/shard_map/ppermute | solution.py:225
  15.8 7.9 %collective-permute-start.6 = (bf16[8,3584]{1,0:T(8,128)(2,1)S(1)}, bf16[8,3584]{1,0:T(8,128)(2,1)S(1)}, u32[]{:S(2)}, u32[]{:S(2)}) collective-permute-start(bf16[8,3584]{1,0:T(8,128)(2,1)S(1)} %get-tuple-element.51), channel_id=1, source_target_pairs={{0,24},{8,0},{16,8},{24,16},{1,25},{9,1},{17,9},{25,17},{2,26},{10... | collective-permute-start | bytes 172040 | tf_op jit(solution)/shard_map/ppermute | solution.py:225
  19.8 33.8 %collective-permute-start.3 = (f32[2,64]{1,0:T(2,128)S(1)}, f32[2,64]{1,0:T(2,128)S(1)}, u32[]{:S(2)}, u32[]{:S(2)}) collective-permute-start(f32[2,64]{1,0:T(2,128)S(1)} %pad_maximum_fusion), channel_id=1, source_target_pairs={{0,32},{32,64},{64,96},{96,128},{128,160},{160,192},{192,224},{224... | collective-permute-start | bytes 1544 | tf_op jit(solution)/shard_map/ppermute | solution.py:225
  23.9 96.1 %collective-permute-start.8 = (bf16[16,3584]{1,0:T(8,128)(2,1)S(1)}, bf16[16,3584]{1,0:T(8,128)(2,1)S(1)}, u32[]{:S(2)}, u32[]{:S(2)}) collective-permute-start(bf16[16,3584]{1,0:T(8,128)(2,1)S(1)} %get-tuple-element.54), channel_id=1, source_target_pairs={{0,6},{2,4},{4,2},{6,0},{1,7},{3,5},{5,3},{7,1},{8,14},{10,12},{12... | collective-permute-start | bytes 344072 | tf_op jit(solution)/shard_map/ppermute | solution.py:225
  39.4 80.6 %collective-permute-start.9 = (bf16[16,3584]{1,0:T(8,128)(2,1)S(1)}, bf16[16,3584]{1,0:T(8,128)(2,1)S(1)}, u32[]{:S(2)}, u32[]{:S(2)}) collective-permute-start(bf16[16,3584]{1,0:T(8,128)(2,1)S(1)} %get-tuple-element.54), channel_id=1, source_target_pairs={{0,4},{2,6},{4,0},{6,2},{1,5},{3,7},{5,1},{7,3},{8,12},{10,14},{12... | collective-permute-start | bytes 344072 | tf_op jit(solution)/shard_map/ppermute | solution.py:225
  51.7 68.2 %collective-permute-start.7 = (bf16[16,3584]{1,0:T(8,128)(2,1)S(1)}, bf16[16,3584]{1,0:T(8,128)(2,1)S(1)}, u32[]{:S(2)}, u32[]{:S(2)}) collective-permute-start(bf16[16,3584]{1,0:T(8,128)(2,1)S(1)} %get-tuple-element.52.refs_2_.refs_0_), channel_id=1, source_target_pairs={{0,2},{2,0},{4,6},{6,4},{1,3},{3,1},{5,7},{7,5},{8,10},{10,8},{12,... | collective-permute-start | bytes 344072 | tf_op jit(solution)/shard_map/ppermute | solution.py:225
  53.7 1.3 copy-start.7
  53.7 1.3 copy-start.2
  55.0 118.4 %all-to-all-start = ((bf16[16,8,1792]{2,1,0:T(8,128)(2,1)}), bf16[16,8,1792]{2,1,0:T(8,128)(2,1)}, u32[]{:S(2)}, u32[]{:S(2)}) async-start(bf16[16,8,1792]{2,1,0:T(8,128)(2,1)} %bitcast.9), calls=%async_computation | async-start | bytes 917504 | tf_op jit(solution)/shard_map/all_to_all | solution.py:257
  74.1 49.7 %copy-start.4 = (bf16[1,1,128,512]{3,2,1,0:T(8,128)(2,1)S(1)}, bf16[1,1,128,512]{3,2,1,0:T(8,128)(2,1)}, u32[]{:S(2)}) copy-start(bf16[1,1,128,512]{3,2,1,0:T(8,128)(2,1)} %param.17) | copy-start | bytes 393220
  74.1 49.7 %copy-start.12 = (bf16[1,3584,512]{2,1,0:T(8,128)(2,1)S(1)}, bf16[1,3584,512]{2,1,0:T(8,128)(2,1)}, u32[]{:S(2)}) copy-start(bf16[1,3584,512]{2,1,0:T(8,128)(2,1)} %param.18) | copy-start | bytes 11010052
  74.1 49.6 %copy-start.13 = (bf16[1,256,3584]{2,1,0:T(8,128)(2,1)S(1)}, bf16[1,256,3584]{2,1,0:T(8,128)(2,1)}, u32[]{:S(2)}) copy-start(bf16[1,256,3584]{2,1,0:T(8,128)(2,1)} %param.19) | copy-start | bytes 5505028
  120.0 3.7 %collective-permute-start.10 = (bf16[64,3584]{1,0:T(8,128)(2,1)S(1)}, bf16[64,3584]{1,0:T(8,128)(2,1)S(1)}, u32[]{:S(2)}, u32[]{:S(2)}) collective-permute-start(bf16[64,3584]{1,0:T(8,128)(2,1)S(1)} %join_b.1.refs_1_), channel_id=1, source_target_pairs={{0,1},{1,0},{2,3},{3,2},{4,5},{5,4},{6,7},{7,6},{8,9},{9,8},{10,11... | collective-permute-start | bytes 1376264 | tf_op jit(solution)/shard_map/ppermute | solution.py:225
  127.0 3.7 %collective-permute-start.11 = (bf16[64,3584]{1,0:T(8,128)(2,1)S(1)}, bf16[64,3584]{1,0:T(8,128)(2,1)S(1)}, u32[]{:S(2)}, u32[]{:S(2)}) collective-permute-start(bf16[64,3584]{1,0:T(8,128)(2,1)S(1)} %get-tuple-element.56), channel_id=1, source_target_pairs={{0,1},{1,0},{2,3},{3,2},{4,5},{5,4},{6,7},{7,6},{8,9},{9,8},{10,11... | collective-permute-start | bytes 1376264 | tf_op jit(solution)/shard_map/ppermute | solution.py:225
  131.5 87.4 %collective-permute-start.12 = (bf16[16,3584]{1,0:T(8,128)(2,1)}, bf16[16,3584]{1,0:T(8,128)(2,1)}, u32[]{:S(2)}, u32[]{:S(2)}) collective-permute-start(bf16[16,3584]{1,0:T(8,128)(2,1)} %get-tuple-element.58), channel_id=1, source_target_pairs={{0,2},{2,0},{4,6},{6,4},{1,3},{3,1},{5,7},{7,5},{8,10},{10,8},{12,... | collective-permute-start | bytes 344072 | tf_op jit(solution)/shard_map/ppermute | solution.py:225
  159.4 59.5 %collective-permute-start.13 = (bf16[16,3584]{1,0:T(8,128)(2,1)}, bf16[16,3584]{1,0:T(8,128)(2,1)}, u32[]{:S(2)}, u32[]{:S(2)}) collective-permute-start(bf16[16,3584]{1,0:T(8,128)(2,1)} %get-tuple-element.59), channel_id=1, source_target_pairs={{0,6},{2,4},{4,2},{6,0},{1,7},{3,5},{5,3},{7,1},{8,14},{10,12},{12... | collective-permute-start | bytes 344072 | tf_op jit(solution)/shard_map/ppermute | solution.py:225
  161.3 57.6 %collective-permute-start.14 = (bf16[16,3584]{1,0:T(8,128)(2,1)}, bf16[16,3584]{1,0:T(8,128)(2,1)}, u32[]{:S(2)}, u32[]{:S(2)}) collective-permute-start(bf16[16,3584]{1,0:T(8,128)(2,1)} %get-tuple-element.60), channel_id=1, source_target_pairs={{0,4},{2,6},{4,0},{6,2},{1,5},{3,7},{5,1},{7,3},{8,12},{10,14},{12... | collective-permute-start | bytes 344072 | tf_op jit(solution)/shard_map/ppermute | solution.py:225
  173.4 3.9 %collective-permute-start = (bf16[128,1792]{1,0:T(8,128)(2,1)}, bf16[128,1792]{1,0:T(8,128)(2,1)S(1)}, u32[]{:S(2)}, u32[]{:S(2)}) collective-permute-start(bf16[128,1792]{1,0:T(8,128)(2,1)} %get-tuple-element.120.refs_0_), channel_id=1, source_target_pairs={{0,1},{1,0},{2,3},{3,2},{4,5},{5,4},{6,7},{7,6},{8,9},{9,8},{10,11... | collective-permute-start | bytes 1376264 | tf_op jit(solution)/shard_map/while/body/ppermute | solution.py:225
  182.2 3.7 %collective-permute-start.1 = (bf16[128,1792]{1,0:T(8,128)(2,1)S(1)}, bf16[128,1792]{1,0:T(8,128)(2,1)S(1)}, u32[]{:S(2)}, u32[]{:S(2)}) collective-permute-start(bf16[128,1792]{1,0:T(8,128)(2,1)S(1)} %get-tuple-element.111), channel_id=1, source_target_pairs={{0,1},{1,0},{2,3},{3,2},{4,5},{5,4},{6,7},{7,6},{8,9},{9,8},{10,11... | collective-permute-start | bytes 1376264 | tf_op jit(solution)/shard_map/while/body/ppermute | solution.py:225
  186.8 69.7 %all-to-all-start.1 = ((bf16[16,8,1792]{2,1,0:T(8,128)(2,1)}), bf16[16,8,1792]{2,1,0:T(8,128)(2,1)S(1)}, u32[]{:S(2)}, u32[]{:S(2)}) async-start(bf16[16,8,1792]{2,1,0:T(8,128)(2,1)} %bitcast.13), calls=%async_computation.1 | async-start | bytes 917504 | tf_op jit(solution)/shard_map/all_to_all | solution.py:257
  218.9 22.5 %copy-start.1 = (bf16[1,64,3584]{2,1,0:T(8,128)(2,1)S(1)}, bf16[1,64,3584]{2,1,0:T(8,128)(2,1)}, u32[]{:S(2)}) copy-start(bf16[1,64,3584]{2,1,0:T(8,128)(2,1)} %param.14) | copy-start | bytes 1376260
  218.9 22.5 %copy-start.6 = (s32[3]{0:T(128)S(1)}, s32[3]{0:T(128)}, u32[]{:S(2)}) copy-start(s32[3]{0:T(128)} %copy-done.5) | copy-start | bytes 40
  218.9 22.5 %copy-start.10 = (s32[1,64,1]{1,2,0:T(1,128)S(1)}, s32[1,64,1]{1,2,0:T(1,128)}, u32[]{:S(2)}) copy-start(s32[1,64,1]{1,2,0:T(1,128)} %param.15) | copy-start | bytes 772
  218.9 37.5 %copy-start.3 = (bf16[64,3584]{1,0:T(8,128)(2,1)S(1)}, bf16[64,3584]{1,0:T(8,128)(2,1)}, u32[]{:S(2)}) copy-start(bf16[64,3584]{1,0:T(8,128)(2,1)} %copy-done.2) | copy-start | bytes 1376260
  219.0 37.5 %copy-start.8 = (f32[2,64]{1,0:T(2,128)S(1)}, f32[2,64]{1,0:T(2,128)}, u32[]{:S(2)}) copy-start(f32[2,64]{1,0:T(2,128)} %copy-done.7) | copy-start | bytes 1540
  220.3 16.7 %collective-permute-start.15 = (bf16[8,3584]{1,0:T(8,128)(2,1)S(1)}, bf16[8,3584]{1,0:T(8,128)(2,1)S(1)}, u32[]{:S(2)}, u32[]{:S(2)}) collective-permute-start(bf16[8,3584]{1,0:T(8,128)(2,1)S(1)} %get-tuple-element.62), channel_id=1, source_target_pairs={{0,24},{8,0},{16,8},{24,16},{1,25},{9,1},{17,9},{25,17},{2,26},{10... | collective-permute-start | bytes 172040 | tf_op jit(solution)/shard_map/ppermute | solution.py:225
  232.2 7.8 %collective-permute-start.16 = (bf16[8,3584]{1,0:T(8,128)(2,1)S(1)}, bf16[8,3584]{1,0:T(8,128)(2,1)S(1)}, u32[]{:S(2)}, u32[]{:S(2)}) collective-permute-start(bf16[8,3584]{1,0:T(8,128)(2,1)S(1)} %get-tuple-element.63), channel_id=1, source_target_pairs={{0,16},{8,24},{16,0},{24,8},{1,17},{9,25},{17,1},{25,9},{2,18},{10... | collective-permute-start | bytes 172040 | tf_op jit(solution)/shard_map/ppermute | solution.py:225
  234.2 7.3 %collective-permute-start.17 = (bf16[8,3584]{1,0:T(8,128)(2,1)S(1)}, bf16[8,3584]{1,0:T(8,128)(2,1)S(1)}, u32[]{:S(2)}, u32[]{:S(2)}) collective-permute-start(bf16[8,3584]{1,0:T(8,128)(2,1)S(1)} %get-tuple-element.64), channel_id=1, source_target_pairs={{0,8},{8,16},{16,24},{24,0},{1,9},{9,17},{17,25},{25,1},{2,10},{10... | collective-permute-start | bytes 172040 | tf_op jit(solution)/shard_map/ppermute | solution.py:225
  242.5 14.0 %collective-permute-start.18 = (bf16[64,3584]{1,0:T(8,128)(2,1)S(1)}, bf16[64,3584]{1,0:T(8,128)(2,1)S(1)}, u32[]{:S(2)}, u32[]{:S(2)}) collective-permute-start(bf16[64,3584]{1,0:T(8,128)(2,1)S(1)} %final_b.1), channel_id=1, source_target_pairs={{0,992},{32,0},{64,32},{96,64},{128,96},{160,128},{192,160},{224,1... | collective-permute-start | bytes 1376264 | tf_op jit(solution)/shard_map/ppermute | solution.py:225

commit v3 on v2

v3 whole, which is shorter than its diff:
```python
import jax
import jax.numpy as jnp
from jax import lax
from jax.experimental import pallas as pl
from jax.experimental.pallas import tpu as pltpu
from jax.sharding import Mesh
from jax.sharding import PartitionSpec as P

CORES = 2
Z_GROUPS = 4
SPLIT = 4
HIDES = {"pack_b": 1e11, "pack_f": 1e11, "merge_b": 1e11}
F32 = jnp.float32
BF16 = jnp.bfloat16
VMEM = pl.BlockSpec(memory_space=pltpu.VMEM)
ANY = pl.BlockSpec(memory_space=pl.ANY)
SMEM = pl.BlockSpec(memory_space=pltpu.SMEM)
PARAMS = pltpu.CompilerParams(vmem_limit_bytes=44 * 1024 * 1024)


def iota(shape, axis):
    return lax.broadcasted_iota(jnp.int32, shape, axis)


def dot(a, b, dims=((1,), (0,))):
    return lax.dot_general(a, b, (dims, ((), ())), preferred_element_type=F32)


def ones_at(where):
    return jnp.where(where, 1.0, 0.0).astype(BF16)


def slots_of(route, experts):
    tokens = route.shape[1]
    onehot = jnp.where(iota((experts, tokens), 0) == route, 1.0, 0.0)
    shape = (tokens, tokens)
    before = dot(onehot.astype(BF16), ones_at(iota(shape, 0) < iota(shape, 1)))
    return jnp.sum(before * onehot, axis=0, keepdims=True).astype(jnp.int32)


def column(row):
    tokens = row.shape[1]
    shape = (tokens, tokens)
    on = iota(shape, 0) == iota(shape, 1)
    return jnp.sum(jnp.where(on, row, jnp.zeros((), row.dtype)), axis=1, keepdims=True)


def joined(rows, cap):
    count = rows.shape[0]
    shape = (count // 2, count)
    r, m = iota(shape, 0), iota(shape, 1)
    same = (m // (2 * cap) == r // cap) & (m % cap == r % cap)
    low = (m % (2 * cap)) // cap == 0
    parts = [dot(ones_at(same & half), rows).astype(BF16) for half in (low, ~low)]
    return jnp.concatenate(parts, axis=1)


def parted(low, high, cap, rows):
    shape = (rows, rows // 2)
    m, r = iota(shape, 0), iota(shape, 1)
    same = (m // (2 * cap) == r // cap) & (m % cap == r % cap)
    first = (m % (2 * cap)) // cap == 0
    return (dot(ones_at(same & first), low) + dot(ones_at(same & ~first), high)).astype(BF16)


def source_of(at_ref, d, block, count):
    return (at_ref[0] + count - d) % count, at_ref[1] ^ block ^ (block // 2)


def slab(refs):
    return jnp.concatenate([r[...] for r in refs], axis=0)


def cut(rows, refs):
    size = rows.shape[0] // len(refs)
    for i, ref in enumerate(refs):
        ref[...] = rows[i * size : (i + 1) * size]


def pack_b_kernel(experts, cap, cot_ref, route_ref, gate_ref, out_ref):
    tokens, width = cot_ref.shape
    rows, half = out_ref.shape
    scaled = (column(gate_ref[...]) * cot_ref[...].astype(F32)).astype(BF16)
    route = route_ref[...]
    slot = slots_of(route, experts)
    m = iota((rows, tokens), 0)
    table = (m // (4 * cap) == route) & (m % cap == slot)
    low = (m % (2 * cap)) // cap == 0
    total = dot(ones_at(table & low), scaled[:, :half])
    total += dot(ones_at(table & ~low), scaled[:, half:])
    out_ref[...] = total.astype(BF16)


def expert_b_kernel(cap, c_ref, own_ref, oth_ref, saved_ref, wgu_ref, wd_ref, mine_ref, send_ref):
    rows, half = own_ref.shape
    hid, width = wd_ref.shape
    values = jnp.concatenate([joined(own_ref[...], cap), joined(oth_ref[...], cap)], axis=0)
    dh = dot(values, wd_ref[...], ((1,), (1,)))
    r, p = iota((rows, rows), 0), iota((rows, rows), 1)
    core = jnp.where(r < rows // 2, c_ref[0], 1 - c_ref[0])
    r = r % (rows // 2)
    pick = (p // (2 * cap) == r // cap) & (p % cap == r % cap) & ((p % (2 * cap)) // cap == core)
    saved = dot(ones_at(pick), saved_ref[...])
    act = saved[:, :hid]
    lin = saved[:, hid:]
    sig = 1.0 / (1.0 + jnp.exp(-act))
    d_act = (dh * lin * sig * (1.0 + act * (1.0 - sig))).astype(BF16)
    d_lin = (dh * act * sig).astype(BF16)
    grads = jnp.concatenate([d_act, d_lin], axis=1)
    step = 256 if half % 256 == 0 else half
    for at in range(0, half, step):
        low, high = (
            dot(grads, wgu_ref[base + at : base + at + step, :], ((1,), (1,))).astype(BF16)
            for base in (0, half)
        )
        mid = rows // 2
        mine_ref[:, at : at + step] = parted(low[:mid], high[:mid], cap, rows)
        send_ref[:, at : at + step] = parted(low[mid:], high[mid:], cap, rows)


def split_b_kernel(cap, at_ref, rows_ref, *out_refs):
    rows = joined(rows_ref[...], cap)
    count = rows.shape[0] // (Z_GROUPS * cap)
    shape = (rows.shape[0], rows.shape[0])
    r, m = iota(shape, 0), iota(shape, 1)
    x, z = source_of(at_ref, (r // cap) % count, r // (count * cap), count)
    pick = m == (x * Z_GROUPS + z) * cap + r % cap
    cut(dot(ones_at(pick), rows).astype(BF16), out_refs)


def merge_kernel(cap, here_ref, partner_ref, mirror_ref, opposite_ref, *out_refs):
    rows = jnp.concatenate([r[...] for r in (here_ref, partner_ref, mirror_ref, opposite_ref)], axis=0)
    shape = (len(out_refs) * 2 * cap, rows.shape[0])
    block = here_ref.shape[0]
    r, m = iota(shape, 0), iota(shape, 1)
    same = ((m % block) // cap == r // (2 * cap)) & (m % cap == r % cap)
    same = same & (m // (2 * block) == (r % (2 * cap)) // cap)
    merged = dot(ones_at(same), rows).astype(BF16)
    for d, out_ref in enumerate(out_refs):
        out_ref[...] = merged[d * 2 * cap : (d + 1) * 2 * cap]


def final_b_kernel(experts, cap, at_ref, cot_ref, route_ref, *refs):
    *in_refs, out_ref = refs
    tokens = cot_ref.shape[0]
    count = len(in_refs)
    rows = jnp.concatenate([r[...] for r in in_refs], axis=0)
    route = route_ref[...]
    slot = column(slots_of(route, experts))
    m = iota((tokens, rows.shape[0]), 1)
    pair = at_ref[1] // 2 ^ ((m % (2 * cap)) // cap)
    expert = (at_ref[0] + m // (2 * cap)) % count * 2 + pair
    total = dot(ones_at((expert == column(route)) & (m % cap == slot)), rows)
    out_ref[...] = (cot_ref[...].astype(F32) + total).astype(BF16)


def pack_f_kernel(experts, cap, at_ref, x_ref, meta_ref, *out_refs):
    tokens = x_ref.shape[0]
    route = meta_ref[0:1, :].astype(jnp.int32)
    slot = slots_of(route, experts)
    count = len(out_refs)
    m = iota((count * 2 * cap, tokens), 0)
    pair = at_ref[1] // 2 ^ ((m % (2 * cap)) // cap)
    expert = (at_ref[0] + m // (2 * cap)) % count * 2 + pair
    packed = dot(ones_at((expert == route) & (m % cap == slot)), x_ref[...]).astype(BF16)
    cut(packed, out_refs)


def pairs_kernel(cap, *refs):
    *in_refs, own_ref, oth_ref = refs
    rows = slab(in_refs)
    shape = (own_ref.shape[0], rows.shape[0])
    r, m = iota(shape, 0), iota(shape, 1)
    same = (m // (2 * cap) == r // cap) & (m % cap == r % cap)
    own = (m % (2 * cap)) // cap == 0
    own_ref[...] = dot(ones_at(same & own), rows).astype(BF16)
    oth_ref[...] = dot(ones_at(same & ~own), rows).astype(BF16)


def join_kernel(*refs):
    refs[-1][...] = slab(refs[:-1])


def expert_f_kernel(own_ref, oth_ref, wgu_ref, wd_ref, mine_ref, send_ref):
    rows = own_ref.shape[0]
    hid, width = wd_ref.shape
    pre = dot(slab((own_ref, oth_ref)), wgu_ref[...])
    gate = pre[:, :hid]
    hidden = (gate / (1.0 + jnp.exp(-gate)) * pre[:, hid:]).astype(BF16)
    step = 512 if width % 512 == 0 else width
    for at in range(0, width, step):
        part = dot(hidden, wd_ref[:, at : at + step]).astype(BF16)
        mine_ref[:, at : at + step] = part[:rows]
        send_ref[:, at : at + step] = part[rows:]


def add_kernel(a_ref, b_ref, *out_refs):
    cut((a_ref[...].astype(F32) + b_ref[...].astype(F32)).astype(BF16), out_refs)


def spread_f_kernel(cap, at_ref, *refs):
    *in_refs, out_ref = refs
    rows = slab(in_refs)
    many, half = out_ref.shape
    count = rows.shape[0] // (Z_GROUPS * cap)
    shape = (many, rows.shape[0])
    m, r = iota(shape, 0), iota(shape, 1)
    x, z = source_of(at_ref, (r // cap) % count, r // (count * cap), count)
    pick = (m // (2 * cap) == x * Z_GROUPS + z) & (m % cap == r % cap)
    low = (m % (2 * cap)) // cap == 0
    total = dot(ones_at(pick & low), rows[:, :half]) + dot(ones_at(pick & ~low), rows[:, half:])
    out_ref[...] = total.astype(BF16)


def final_f_kernel(experts, cap, x_ref, meta_ref, back_ref, out_ref):
    tokens = x_ref.shape[0]
    rows, half = back_ref.shape
    meta = meta_ref[...]
    route = meta[0:1, :].astype(jnp.int32)
    slot = column(slots_of(route, experts))
    gate = column(meta[1:2, :])
    m = iota((tokens, rows), 1)
    table = (m // (4 * cap) == column(route)) & (m % cap == slot)
    low = (m % (2 * cap)) // cap == 0
    back = back_ref[...]
    for base, part in ((0, low), (half, ~low)):
        total = gate * dot(ones_at(table & part), back)
        x = x_ref[:, base : base + half].astype(F32)
        out_ref[:, base : base + half] = (x + total).astype(BF16)


def call(kernel, name, shapes, operands, flops, earlier=()):
    out = [jax.ShapeDtypeStruct(s, BF16) for s in shapes]
    nbytes = sum(a.size * a.dtype.itemsize for a in (*operands, *out))
    count = len(operands)

    def body(*refs):
        kernel(*refs[:count], *refs[count + len(earlier) :])

    return pl.pallas_call(
        body,
        out_shape=out,
        in_specs=[SMEM if a.ndim == 1 else VMEM for a in operands] + [ANY] * len(earlier),
        out_specs=[VMEM] * len(out),
        compiler_params=PARAMS,
        name=name,
        cost_estimate=pl.CostEstimate(
            flops=flops + int(HIDES.get(name, 0)), bytes_accessed=nbytes, transcendentals=0
        ),
    )(*operands, *earlier)


def moved(block, axis, to):
    return lax.ppermute(block, axis, [(i, to(i)) for i in range(lax.axis_size(axis))])


def swap_core(block):
    return moved(block, "c", lambda i: 1 - i)


def shift(block, distance):
    count = lax.axis_size("pp")
    return moved(block, "pp", lambda i: (i + distance) % count)


def along_x(blocks, sign):
    count = len(blocks)
    rest = [moved(b, "x", lambda i, d=d: (i + sign * d) % count) for d, b in enumerate(blocks) if d]
    return [blocks[0]] + rest


def exchange(rows, cap):
    width = rows.shape[1]
    blocks = rows.reshape(-1, 2 * cap, width)
    blocks = lax.all_to_all(blocks, ("x", "zh"), split_axis=0, concat_axis=0, tiled=True)
    return blocks.reshape(-1, width)


def partner(block):
    return moved(block, "zh", lambda i: i ^ 1)


def mirror(block):
    return moved(block, "zh", lambda i: 3 - i)


def opposite(block):
    return moved(block, "zh", lambda i: i ^ 2)


def shards(fwd_in, fwd_route, fwd_gate, bwd_cot, bwd_route, bwd_gate, saved_pre, w_gate_up, w_down):
    devices = lax.axis_size(("x", "zh", "c"))
    experts = devices // SPLIT
    cap = saved_pre.shape[2] // devices
    cot = bwd_cot[0]
    tokens, width = cot.shape
    hid = w_down.shape[1]
    wgu, wd = w_gate_up[0], w_down[0]
    at = jnp.stack([lax.axis_index(a) for a in ("x", "zh", "c")]).astype(jnp.int32)
    many = devices * cap
    few = many // 2
    half = (many, width // 2)
    block = few // Z_GROUPS

    def kernel(body, *head):
        return lambda *refs: body(*head, *refs)

    route_b, gate_b = bwd_route.reshape(1, tokens), bwd_gate.reshape(1, tokens)
    meta = jnp.concatenate(
        [fwd_route.reshape(1, tokens).astype(F32), fwd_gate.reshape(1, tokens)], axis=0
    )
    x = shift(fwd_in[0], 1)
    meta = shift(meta, 1)
    core = at[2:]
    rounds = jnp.minimum(jnp.sum((bwd_route < experts).astype(jnp.int32)), 1)

    (packed,) = call(
        kernel(pack_b_kernel, experts, cap),
        "pack_b",
        [half],
        (cot, route_b, gate_b),
        2 * many * tokens * width,
    )
    own_b = exchange(packed, cap)

    chunks = call(
        kernel(pack_f_kernel, experts, cap),
        "pack_f",
        [(2 * cap, width)] * (block // cap),
        (at, x, meta),
        4 * block * tokens * width,
        earlier=(packed,),
    )
    chunks = along_x(chunks, 1)
    here, away = call(
        kernel(pairs_kernel, cap), "pairs_f", [(block, width)] * 2, chunks, 4 * block * block * width
    )
    blocks_f = (here, partner(here), mirror(away), opposite(away))

    def chain_b(_, rows):
        mine, send = call(
            kernel(expert_b_kernel, cap),
            "expert_b",
            [half] * 2,
            (core, rows, swap_core(rows), saved_pre[0, 0], wgu, wd),
            6 * many * hid * width,
        )
        return (mine.astype(F32) + swap_core(send).astype(F32)).astype(BF16)

    summed_b = lax.fori_loop(0, rounds, chain_b, own_b)
    here, to_partner, to_mirror, to_opposite = call(
        kernel(split_b_kernel, cap),
        "split_b",
        [(block, width)] * Z_GROUPS,
        (at, summed_b),
        2 * few * many * width,
    )
    blocks_b = (here, partner(to_partner), mirror(to_mirror), opposite(to_opposite))

    def chain_f(_, blocks):
        (own,) = call(join_kernel, "join_f", [(few, width)], blocks, few * width)
        mine, send = call(
            expert_f_kernel, "expert_f", [(few, width)] * 2, (own, swap_core(own), wgu, wd), 6 * many * hid * width
        )
        return tuple(
            call(add_kernel, "add_f", [(block, width)] * Z_GROUPS, (mine, swap_core(send)), few * width)
        )

    summed_f = lax.fori_loop(0, rounds, chain_f, blocks_f)
    (spread,) = call(
        kernel(spread_f_kernel, cap), "spread_f", [half], (at, *summed_f), 2 * few * many * width
    )
    back_f = exchange(spread, cap)

    chunks = call(
        kernel(merge_kernel, cap),
        "merge_b",
        [(2 * cap, width)] * (block // cap),
        blocks_b,
        4 * block * few * width,
    )
    chunks = along_x(chunks, -1)
    (out_b,) = call(
        kernel(final_b_kernel, experts, cap),
        "final_b",
        [(tokens, width)],
        (at, cot, route_b, *chunks),
        4 * block * tokens * width,
    )
    out_b = shift(out_b, -1)
    (out_f,) = call(
        kernel(final_f_kernel, experts, cap),
        "final_f",
        [(tokens, width)],
        (x, meta, back_f),
        2 * many * tokens * width,
    )
    return out_f[None], out_b[None]


def solution(mesh):
    sections, members = mesh.devices.shape
    fine = Mesh(
        mesh.devices.reshape(sections, members // (Z_GROUPS * CORES), Z_GROUPS, CORES),
        ("pp", "x", "zh", "c"),
    )
    ep = ("x", "zh", "c")
    rows = P("pp", ep, None)
    return jax.shard_map(
        shards,
        mesh=fine,
        in_specs=(rows,) * 6 + (P("pp", ep, None, None), P(ep, None, None), P(ep, None, None)),
        out_specs=(rows, rows),
        check_vma=False,
    )
```

time: 259 us -> 246 us (0.950)
  the two profiles are of different devices: /device:TPU:184 before, /device:TPU:217 now
where the time goes in v3:
time: 246 us
  starting transfers between devices  145 us (59%)
  waiting for transfers between devices  75 us (30%)
  Pallas kernels  18.1 us (7%)
  local copies, waits for them, and re-layouts  3.1 us (1%)
    ppermute x19, starting transfers between devices, moved(): lax.ppermute(block, axis, [(i, to(i)) for i in range(lax.axis_size(axis))])  102 us
    all_to_all x2, starting transfers between devices, exchange(): lax.all_to_all(blocks, ('x', 'zh'), split_axis=0, concat_axis=0, tiled=True)  43.7 us
    all_to_all x2, waiting for transfers between devices, exchange(): lax.all_to_all(blocks, ('x', 'zh'), split_axis=0, concat_axis=0, tiled=True)  41.7 us
    ppermute x19, waiting for transfers between devices, moved(): lax.ppermute(block, axis, [(i, to(i)) for i in range(lax.axis_size(axis))])  33.3 us
    pallas_call x12, Pallas kernels, call(): pl.pallas_call(body, out_shape=out, in_specs=[SMEM if a.ndim == 1 else VM...  18.1 us
  transfers between devices with their start and end apart: 21, of which 10 were waited for; matrix products, arithmetic and copies ran while one was open for 0% of the time, Pallas kernels for 7%

profile of v3, /device:TPU:217, one launch (start us, length us, event | category | flops | bytes accessed | tf_op | source)
XLA Modules:
  0.0 245.5 jit_solution(13070325668824330242)
XLA Ops:
  0.6 0.7 convert_bitcast_fusion
  1.3 0.7 pad_maximum_fusion
  2.0 3.5 %collective-permute-start.5 = (f32[2,64]{1,0:T(2,128)S(1)}, f32[2,64]{1,0:T(2,128)S(1)}, u32[]{:S(2)}, u32[]{:S(2)}) collective-permute-start(f32[2,64]{1,0:T(2,128)S(1)} %pad_maximum_fusion), channel_id=1, source_target_pairs={{0,32},{32,64},{64,96},{96,128},{128,160},{160,192},{192,224},{224... | collective-permute-start | bytes 1544 | tf_op jit(solution)/shard_map/ppermute | solution.py:254
  5.5 1.9 collective-permute-start.4
  7.4 0.0 copy-start
  7.4 1.0 copy-done
  8.4 0.7 copy-done.2
  9.1 0.7 copy-done.4
  9.8 1.3 pack_b.1.refs_3_
  11.0 27.4 %all-to-all-start.1 = ((bf16[16,8,1792]{2,1,0:T(8,128)(2,1)}), bf16[16,8,1792]{2,1,0:T(8,128)(2,1)S(1)}, u32[]{:S(2)}, u32[]{:S(2)}) async-start(bf16[16,8,1792]{2,1,0:T(8,128)(2,1)} %bitcast.15), calls=%async_computation.1 | async-start | bytes 917504 | tf_op jit(solution)/shard_map/all_to_all | solution.py:275
  38.4 0.1 pad_add_fusion.refs_0_
  38.5 0.0 collective-permute-done.5.refs_2_.refs_1_
  38.5 0.0 collective-permute-done.4.refs_1_.refs_0_
  38.5 0.9 pack_f.1
  39.4 3.3 %collective-permute-start.6 = (bf16[8,3584]{1,0:T(8,128)(2,1)S(1)}, bf16[8,3584]{1,0:T(8,128)(2,1)S(1)}, u32[]{:S(2)}, u32[]{:S(2)}) collective-permute-start(bf16[8,3584]{1,0:T(8,128)(2,1)S(1)} %get-tuple-element.109), channel_id=1, source_target_pairs={{0,8},{8,16},{16,24},{24,0},{1,9},{9,17},{17,25},{25,1},{2,10},{10... | collective-permute-start | bytes 172040 | tf_op jit(solution)/shard_map/ppermute | solution.py:254
  42.7 4.3 %collective-permute-start.7 = (bf16[8,3584]{1,0:T(8,128)(2,1)S(1)}, bf16[8,3584]{1,0:T(8,128)(2,1)S(1)}, u32[]{:S(2)}, u32[]{:S(2)}) collective-permute-start(bf16[8,3584]{1,0:T(8,128)(2,1)S(1)} %get-tuple-element.110), channel_id=1, source_target_pairs={{0,16},{8,24},{16,0},{24,8},{1,17},{9,25},{17,1},{25,9},{2,18},{10... | collective-permute-start | bytes 172040 | tf_op jit(solution)/shard_map/ppermute | solution.py:254
  47.0 3.1 %collective-permute-start.8 = (bf16[8,3584]{1,0:T(8,128)(2,1)S(1)}, bf16[8,3584]{1,0:T(8,128)(2,1)S(1)}, u32[]{:S(2)}, u32[]{:S(2)}) collective-permute-start(bf16[8,3584]{1,0:T(8,128)(2,1)S(1)} %get-tuple-element.111), channel_id=1, source_target_pairs={{0,24},{8,0},{16,8},{24,16},{1,25},{9,1},{17,9},{25,17},{2,26},{10... | collective-permute-start | bytes 172040 | tf_op jit(solution)/shard_map/ppermute | solution.py:254
  50.1 0.7 fusion
  51.5 0.0 collective-permute-done.6.refs_1_
  51.5 0.0 collective-permute-done.7.refs_2_
  51.5 0.7 collective-permute-done.8.refs_3_
  52.2 0.2 pairs_f.1
  52.4 21.4 %collective-permute-start.11 = (bf16[16,3584]{1,0:T(8,128)(2,1)S(1)}, bf16[16,3584]{1,0:T(8,128)(2,1)S(1)}, u32[]{:S(2)}, u32[]{:S(2)}) collective-permute-start(bf16[16,3584]{1,0:T(8,128)(2,1)S(1)} %get-tuple-element.113), channel_id=1, source_target_pairs={{0,4},{2,6},{4,0},{6,2},{1,5},{3,7},{5,1},{7,3},{8,12},{10,14},{12... | collective-permute-start | bytes 344072 | tf_op jit(solution)/shard_map/ppermute | solution.py:254
  73.8 2.0 collective-permute-start.10
  75.8 2.4 collective-permute-start.9
  78.2 25.3 %all-to-all-done.1 = bf16[16,8,1792]{2,1,0:T(8,128)(2,1)S(1)} async-done(((bf16[16,8,1792]{2,1,0:T(8,128)(2,1)}), bf16[16,8,1792]{2,1,0:T(8,128)(2,1)S(1)}, u32[]{:S(2)}, u32[]{:S(2)}) %all-to-all-start.1) | async-done | bytes 458784 | tf_op jit(solution)/shard_map/all_to_all | solution.py:275
  103.5 15.2 %while.27 = (s32[]{:T(128)}, bf16[128,1792]{1,0:T(8,128)(2,1)S(1)}, s32[]{:T(128)}, bf16[1,1,128,512]{3,2,1,0:T(8,128)(2,1)S(1)}, s32[1]{0:T(128)}, /*index=5*/b...) while((s32[]{:T(128)}, bf16[128,1792]{1,0:T(8,128)(2,1)S(1)}, s32[]{:T(128)}, ...), condition=%wide.region_4.0_spmd, body=%wide.region_3.0_spmd.sunk | while | flops 705560576 | bytes 12517545 | solution.py:350
  103.5 3.1 %collective-permute-start.2 = (bf16[128,1792]{1,0:T(8,128)(2,1)S(1)}, bf16[128,1792]{1,0:T(8,128)(2,1)S(1)}, u32[]{:S(2)}, u32[]{:S(2)}) collective-permute-start(bf16[128,1792]{1,0:T(8,128)(2,1)S(1)} %get-tuple-element.303.refs_1_), channel_id=1, source_target_pairs={{0,1},{1,0},{2,3},{3,2},{4,5},{5,4},{6,7},{7,6},{8,9},{9,8},{10,11... | collective-permute-start | bytes 1376264 | tf_op jit(solution)/shard_map/while/body/ppermute | solution.py:254
  106.6 1.4 collective-permute-done.2.refs_2_
  108.0 6.8 %expert_b.1 = (bf16[128,1792]{1,0:T(8,128)(2,1)S(1)}, bf16[128,1792]{1,0:T(8,128)(2,1)S(1)}) custom-call(s32[1]{0:T(128)} %get-tuple-element.314.refs_0_, bf16[128,1792]{1,0:T(8,128)(2,1)S(1)} %get-tuple-element.303.refs_1_, bf16[128,1792]{1,0:T(8,128)(2,1)S(1)} %collective-permute-done.2.refs_2_, bf16[128,512]{1,0:T(8,128)(2,1)S(1)} %bitcast.30, ...), custom_call_target="tpu_custom_call" | custom-call | flops 704643072 | bytes 7471108 | tf_op jit(solution)/shard_map/while/body/expert_b/pallas_call | solution.py:240
  114.8 2.3 collective-permute-start.3
  117.1 1.4 collective-permute-done.3
  118.5 0.1 add_convert_fusion.2
  118.6 1.0 split_b.1
  119.6 24.2 %collective-permute-start.12 = (bf16[16,3584]{1,0:T(8,128)(2,1)S(1)}, bf16[16,3584]{1,0:T(8,128)(2,1)S(1)}, u32[]{:S(2)}, u32[]{:S(2)}) collective-permute-start(bf16[16,3584]{1,0:T(8,128)(2,1)S(1)} %get-tuple-element.120), channel_id=1, source_target_pairs={{0,2},{2,0},{4,6},{6,4},{1,3},{3,1},{5,7},{7,5},{8,10},{10,8},{12,... | collective-permute-start | bytes 344072 | tf_op jit(solution)/shard_map/ppermute | solution.py:254
  143.8 1.9 collective-permute-start.13
  145.8 0.0 collective-permute-done.9
  145.8 11.8 %collective-permute-start.14 = (bf16[16,3584]{1,0:T(8,128)(2,1)S(1)}, bf16[16,3584]{1,0:T(8,128)(2,1)S(1)}, u32[]{:S(2)}, u32[]{:S(2)}) collective-permute-start(bf16[16,3584]{1,0:T(8,128)(2,1)S(1)} %get-tuple-element.122), channel_id=1, source_target_pairs={{0,4},{2,6},{4,0},{6,2},{1,5},{3,7},{5,1},{7,3},{8,12},{10,14},{12... | collective-permute-start | bytes 344072 | tf_op jit(solution)/shard_map/ppermute | solution.py:254
  157.6 0.0 collective-permute-done.11
  157.6 0.0 collective-permute-done.10
  157.6 11.8 %while.26 = (s32[]{:T(128)}, bf16[16,3584]{1,0:T(8,128)(2,1)S(1)}, bf16[16,3584]{1,0:T(8,128)(2,1)S(1)}, bf16[16,3584]{1,0:T(8,128)(2,1)S(1)}, bf16[16,3584]{1,0...) while((s32[]{:T(128)}, bf16[16,3584]{1,0:T(8,128)(2,1)S(1)}, ...), condition=%wide.region_2.0_spmd, body=%wide.region_1.0_spmd.sunk | while | flops 705101824 | bytes 13303981 | solution.py:369
  157.7 2.8 %collective-permute-start = (bf16[64,3584]{1,0:T(8,128)(2,1)S(1)}, bf16[64,3584]{1,0:T(8,128)(2,1)S(1)}, u32[]{:S(2)}, u32[]{:S(2)}) collective-permute-start(bf16[64,3584]{1,0:T(8,128)(2,1)S(1)} %join_f.1.refs_0_), channel_id=1, source_target_pairs={{0,1},{1,0},{2,3},{3,2},{4,5},{5,4},{6,7},{7,6},{8,9},{9,8},{10,11... | collective-permute-start | bytes 1376264 | tf_op jit(solution)/shard_map/while/body/ppermute | solution.py:254
  160.5 1.4 collective-permute-done.refs_1_
  161.9 3.6 %expert_f.1 = (bf16[64,3584]{1,0:T(8,128)(2,1)S(1)}, bf16[64,3584]{1,0:T(8,128)(2,1)S(1)}) custom-call(bf16[64,3584]{1,0:T(8,128)(2,1)S(1)} %join_f.1.refs_0_, bf16[64,3584]{1,0:T(8,128)(2,1)S(1)} %collective-permute-done.refs_1_, bf16[3584,512]{1,0:T(8,128)(2,1)} %get-tuple-element.291.refs_2_, bf16[256,3584]{1,0:T(8,128)(2,1)} %get-tuple-element.292.refs_3_), custom_call_target="tpu_custom_call" | custom-call | flops 704643072 | bytes 7340032 | tf_op jit(solution)/shard_map/while/body/expert_f/pallas_call | solution.py:240
  165.6 2.3 collective-permute-start.1
  167.9 1.4 collective-permute-done.1.refs_1_
  169.3 0.1 add_f.1
  169.4 1.7 spread_f.1
  171.1 16.3 %all-to-all-start = ((bf16[16,8,1792]{2,1,0:T(8,128)(2,1)}), bf16[16,8,1792]{2,1,0:T(8,128)(2,1)S(1)}, u32[]{:S(2)}, u32[]{:S(2)}) async-start(bf16[16,8,1792]{2,1,0:T(8,128)(2,1)} %bitcast.12), calls=%async_computation | async-start | bytes 917504 | tf_op jit(solution)/shard_map/all_to_all | solution.py:275
  187.5 0.0 collective-permute-done.12.refs_1_
  187.5 0.0 collective-permute-done.13.refs_2_
  187.5 0.0 copy-start.1
  187.5 0.2 merge_b.1
  187.7 4.5 %collective-permute-start.15 = (bf16[8,3584]{1,0:T(8,128)(2,1)S(1)}, bf16[8,3584]{1,0:T(8,128)(2,1)S(1)}, u32[]{:S(2)}, u32[]{:S(2)}) collective-permute-start(bf16[8,3584]{1,0:T(8,128)(2,1)S(1)} %get-tuple-element.124), channel_id=1, source_target_pairs={{0,24},{8,0},{16,8},{24,16},{1,25},{9,1},{17,9},{25,17},{2,26},{10... | collective-permute-start | bytes 172040 | tf_op jit(solution)/shard_map/ppermute | solution.py:254
  192.2 2.5 %collective-permute-start.16 = (bf16[8,3584]{1,0:T(8,128)(2,1)S(1)}, bf16[8,3584]{1,0:T(8,128)(2,1)S(1)}, u32[]{:S(2)}, u32[]{:S(2)}) collective-permute-start(bf16[8,3584]{1,0:T(8,128)(2,1)S(1)} %get-tuple-element.125), channel_id=1, source_target_pairs={{0,16},{8,24},{16,0},{24,8},{1,17},{9,25},{17,1},{25,9},{2,18},{10... | collective-permute-start | bytes 172040 | tf_op jit(solution)/shard_map/ppermute | solution.py:254
  194.7 2.5 %collective-permute-start.17 = (bf16[8,3584]{1,0:T(8,128)(2,1)S(1)}, bf16[8,3584]{1,0:T(8,128)(2,1)S(1)}, u32[]{:S(2)}, u32[]{:S(2)}) collective-permute-start(bf16[8,3584]{1,0:T(8,128)(2,1)S(1)} %get-tuple-element.126), channel_id=1, source_target_pairs={{0,8},{8,16},{16,24},{24,0},{1,9},{9,17},{17,25},{25,1},{2,10},{10... | collective-permute-start | bytes 172040 | tf_op jit(solution)/shard_map/ppermute | solution.py:254
  197.2 1.4 collective-permute-done.16.refs_5_
  198.6 2.4 collective-permute-done.17.refs_6_
  201.1 1.0 final_b.1
  202.1 1.9 collective-permute-start.18
  204.0 23.1 %collective-permute-done.18 = bf16[64,3584]{1,0:T(8,128)(2,1)S(1)} collective-permute-done((bf16[64,3584]{1,0:T(8,128)(2,1)S(1)}, bf16[64,3584]{1,0:T(8,128)(2,1)S(1)}, u32[]{:S(2)}, u32[]{:S(2)}) %collective-permute-start.18) | collective-permute-done | bytes 458784 | tf_op jit(solution)/shard_map/ppermute | solution.py:254
  227.1 16.4 %all-to-all-done = bf16[16,8,1792]{2,1,0:T(8,128)(2,1)S(1)} async-done(((bf16[16,8,1792]{2,1,0:T(8,128)(2,1)}), bf16[16,8,1792]{2,1,0:T(8,128)(2,1)S(1)}, u32[]{:S(2)}, u32[]{:S(2)}) %all-to-all-start) | async-done | bytes 458784 | tf_op jit(solution)/shard_map/all_to_all | solution.py:275
  243.5 1.3 final_f.1
  244.8 0.8 copy.34
  (10 shorter events, 0.1 us)
Async XLA Ops:
  2.0 36.6 %collective-permute-start.5 = (f32[2,64]{1,0:T(2,128)S(1)}, f32[2,64]{1,0:T(2,128)S(1)}, u32[]{:S(2)}, u32[]{:S(2)}) collective-permute-start(f32[2,64]{1,0:T(2,128)S(1)} %pad_maximum_fusion), channel_id=1, source_target_pairs={{0,32},{32,64},{64,96},{96,128},{128,160},{160,192},{192,224},{224... | collective-permute-start | bytes 1544 | tf_op jit(solution)/shard_map/ppermute | solution.py:254
  5.5 33.0 %collective-permute-start.4 = (bf16[64,3584]{1,0:T(8,128)(2,1)}, bf16[64,3584]{1,0:T(8,128)(2,1)S(1)}, u32[]{:S(2)}, u32[]{:S(2)}) collective-permute-start(bf16[64,3584]{1,0:T(8,128)(2,1)} %bitcast.34), channel_id=1, source_target_pairs={{0,32},{32,64},{64,96},{96,128},{128,160},{160,192},{192,224},{224... | collective-permute-start | bytes 1376264 | tf_op jit(solution)/shard_map/ppermute | solution.py:254
  7.4 1.0 copy-start
  8.4 0.7 copy-start.2
  9.1 0.7 copy-start.4
  11.0 92.4 %all-to-all-start.1 = ((bf16[16,8,1792]{2,1,0:T(8,128)(2,1)}), bf16[16,8,1792]{2,1,0:T(8,128)(2,1)S(1)}, u32[]{:S(2)}, u32[]{:S(2)}) async-start(bf16[16,8,1792]{2,1,0:T(8,128)(2,1)} %bitcast.15), calls=%async_computation.1 | async-start | bytes 917504 | tf_op jit(solution)/shard_map/all_to_all | solution.py:275
  38.5 11.6 %copy-start.3 = (s32[1,64,1]{1,2,0:T(1,128)S(1)}, s32[1,64,1]{1,2,0:T(1,128)}, u32[]{:S(2)}) copy-start(s32[1,64,1]{1,2,0:T(1,128)} %param.17) | copy-start | bytes 772
  38.5 65.0 %copy-start.5 = (bf16[1,1,128,512]{3,2,1,0:T(8,128)(2,1)S(1)}, bf16[1,1,128,512]{3,2,1,0:T(8,128)(2,1)}, u32[]{:S(2)}) copy-start(bf16[1,1,128,512]{3,2,1,0:T(8,128)(2,1)} %param.19) | copy-start | bytes 393220
  39.4 12.1 %collective-permute-start.6 = (bf16[8,3584]{1,0:T(8,128)(2,1)S(1)}, bf16[8,3584]{1,0:T(8,128)(2,1)S(1)}, u32[]{:S(2)}, u32[]{:S(2)}) collective-permute-start(bf16[8,3584]{1,0:T(8,128)(2,1)S(1)} %get-tuple-element.109), channel_id=1, source_target_pairs={{0,8},{8,16},{16,24},{24,0},{1,9},{9,17},{17,25},{25,1},{2,10},{10... | collective-permute-start | bytes 172040 | tf_op jit(solution)/shard_map/ppermute | solution.py:254
  42.7 8.8 %collective-permute-start.7 = (bf16[8,3584]{1,0:T(8,128)(2,1)S(1)}, bf16[8,3584]{1,0:T(8,128)(2,1)S(1)}, u32[]{:S(2)}, u32[]{:S(2)}) collective-permute-start(bf16[8,3584]{1,0:T(8,128)(2,1)S(1)} %get-tuple-element.110), channel_id=1, source_target_pairs={{0,16},{8,24},{16,0},{24,8},{1,17},{9,25},{17,1},{25,9},{2,18},{10... | collective-permute-start | bytes 172040 | tf_op jit(solution)/shard_map/ppermute | solution.py:254
  47.0 5.2 %collective-permute-start.8 = (bf16[8,3584]{1,0:T(8,128)(2,1)S(1)}, bf16[8,3584]{1,0:T(8,128)(2,1)S(1)}, u32[]{:S(2)}, u32[]{:S(2)}) collective-permute-start(bf16[8,3584]{1,0:T(8,128)(2,1)S(1)} %get-tuple-element.111), channel_id=1, source_target_pairs={{0,24},{8,0},{16,8},{24,16},{1,25},{9,1},{17,9},{25,17},{2,26},{10... | collective-permute-start | bytes 172040 | tf_op jit(solution)/shard_map/ppermute | solution.py:254
  52.4 105.2 %collective-permute-start.11 = (bf16[16,3584]{1,0:T(8,128)(2,1)S(1)}, bf16[16,3584]{1,0:T(8,128)(2,1)S(1)}, u32[]{:S(2)}, u32[]{:S(2)}) collective-permute-start(bf16[16,3584]{1,0:T(8,128)(2,1)S(1)} %get-tuple-element.113), channel_id=1, source_target_pairs={{0,4},{2,6},{4,0},{6,2},{1,5},{3,7},{5,1},{7,3},{8,12},{10,14},{12... | collective-permute-start | bytes 344072 | tf_op jit(solution)/shard_map/ppermute | solution.py:254
  73.8 83.8 %collective-permute-start.10 = (bf16[16,3584]{1,0:T(8,128)(2,1)S(1)}, bf16[16,3584]{1,0:T(8,128)(2,1)S(1)}, u32[]{:S(2)}, u32[]{:S(2)}) collective-permute-start(bf16[16,3584]{1,0:T(8,128)(2,1)S(1)} %get-tuple-element.113), channel_id=1, source_target_pairs={{0,6},{2,4},{4,2},{6,0},{1,7},{3,5},{5,3},{7,1},{8,14},{10,12},{12... | collective-permute-start | bytes 344072 | tf_op jit(solution)/shard_map/ppermute | solution.py:254
  75.8 69.9 %collective-permute-start.9 = (bf16[16,3584]{1,0:T(8,128)(2,1)S(1)}, bf16[16,3584]{1,0:T(8,128)(2,1)S(1)}, u32[]{:S(2)}, u32[]{:S(2)}) collective-permute-start(bf16[16,3584]{1,0:T(8,128)(2,1)S(1)} %get-tuple-element.268), channel_id=1, source_target_pairs={{0,2},{2,0},{4,6},{6,4},{1,3},{3,1},{5,7},{7,5},{8,10},{10,8},{12,... | collective-permute-start | bytes 344072 | tf_op jit(solution)/shard_map/ppermute | solution.py:254
  103.5 4.5 %collective-permute-start.2 = (bf16[128,1792]{1,0:T(8,128)(2,1)S(1)}, bf16[128,1792]{1,0:T(8,128)(2,1)S(1)}, u32[]{:S(2)}, u32[]{:S(2)}) collective-permute-start(bf16[128,1792]{1,0:T(8,128)(2,1)S(1)} %get-tuple-element.303.refs_1_), channel_id=1, source_target_pairs={{0,1},{1,0},{2,3},{3,2},{4,5},{5,4},{6,7},{7,6},{8,9},{9,8},{10,11... | collective-permute-start | bytes 1376264 | tf_op jit(solution)/shard_map/while/body/ppermute | solution.py:254
  114.8 3.7 %collective-permute-start.3 = (bf16[128,1792]{1,0:T(8,128)(2,1)S(1)}, bf16[128,1792]{1,0:T(8,128)(2,1)S(1)}, u32[]{:S(2)}, u32[]{:S(2)}) collective-permute-start(bf16[128,1792]{1,0:T(8,128)(2,1)S(1)} %get-tuple-element.265), channel_id=1, source_target_pairs={{0,1},{1,0},{2,3},{3,2},{4,5},{5,4},{6,7},{7,6},{8,9},{9,8},{10,11... | collective-permute-start | bytes 1376264 | tf_op jit(solution)/shard_map/while/body/ppermute | solution.py:254
  119.6 67.8 %collective-permute-start.12 = (bf16[16,3584]{1,0:T(8,128)(2,1)S(1)}, bf16[16,3584]{1,0:T(8,128)(2,1)S(1)}, u32[]{:S(2)}, u32[]{:S(2)}) collective-permute-start(bf16[16,3584]{1,0:T(8,128)(2,1)S(1)} %get-tuple-element.120), channel_id=1, source_target_pairs={{0,2},{2,0},{4,6},{6,4},{1,3},{3,1},{5,7},{7,5},{8,10},{10,8},{12,... | collective-permute-start | bytes 344072 | tf_op jit(solution)/shard_map/ppermute | solution.py:254
  143.8 43.6 %collective-permute-start.13 = (bf16[16,3584]{1,0:T(8,128)(2,1)S(1)}, bf16[16,3584]{1,0:T(8,128)(2,1)S(1)}, u32[]{:S(2)}, u32[]{:S(2)}) collective-permute-start(bf16[16,3584]{1,0:T(8,128)(2,1)S(1)} %get-tuple-element.121), channel_id=1, source_target_pairs={{0,6},{2,4},{4,2},{6,0},{1,7},{3,5},{5,3},{7,1},{8,14},{10,12},{12... | collective-permute-start | bytes 344072 | tf_op jit(solution)/shard_map/ppermute | solution.py:254
  145.8 41.7 %collective-permute-start.14 = (bf16[16,3584]{1,0:T(8,128)(2,1)S(1)}, bf16[16,3584]{1,0:T(8,128)(2,1)S(1)}, u32[]{:S(2)}, u32[]{:S(2)}) collective-permute-start(bf16[16,3584]{1,0:T(8,128)(2,1)S(1)} %get-tuple-element.122), channel_id=1, source_target_pairs={{0,4},{2,6},{4,0},{6,2},{1,5},{3,7},{5,1},{7,3},{8,12},{10,14},{12... | collective-permute-start | bytes 344072 | tf_op jit(solution)/shard_map/ppermute | solution.py:254
  157.7 4.3 %collective-permute-start = (bf16[64,3584]{1,0:T(8,128)(2,1)S(1)}, bf16[64,3584]{1,0:T(8,128)(2,1)S(1)}, u32[]{:S(2)}, u32[]{:S(2)}) collective-permute-start(bf16[64,3584]{1,0:T(8,128)(2,1)S(1)} %join_f.1.refs_0_), channel_id=1, source_target_pairs={{0,1},{1,0},{2,3},{3,2},{4,5},{5,4},{6,7},{7,6},{8,9},{9,8},{10,11... | collective-permute-start | bytes 1376264 | tf_op jit(solution)/shard_map/while/body/ppermute | solution.py:254
  165.6 3.7 %collective-permute-start.1 = (bf16[64,3584]{1,0:T(8,128)(2,1)S(1)}, bf16[64,3584]{1,0:T(8,128)(2,1)S(1)}, u32[]{:S(2)}, u32[]{:S(2)}) collective-permute-start(bf16[64,3584]{1,0:T(8,128)(2,1)S(1)} %get-tuple-element.253), channel_id=1, source_target_pairs={{0,1},{1,0},{2,3},{3,2},{4,5},{5,4},{6,7},{7,6},{8,9},{9,8},{10,11... | collective-permute-start | bytes 1376264 | tf_op jit(solution)/shard_map/while/body/ppermute | solution.py:254
  171.1 72.4 %all-to-all-start = ((bf16[16,8,1792]{2,1,0:T(8,128)(2,1)}), bf16[16,8,1792]{2,1,0:T(8,128)(2,1)S(1)}, u32[]{:S(2)}, u32[]{:S(2)}) async-start(bf16[16,8,1792]{2,1,0:T(8,128)(2,1)} %bitcast.12), calls=%async_computation | async-start | bytes 917504 | tf_op jit(solution)/shard_map/all_to_all | solution.py:275
  187.5 13.6 %copy-start.1 = (bf16[1,64,3584]{2,1,0:T(8,128)(2,1)S(1)}, bf16[1,64,3584]{2,1,0:T(8,128)(2,1)}, u32[]{:S(2)}) copy-start(bf16[1,64,3584]{2,1,0:T(8,128)(2,1)} %param.16) | copy-start | bytes 1376260
  187.7 9.5 %collective-permute-start.15 = (bf16[8,3584]{1,0:T(8,128)(2,1)S(1)}, bf16[8,3584]{1,0:T(8,128)(2,1)S(1)}, u32[]{:S(2)}, u32[]{:S(2)}) collective-permute-start(bf16[8,3584]{1,0:T(8,128)(2,1)S(1)} %get-tuple-element.124), channel_id=1, source_target_pairs={{0,24},{8,0},{16,8},{24,16},{1,25},{9,1},{17,9},{25,17},{2,26},{10... | collective-permute-start | bytes 172040 | tf_op jit(solution)/shard_map/ppermute | solution.py:254
  192.2 6.4 %collective-permute-start.16 = (bf16[8,3584]{1,0:T(8,128)(2,1)S(1)}, bf16[8,3584]{1,0:T(8,128)(2,1)S(1)}, u32[]{:S(2)}, u32[]{:S(2)}) collective-permute-start(bf16[8,3584]{1,0:T(8,128)(2,1)S(1)} %get-tuple-element.125), channel_id=1, source_target_pairs={{0,16},{8,24},{16,0},{24,8},{1,17},{9,25},{17,1},{25,9},{2,18},{10... | collective-permute-start | bytes 172040 | tf_op jit(solution)/shard_map/ppermute | solution.py:254
  194.7 6.4 %collective-permute-start.17 = (bf16[8,3584]{1,0:T(8,128)(2,1)S(1)}, bf16[8,3584]{1,0:T(8,128)(2,1)S(1)}, u32[]{:S(2)}, u32[]{:S(2)}) collective-permute-start(bf16[8,3584]{1,0:T(8,128)(2,1)S(1)} %get-tuple-element.126), channel_id=1, source_target_pairs={{0,8},{8,16},{16,24},{24,0},{1,9},{9,17},{17,25},{25,1},{2,10},{10... | collective-permute-start | bytes 172040 | tf_op jit(solution)/shard_map/ppermute | solution.py:254
  202.1 25.0 %collective-permute-start.18 = (bf16[64,3584]{1,0:T(8,128)(2,1)S(1)}, bf16[64,3584]{1,0:T(8,128)(2,1)S(1)}, u32[]{:S(2)}, u32[]{:S(2)}) collective-permute-start(bf16[64,3584]{1,0:T(8,128)(2,1)S(1)} %final_b.1), channel_id=1, source_target_pairs={{0,992},{32,0},{64,32},{96,64},{128,96},{160,128},{192,160},{224,1... | collective-permute-start | bytes 1376264 | tf_op jit(solution)/shard_map/ppermute | solution.py:254

commit v4 on v3

--- a/solution.py
+++ b/solution.py
@@ -65,6 +65,16 @@
 
 def source_of(at_ref, d, block, count):
     return (at_ref[0] + count - d) % count, at_ref[1] ^ block ^ (block // 2)
+
+
+def stream(far_refs, near_refs, sems):
+    copies = [
+        pltpu.make_async_copy(far, near, sems.at[i])
+        for i, (far, near) in enumerate(zip(far_refs, near_refs))
+    ]
+    for copy in copies:
+        copy.start()
+    return copies
 
 
 def slab(refs):
@@ -91,15 +101,20 @@
     out_ref[...] = total.astype(BF16)
 
 
-def expert_b_kernel(cap, c_ref, own_ref, oth_ref, saved_ref, wgu_ref, wd_ref, mine_ref, send_ref):
+def expert_b_kernel(cap, c_ref, own_ref, oth_ref, *refs):
+    far, (mine_ref, send_ref), near, sems = refs[:3], refs[3:5], refs[5:8], refs[8]
+    wd_ref, saved_ref, wgu_ref = near
+    wd_copy, saved_copy, wgu_copy = stream(far, near, sems)
     rows, half = own_ref.shape
     hid, width = wd_ref.shape
     values = jnp.concatenate([joined(own_ref[...], cap), joined(oth_ref[...], cap)], axis=0)
+    wd_copy.wait()
     dh = dot(values, wd_ref[...], ((1,), (1,)))
     r, p = iota((rows, rows), 0), iota((rows, rows), 1)
     core = jnp.where(r < rows // 2, c_ref[0], 1 - c_ref[0])
     r = r % (rows // 2)
     pick = (p // (2 * cap) == r // cap) & (p % cap == r % cap) & ((p % (2 * cap)) // cap == core)
+    saved_copy.wait()
     saved = dot(ones_at(pick), saved_ref[...])
     act = saved[:, :hid]
     lin = saved[:, hid:]
@@ -107,6 +122,7 @@
     d_act = (dh * lin * sig * (1.0 + act * (1.0 - sig))).astype(BF16)
     d_lin = (dh * act * sig).astype(BF16)
     grads = jnp.concatenate([d_act, d_lin], axis=1)
+    wgu_copy.wait()
     step = 256 if half % 256 == 0 else half
     for at in range(0, half, step):
         low, high = (
@@ -154,9 +170,9 @@
     out_ref[...] = (cot_ref[...].astype(F32) + total).astype(BF16)
 
 
-def pack_f_kernel(experts, cap, at_ref, x_ref, meta_ref, *out_refs):
+def pack_f_kernel(experts, cap, at_ref, x_ref, route_ref, *out_refs):
     tokens = x_ref.shape[0]
-    route = meta_ref[0:1, :].astype(jnp.int32)
+    route = route_ref[...]
     slot = slots_of(route, experts)
     count = len(out_refs)
     m = iota((count * 2 * cap, tokens), 0)
@@ -181,12 +197,18 @@
     refs[-1][...] = slab(refs[:-1])
 
 
-def expert_f_kernel(own_ref, oth_ref, wgu_ref, wd_ref, mine_ref, send_ref):
+def expert_f_kernel(own_ref, oth_ref, *refs):
+    far, (mine_ref, send_ref), near, sems = refs[:2], refs[2:4], refs[4:6], refs[6]
+    wgu_ref, wd_ref = near
+    wgu_copy, wd_copy = stream(far, near, sems)
     rows = own_ref.shape[0]
     hid, width = wd_ref.shape
-    pre = dot(slab((own_ref, oth_ref)), wgu_ref[...])
+    values = slab((own_ref, oth_ref))
+    wgu_copy.wait()
+    pre = dot(values, wgu_ref[...])
     gate = pre[:, :hid]
     hidden = (gate / (1.0 + jnp.exp(-gate)) * pre[:, hid:]).astype(BF16)
+    wd_copy.wait()
     step = 512 if width % 512 == 0 else width
     for at in range(0, width, step):
         part = dot(hidden, wd_ref[:, at : at + step]).astype(BF16)
@@ -212,13 +234,12 @@
     out_ref[...] = total.astype(BF16)
 
 
-def final_f_kernel(experts, cap, x_ref, meta_ref, back_ref, out_ref):
+def final_f_kernel(experts, cap, x_ref, route_ref, gate_ref, back_ref, out_ref):
     tokens = x_ref.shape[0]
     rows, half = back_ref.shape
-    meta = meta_ref[...]
-    route = meta[0:1, :].astype(jnp.int32)
+    route = route_ref[...]
     slot = column(slots_of(route, experts))
-    gate = column(meta[1:2, :])
+    gate = column(gate_ref[...])
     m = iota((tokens, rows), 1)
     table = (m // (4 * cap) == column(route)) & (m % cap == slot)
     low = (m % (2 * cap)) // cap == 0
@@ -229,19 +250,23 @@
         out_ref[:, base : base + half] = (x + total).astype(BF16)
 
 
-def call(kernel, name, shapes, operands, flops, earlier=()):
+def call(kernel, name, shapes, operands, flops, earlier=(), streamed=0):
     out = [jax.ShapeDtypeStruct(s, BF16) for s in shapes]
     nbytes = sum(a.size * a.dtype.itemsize for a in (*operands, *out))
     count = len(operands)
+    far = operands[count - streamed :]
 
     def body(*refs):
         kernel(*refs[:count], *refs[count + len(earlier) :])
 
+    scratch = [pltpu.VMEM(a.shape, a.dtype) for a in far]
     return pl.pallas_call(
         body,
         out_shape=out,
-        in_specs=[SMEM if a.ndim == 1 else VMEM for a in operands] + [ANY] * len(earlier),
+        in_specs=[SMEM if a.ndim == 1 else VMEM for a in operands[: count - streamed]]
+        + [ANY] * (streamed + len(earlier)),
         out_specs=[VMEM] * len(out),
+        scratch_shapes=scratch + [pltpu.SemaphoreType.DMA((streamed,))] * (streamed > 0),
         compiler_params=PARAMS,
         name=name,
         cost_estimate=pl.CostEstimate(
@@ -306,11 +331,9 @@
         return lambda *refs: body(*head, *refs)
 
     route_b, gate_b = bwd_route.reshape(1, tokens), bwd_gate.reshape(1, tokens)
-    meta = jnp.concatenate(
-        [fwd_route.reshape(1, tokens).astype(F32), fwd_gate.reshape(1, tokens)], axis=0
-    )
     x = shift(fwd_in[0], 1)
-    meta = shift(meta, 1)
+    route_f = shift(fwd_route.reshape(1, tokens), 1)
+    gate_f = shift(fwd_gate.reshape(1, tokens), 1)
     core = at[2:]
     rounds = jnp.minimum(jnp.sum((bwd_route < experts).astype(jnp.int32)), 1)
 
@@ -327,7 +350,7 @@
         kernel(pack_f_kernel, experts, cap),
         "pack_f",
         [(2 * cap, width)] * (block // cap),
-        (at, x, meta),
+        (at, x, route_f),
         4 * block * tokens * width,
         earlier=(packed,),
     )
@@ -342,8 +365,9 @@
             kernel(expert_b_kernel, cap),
             "expert_b",
             [half] * 2,
-            (core, rows, swap_core(rows), saved_pre[0, 0], wgu, wd),
+            (core, rows, swap_core(rows), wd, saved_pre[0, 0], wgu),
             6 * many * hid * width,
+            streamed=3,
         )
         return (mine.astype(F32) + swap_core(send).astype(F32)).astype(BF16)
 
@@ -360,7 +384,7 @@
     def chain_f(_, blocks):
         (own,) = call(join_kernel, "join_f", [(few, width)], blocks, few * width)
         mine, send = call(
-            expert_f_kernel, "expert_f", [(few, width)] * 2, (own, swap_core(own), wgu, wd), 6 * many * hid * width
+            expert_f_kernel, "expert_f", [(few, width)] * 2, (own, swap_core(own), wgu, wd), 6 * many * hid * width, streamed=2
         )
         return tuple(
             call(add_kernel, "add_f", [(block, width)] * Z_GROUPS, (mine, swap_core(send)), few * width)
@@ -392,7 +416,7 @@
         kernel(final_f_kernel, experts, cap),
         "final_f",
         [(tokens, width)],
-        (x, meta, back_f),
+        (x, route_f, gate_f, back_f),
         2 * many * tokens * width,
     )
     return out_f[None], out_b[None]

time: 246 us -> 258 us (1.049)
  the two profiles are of different devices: /device:TPU:217 before, /device:TPU:1 now
where the time goes in v4:
time: 258 us; the launch traced here: 257 us
  starting transfers between devices  185 us (72%)
  waiting for transfers between devices  49.5 us (19%)
  Pallas kernels  16.5 us (6%)
  local copies, waits for them, and re-layouts  3.11 us (1%)
    ppermute x20, starting transfers between devices, moved(): lax.ppermute(block, axis, [(i, to(i)) for i in range(lax.axis_size(axis))])  131 us
    all_to_all x2, starting transfers between devices, exchange(): lax.all_to_all(blocks, ('x', 'zh'), split_axis=0, concat_axis=0, tiled=True)  53.7 us
    ppermute x20, waiting for transfers between devices, moved(): lax.ppermute(block, axis, [(i, to(i)) for i in range(lax.axis_size(axis))])  45.9 us
    pallas_call x12, Pallas kernels, call(): pl.pallas_call(body, out_shape=out, in_specs=[SMEM if a.ndim == 1 else VM...  16.5 us
  transfers between devices with their start and end apart: 22, of which 10 were waited for; matrix products, arithmetic and copies ran while one was open for 0% of the time, Pallas kernels for 6%

profile of v4, /device:TPU:1, one launch (start us, length us, event | category | flops | bytes accessed | tf_op | source)
XLA Modules:
  0.0 256.6 jit_solution(6928846579670164022)
XLA Ops:
  0.6 4.4 %collective-permute-start.4 = (bf16[64,3584]{1,0:T(8,128)(2,1)}, bf16[64,3584]{1,0:T(8,128)(2,1)S(1)}, u32[]{:S(2)}, u32[]{:S(2)}) collective-permute-start(bf16[64,3584]{1,0:T(8,128)(2,1)} %bitcast.32), channel_id=1, source_target_pairs={{0,32},{32,64},{64,96},{96,128},{128,160},{160,192},{192,224},{224... | collective-permute-start | bytes 1376264 | tf_op jit(solution)/shard_map/ppermute | solution.py:279
  5.0 0.0 copy-start
  5.0 1.0 copy-done
  6.0 0.7 copy-done.2
  6.7 0.7 copy-done.4
  7.3 1.3 pack_b.1.refs_3_
  8.6 29.7 %all-to-all-start.1 = ((bf16[16,8,1792]{2,1,0:T(8,128)(2,1)}), bf16[16,8,1792]{2,1,0:T(8,128)(2,1)S(1)}, u32[]{:S(2)}, u32[]{:S(2)}) async-start(bf16[16,8,1792]{2,1,0:T(8,128)(2,1)} %bitcast.15), calls=%async_computation.1 | async-start | bytes 917504 | tf_op jit(solution)/shard_map/all_to_all | solution.py:300
  38.4 2.6 %collective-permute-start.5 = (s32[1,64]{1,0:T(1,128)S(1)}, s32[1,64]{1,0:T(1,128)S(1)}, u32[]{:S(2)}, u32[]{:S(2)}) collective-permute-start(s32[1,64]{1,0:T(1,128)S(1)} %bitcast.33), channel_id=1, source_target_pairs={{0,32},{32,64},{64,96},{96,128},{128,160},{160,192},{192,224},{224... | collective-permute-start | bytes 776 | tf_op jit(solution)/shard_map/ppermute | solution.py:279
  41.0 0.1 pad_add_fusion.refs_0_
  41.1 19.5 %collective-permute-done.5.refs_2_.refs_1_ = s32[1,64]{1,0:T(1,128)S(1)} collective-permute-done((s32[1,64]{1,0:T(1,128)S(1)}, s32[1,64]{1,0:T(1,128)S(1)}, u32[]{:S(2)}, u32[]{:S(2)}) %collective-permute-start.5) | collective-permute-done | bytes 288 | tf_op jit(solution)/shard_map/ppermute | solution.py:279
  60.6 0.0 collective-permute-done.4.refs_1_.refs_0_
  60.6 0.9 pack_f.1
  61.5 3.1 %collective-permute-start.7 = (bf16[8,3584]{1,0:T(8,128)(2,1)S(1)}, bf16[8,3584]{1,0:T(8,128)(2,1)S(1)}, u32[]{:S(2)}, u32[]{:S(2)}) collective-permute-start(bf16[8,3584]{1,0:T(8,128)(2,1)S(1)} %get-tuple-element.109), channel_id=1, source_target_pairs={{0,8},{8,16},{16,24},{24,0},{1,9},{9,17},{17,25},{25,1},{2,10},{10... | collective-permute-start | bytes 172040 | tf_op jit(solution)/shard_map/ppermute | solution.py:279
  64.6 4.3 %collective-permute-start.8 = (bf16[8,3584]{1,0:T(8,128)(2,1)S(1)}, bf16[8,3584]{1,0:T(8,128)(2,1)S(1)}, u32[]{:S(2)}, u32[]{:S(2)}) collective-permute-start(bf16[8,3584]{1,0:T(8,128)(2,1)S(1)} %get-tuple-element.110), channel_id=1, source_target_pairs={{0,16},{8,24},{16,0},{24,8},{1,17},{9,25},{17,1},{25,9},{2,18},{10... | collective-permute-start | bytes 172040 | tf_op jit(solution)/shard_map/ppermute | solution.py:279
  68.9 3.1 %collective-permute-start.9 = (bf16[8,3584]{1,0:T(8,128)(2,1)S(1)}, bf16[8,3584]{1,0:T(8,128)(2,1)S(1)}, u32[]{:S(2)}, u32[]{:S(2)}) collective-permute-start(bf16[8,3584]{1,0:T(8,128)(2,1)S(1)} %get-tuple-element.111), channel_id=1, source_target_pairs={{0,24},{8,0},{16,8},{24,16},{1,25},{9,1},{17,9},{25,17},{2,26},{10... | collective-permute-start | bytes 172040 | tf_op jit(solution)/shard_map/ppermute | solution.py:279
  72.0 0.7 fusion
  73.3 0.0 collective-permute-done.7.refs_1_
  73.3 0.8 collective-permute-done.9.refs_3_
  74.1 0.2 pairs_f.1
  74.3 22.2 %collective-permute-start.11 = (bf16[16,3584]{1,0:T(8,128)(2,1)S(1)}, bf16[16,3584]{1,0:T(8,128)(2,1)S(1)}, u32[]{:S(2)}, u32[]{:S(2)}) collective-permute-start(bf16[16,3584]{1,0:T(8,128)(2,1)S(1)} %get-tuple-element.113), channel_id=1, source_target_pairs={{0,6},{2,4},{4,2},{6,0},{1,7},{3,5},{5,3},{7,1},{8,14},{10,12},{12... | collective-permute-start | bytes 344072 | tf_op jit(solution)/shard_map/ppermute | solution.py:279
  96.5 3.3 %collective-permute-start.12 = (bf16[16,3584]{1,0:T(8,128)(2,1)S(1)}, bf16[16,3584]{1,0:T(8,128)(2,1)S(1)}, u32[]{:S(2)}, u32[]{:S(2)}) collective-permute-start(bf16[16,3584]{1,0:T(8,128)(2,1)S(1)} %get-tuple-element.113), channel_id=1, source_target_pairs={{0,4},{2,6},{4,0},{6,2},{1,5},{3,7},{5,1},{7,3},{8,12},{10,14},{12... | collective-permute-start | bytes 344072 | tf_op jit(solution)/shard_map/ppermute | solution.py:279
  99.8 10.4 %collective-permute-start.10 = (bf16[16,3584]{1,0:T(8,128)(2,1)S(1)}, bf16[16,3584]{1,0:T(8,128)(2,1)S(1)}, u32[]{:S(2)}, u32[]{:S(2)}) collective-permute-start(bf16[16,3584]{1,0:T(8,128)(2,1)S(1)} %get-tuple-element.268), channel_id=1, source_target_pairs={{0,2},{2,0},{4,6},{6,4},{1,3},{3,1},{5,7},{7,5},{8,10},{10,8},{12,... | collective-permute-start | bytes 344072 | tf_op jit(solution)/shard_map/ppermute | solution.py:279
  110.2 0.0 all-to-all-done.1
  110.2 24.4 %while.27 = (s32[]{:T(128)}, bf16[128,1792]{1,0:T(8,128)(2,1)S(1)}, s32[]{:T(128)}, bf16[1,1,128,512]{3,2,1,0:T(8,128)(2,1)S(1)}, s32[1]{0:T(128)}, /*index=5*/b...) while((s32[]{:T(128)}, bf16[128,1792]{1,0:T(8,128)(2,1)S(1)}, s32[]{:T(128)}, ...), condition=%wide.region_4.0_spmd, body=%wide.region_3.0_spmd.sunk | while | flops 705560576 | bytes 12517545 | solution.py:374
  110.3 13.4 %collective-permute-start.2 = (bf16[128,1792]{1,0:T(8,128)(2,1)S(1)}, bf16[128,1792]{1,0:T(8,128)(2,1)S(1)}, u32[]{:S(2)}, u32[]{:S(2)}) collective-permute-start(bf16[128,1792]{1,0:T(8,128)(2,1)S(1)} %get-tuple-element.303.refs_1_), channel_id=1, source_target_pairs={{0,1},{1,0},{2,3},{3,2},{4,5},{5,4},{6,7},{7,6},{8,9},{9,8},{10,11... | collective-permute-start | bytes 1376264 | tf_op jit(solution)/shard_map/while/body/ppermute | solution.py:279
  123.7 1.4 collective-permute-done.2.refs_2_
  125.1 5.7 %expert_b.1 = (bf16[128,1792]{1,0:T(8,128)(2,1)S(1)}, bf16[128,1792]{1,0:T(8,128)(2,1)S(1)}) custom-call(s32[1]{0:T(128)} %get-tuple-element.314.refs_0_, bf16[128,1792]{1,0:T(8,128)(2,1)S(1)} %get-tuple-element.303.refs_1_, bf16[128,1792]{1,0:T(8,128)(2,1)S(1)} %collective-permute-done.2.refs_2_, bf16[256,3584]{1,0:T(8,128)(2,1)} %get-tuple-element.315.refs_3_, ...), custom_call_target="tpu_custom_call" | custom-call | flops 704643072 | bytes 7471108 | tf_op jit(solution)/shard_map/while/body/expert_b/pallas_call | solution.py:263
  130.8 2.3 collective-permute-start.3
  133.1 1.4 collective-permute-done.3
  134.5 0.1 add_convert_fusion.2
  134.7 1.0 split_b.1
  135.6 3.2 %collective-permute-start.13 = (bf16[16,3584]{1,0:T(8,128)(2,1)S(1)}, bf16[16,3584]{1,0:T(8,128)(2,1)S(1)}, u32[]{:S(2)}, u32[]{:S(2)}) collective-permute-start(bf16[16,3584]{1,0:T(8,128)(2,1)S(1)} %get-tuple-element.120), channel_id=1, source_target_pairs={{0,2},{2,0},{4,6},{6,4},{1,3},{3,1},{5,7},{7,5},{8,10},{10,8},{12,... | collective-permute-start | bytes 344072 | tf_op jit(solution)/shard_map/ppermute | solution.py:279
  138.8 12.4 %collective-permute-start.14 = (bf16[16,3584]{1,0:T(8,128)(2,1)S(1)}, bf16[16,3584]{1,0:T(8,128)(2,1)S(1)}, u32[]{:S(2)}, u32[]{:S(2)}) collective-permute-start(bf16[16,3584]{1,0:T(8,128)(2,1)S(1)} %get-tuple-element.121), channel_id=1, source_target_pairs={{0,6},{2,4},{4,2},{6,0},{1,7},{3,5},{5,3},{7,1},{8,14},{10,12},{12... | collective-permute-start | bytes 344072 | tf_op jit(solution)/shard_map/ppermute | solution.py:279
  151.2 0.0 collective-permute-done.10
  151.2 10.6 %collective-permute-start.15 = (bf16[16,3584]{1,0:T(8,128)(2,1)S(1)}, bf16[16,3584]{1,0:T(8,128)(2,1)S(1)}, u32[]{:S(2)}, u32[]{:S(2)}) collective-permute-start(bf16[16,3584]{1,0:T(8,128)(2,1)S(1)} %get-tuple-element.122), channel_id=1, source_target_pairs={{0,4},{2,6},{4,0},{6,2},{1,5},{3,7},{5,1},{7,3},{8,12},{10,14},{12... | collective-permute-start | bytes 344072 | tf_op jit(solution)/shard_map/ppermute | solution.py:279
  161.8 0.0 collective-permute-done.12
  161.8 13.9 %while.26 = (s32[]{:T(128)}, bf16[16,3584]{1,0:T(8,128)(2,1)S(1)}, bf16[16,3584]{1,0:T(8,128)(2,1)S(1)}, bf16[16,3584]{1,0:T(8,128)(2,1)S(1)}, bf16[16,3584]{1,0...) while((s32[]{:T(128)}, bf16[16,3584]{1,0:T(8,128)(2,1)S(1)}, ...), condition=%wide.region_2.0_spmd, body=%wide.region_1.0_spmd.sunk | while | flops 705101824 | bytes 13303981 | solution.py:393
  161.8 5.5 %collective-permute-start = (bf16[64,3584]{1,0:T(8,128)(2,1)S(1)}, bf16[64,3584]{1,0:T(8,128)(2,1)S(1)}, u32[]{:S(2)}, u32[]{:S(2)}) collective-permute-start(bf16[64,3584]{1,0:T(8,128)(2,1)S(1)} %join_f.1.refs_0_), channel_id=1, source_target_pairs={{0,1},{1,0},{2,3},{3,2},{4,5},{5,4},{6,7},{7,6},{8,9},{9,8},{10,11... | collective-permute-start | bytes 1376264 | tf_op jit(solution)/shard_map/while/body/ppermute | solution.py:279
  167.3 1.4 collective-permute-done.refs_1_
  168.8 3.1 %expert_f.1 = (bf16[64,3584]{1,0:T(8,128)(2,1)S(1)}, bf16[64,3584]{1,0:T(8,128)(2,1)S(1)}) custom-call(bf16[64,3584]{1,0:T(8,128)(2,1)S(1)} %join_f.1.refs_0_, bf16[64,3584]{1,0:T(8,128)(2,1)S(1)} %collective-permute-done.refs_1_, bf16[3584,512]{1,0:T(8,128)(2,1)} %get-tuple-element.291.refs_2_, bf16[256,3584]{1,0:T(8,128)(2,1)} %get-tuple-element.292.refs_3_), custom_call_target="tpu_custom_call" | custom-call | flops 704643072 | bytes 7340032 | tf_op jit(solution)/shard_map/while/body/expert_f/pallas_call | solution.py:263
  171.9 2.3 collective-permute-start.1
  174.2 1.4 collective-permute-done.1.refs_1_
  175.6 0.1 add_f.1
  175.7 1.7 spread_f.1
  177.4 23.9 %all-to-all-start = ((bf16[16,8,1792]{2,1,0:T(8,128)(2,1)}), bf16[16,8,1792]{2,1,0:T(8,128)(2,1)S(1)}, u32[]{:S(2)}, u32[]{:S(2)}) async-start(bf16[16,8,1792]{2,1,0:T(8,128)(2,1)} %bitcast.12), calls=%async_computation | async-start | bytes 917504 | tf_op jit(solution)/shard_map/all_to_all | solution.py:300
  201.4 0.0 collective-permute-done.14.refs_2_
  201.4 0.0 collective-permute-done.15.refs_3_
  201.4 0.0 copy-start.1
  201.4 0.0 copy-start.7
  201.4 0.2 merge_b.1
  201.6 4.5 %collective-permute-start.16 = (bf16[8,3584]{1,0:T(8,128)(2,1)S(1)}, bf16[8,3584]{1,0:T(8,128)(2,1)S(1)}, u32[]{:S(2)}, u32[]{:S(2)}) collective-permute-start(bf16[8,3584]{1,0:T(8,128)(2,1)S(1)} %get-tuple-element.124), channel_id=1, source_target_pairs={{0,24},{8,0},{16,8},{24,16},{1,25},{9,1},{17,9},{25,17},{2,26},{10... | collective-permute-start | bytes 172040 | tf_op jit(solution)/shard_map/ppermute | solution.py:279
  206.1 2.5 collective-permute-start.17
  208.6 2.5 collective-permute-start.18
  211.1 0.0 collective-permute-done.16.refs_4_
  211.1 1.4 collective-permute-done.17.refs_5_
  212.6 2.4 collective-permute-done.18.refs_6_
  215.0 1.0 final_b.1
  216.0 17.0 %collective-permute-start.19 = (bf16[64,3584]{1,0:T(8,128)(2,1)S(1)}, bf16[64,3584]{1,0:T(8,128)(2,1)S(1)}, u32[]{:S(2)}, u32[]{:S(2)}) collective-permute-start(bf16[64,3584]{1,0:T(8,128)(2,1)S(1)} %final_b.1), channel_id=1, source_target_pairs={{0,992},{32,0},{64,32},{96,64},{128,96},{160,128},{192,160},{224,1... | collective-permute-start | bytes 1376264 | tf_op jit(solution)/shard_map/ppermute | solution.py:279
  233.1 1.9 collective-permute-start.6
  235.0 16.0 %collective-permute-done.19 = bf16[64,3584]{1,0:T(8,128)(2,1)S(1)} collective-permute-done((bf16[64,3584]{1,0:T(8,128)(2,1)S(1)}, bf16[64,3584]{1,0:T(8,128)(2,1)S(1)}, u32[]{:S(2)}, u32[]{:S(2)}) %collective-permute-start.19) | collective-permute-done | bytes 458784 | tf_op jit(solution)/shard_map/ppermute | solution.py:279
  251.0 0.0 collective-permute-done.6.refs_2_
  251.0 3.6 %all-to-all-done = bf16[16,8,1792]{2,1,0:T(8,128)(2,1)S(1)} async-done(((bf16[16,8,1792]{2,1,0:T(8,128)(2,1)}), bf16[16,8,1792]{2,1,0:T(8,128)(2,1)S(1)}, u32[]{:S(2)}, u32[]{:S(2)}) %all-to-all-start) | async-done | bytes 458784 | tf_op jit(solution)/shard_map/all_to_all | solution.py:300
  254.6 1.3 final_f.1
  255.9 0.8 copy.34
  (14 shorter events, 0.1 us)
Async XLA Ops:
  0.6 60.0 %collective-permute-start.4 = (bf16[64,3584]{1,0:T(8,128)(2,1)}, bf16[64,3584]{1,0:T(8,128)(2,1)S(1)}, u32[]{:S(2)}, u32[]{:S(2)}) collective-permute-start(bf16[64,3584]{1,0:T(8,128)(2,1)} %bitcast.32), channel_id=1, source_target_pairs={{0,32},{32,64},{64,96},{96,128},{128,160},{160,192},{192,224},{224... | collective-permute-start | bytes 1376264 | tf_op jit(solution)/shard_map/ppermute | solution.py:279
  5.0 1.0 copy-start
  6.0 0.7 copy-start.2
  6.7 0.7 copy-start.4
  7.3 31.0 %copy-start.6 = (s32[1,64,1]{1,2,0:T(1,128)S(1)}, s32[1,64,1]{1,2,0:T(1,128)}, u32[]{:S(2)}) copy-start(s32[1,64,1]{1,2,0:T(1,128)} %param.14) | copy-start | bytes 772
  8.6 101.6 %all-to-all-start.1 = ((bf16[16,8,1792]{2,1,0:T(8,128)(2,1)}), bf16[16,8,1792]{2,1,0:T(8,128)(2,1)S(1)}, u32[]{:S(2)}, u32[]{:S(2)}) async-start(bf16[16,8,1792]{2,1,0:T(8,128)(2,1)} %bitcast.15), calls=%async_computation.1 | async-start | bytes 917504 | tf_op jit(solution)/shard_map/all_to_all | solution.py:300
  38.4 22.2 %collective-permute-start.5 = (s32[1,64]{1,0:T(1,128)S(1)}, s32[1,64]{1,0:T(1,128)S(1)}, u32[]{:S(2)}, u32[]{:S(2)}) collective-permute-start(s32[1,64]{1,0:T(1,128)S(1)} %bitcast.33), channel_id=1, source_target_pairs={{0,32},{32,64},{64,96},{96,128},{128,160},{160,192},{192,224},{224... | collective-permute-start | bytes 776 | tf_op jit(solution)/shard_map/ppermute | solution.py:279
  41.1 30.9 %copy-start.3 = (s32[1,64,1]{1,2,0:T(1,128)S(1)}, s32[1,64,1]{1,2,0:T(1,128)}, u32[]{:S(2)}) copy-start(s32[1,64,1]{1,2,0:T(1,128)} %param.17) | copy-start | bytes 772
  41.1 69.1 %copy-start.5 = (bf16[1,1,128,512]{3,2,1,0:T(8,128)(2,1)S(1)}, bf16[1,1,128,512]{3,2,1,0:T(8,128)(2,1)}, u32[]{:S(2)}) copy-start(bf16[1,1,128,512]{3,2,1,0:T(8,128)(2,1)} %param.19) | copy-start | bytes 393220
  61.5 11.8 %collective-permute-start.7 = (bf16[8,3584]{1,0:T(8,128)(2,1)S(1)}, bf16[8,3584]{1,0:T(8,128)(2,1)S(1)}, u32[]{:S(2)}, u32[]{:S(2)}) collective-permute-start(bf16[8,3584]{1,0:T(8,128)(2,1)S(1)} %get-tuple-element.109), channel_id=1, source_target_pairs={{0,8},{8,16},{16,24},{24,0},{1,9},{9,17},{17,25},{25,1},{2,10},{10... | collective-permute-start | bytes 172040 | tf_op jit(solution)/shard_map/ppermute | solution.py:279
  64.6 8.7 %collective-permute-start.8 = (bf16[8,3584]{1,0:T(8,128)(2,1)S(1)}, bf16[8,3584]{1,0:T(8,128)(2,1)S(1)}, u32[]{:S(2)}, u32[]{:S(2)}) collective-permute-start(bf16[8,3584]{1,0:T(8,128)(2,1)S(1)} %get-tuple-element.110), channel_id=1, source_target_pairs={{0,16},{8,24},{16,0},{24,8},{1,17},{9,25},{17,1},{25,9},{2,18},{10... | collective-permute-start | bytes 172040 | tf_op jit(solution)/shard_map/ppermute | solution.py:279
  68.9 5.2 %collective-permute-start.9 = (bf16[8,3584]{1,0:T(8,128)(2,1)S(1)}, bf16[8,3584]{1,0:T(8,128)(2,1)S(1)}, u32[]{:S(2)}, u32[]{:S(2)}) collective-permute-start(bf16[8,3584]{1,0:T(8,128)(2,1)S(1)} %get-tuple-element.111), channel_id=1, source_target_pairs={{0,24},{8,0},{16,8},{24,16},{1,25},{9,1},{17,9},{25,17},{2,26},{10... | collective-permute-start | bytes 172040 | tf_op jit(solution)/shard_map/ppermute | solution.py:279
  74.3 87.5 %collective-permute-start.11 = (bf16[16,3584]{1,0:T(8,128)(2,1)S(1)}, bf16[16,3584]{1,0:T(8,128)(2,1)S(1)}, u32[]{:S(2)}, u32[]{:S(2)}) collective-permute-start(bf16[16,3584]{1,0:T(8,128)(2,1)S(1)} %get-tuple-element.113), channel_id=1, source_target_pairs={{0,6},{2,4},{4,2},{6,0},{1,7},{3,5},{5,3},{7,1},{8,14},{10,12},{12... | collective-permute-start | bytes 344072 | tf_op jit(solution)/shard_map/ppermute | solution.py:279
  96.5 65.3 %collective-permute-start.12 = (bf16[16,3584]{1,0:T(8,128)(2,1)S(1)}, bf16[16,3584]{1,0:T(8,128)(2,1)S(1)}, u32[]{:S(2)}, u32[]{:S(2)}) collective-permute-start(bf16[16,3584]{1,0:T(8,128)(2,1)S(1)} %get-tuple-element.113), channel_id=1, source_target_pairs={{0,4},{2,6},{4,0},{6,2},{1,5},{3,7},{5,1},{7,3},{8,12},{10,14},{12... | collective-permute-start | bytes 344072 | tf_op jit(solution)/shard_map/ppermute | solution.py:279
  99.8 51.4 %collective-permute-start.10 = (bf16[16,3584]{1,0:T(8,128)(2,1)S(1)}, bf16[16,3584]{1,0:T(8,128)(2,1)S(1)}, u32[]{:S(2)}, u32[]{:S(2)}) collective-permute-start(bf16[16,3584]{1,0:T(8,128)(2,1)S(1)} %get-tuple-element.268), channel_id=1, source_target_pairs={{0,2},{2,0},{4,6},{6,4},{1,3},{3,1},{5,7},{7,5},{8,10},{10,8},{12,... | collective-permute-start | bytes 344072 | tf_op jit(solution)/shard_map/ppermute | solution.py:279
  110.3 14.8 %collective-permute-start.2 = (bf16[128,1792]{1,0:T(8,128)(2,1)S(1)}, bf16[128,1792]{1,0:T(8,128)(2,1)S(1)}, u32[]{:S(2)}, u32[]{:S(2)}) collective-permute-start(bf16[128,1792]{1,0:T(8,128)(2,1)S(1)} %get-tuple-element.303.refs_1_), channel_id=1, source_target_pairs={{0,1},{1,0},{2,3},{3,2},{4,5},{5,4},{6,7},{7,6},{8,9},{9,8},{10,11... | collective-permute-start | bytes 1376264 | tf_op jit(solution)/shard_map/while/body/ppermute | solution.py:279
  130.8 3.7 %collective-permute-start.3 = (bf16[128,1792]{1,0:T(8,128)(2,1)S(1)}, bf16[128,1792]{1,0:T(8,128)(2,1)S(1)}, u32[]{:S(2)}, u32[]{:S(2)}) collective-permute-start(bf16[128,1792]{1,0:T(8,128)(2,1)S(1)} %get-tuple-element.265), channel_id=1, source_target_pairs={{0,1},{1,0},{2,3},{3,2},{4,5},{5,4},{6,7},{7,6},{8,9},{9,8},{10,11... | collective-permute-start | bytes 1376264 | tf_op jit(solution)/shard_map/while/body/ppermute | solution.py:279
  135.6 65.7 %collective-permute-start.13 = (bf16[16,3584]{1,0:T(8,128)(2,1)S(1)}, bf16[16,3584]{1,0:T(8,128)(2,1)S(1)}, u32[]{:S(2)}, u32[]{:S(2)}) collective-permute-start(bf16[16,3584]{1,0:T(8,128)(2,1)S(1)} %get-tuple-element.120), channel_id=1, source_target_pairs={{0,2},{2,0},{4,6},{6,4},{1,3},{3,1},{5,7},{7,5},{8,10},{10,8},{12,... | collective-permute-start | bytes 344072 | tf_op jit(solution)/shard_map/ppermute | solution.py:279
  138.8 62.6 %collective-permute-start.14 = (bf16[16,3584]{1,0:T(8,128)(2,1)S(1)}, bf16[16,3584]{1,0:T(8,128)(2,1)S(1)}, u32[]{:S(2)}, u32[]{:S(2)}) collective-permute-start(bf16[16,3584]{1,0:T(8,128)(2,1)S(1)} %get-tuple-element.121), channel_id=1, source_target_pairs={{0,6},{2,4},{4,2},{6,0},{1,7},{3,5},{5,3},{7,1},{8,14},{10,12},{12... | collective-permute-start | bytes 344072 | tf_op jit(solution)/shard_map/ppermute | solution.py:279
  151.2 50.2 %collective-permute-start.15 = (bf16[16,3584]{1,0:T(8,128)(2,1)S(1)}, bf16[16,3584]{1,0:T(8,128)(2,1)S(1)}, u32[]{:S(2)}, u32[]{:S(2)}) collective-permute-start(bf16[16,3584]{1,0:T(8,128)(2,1)S(1)} %get-tuple-element.122), channel_id=1, source_target_pairs={{0,4},{2,6},{4,0},{6,2},{1,5},{3,7},{5,1},{7,3},{8,12},{10,14},{12... | collective-permute-start | bytes 344072 | tf_op jit(solution)/shard_map/ppermute | solution.py:279
  161.8 6.9 %collective-permute-start = (bf16[64,3584]{1,0:T(8,128)(2,1)S(1)}, bf16[64,3584]{1,0:T(8,128)(2,1)S(1)}, u32[]{:S(2)}, u32[]{:S(2)}) collective-permute-start(bf16[64,3584]{1,0:T(8,128)(2,1)S(1)} %join_f.1.refs_0_), channel_id=1, source_target_pairs={{0,1},{1,0},{2,3},{3,2},{4,5},{5,4},{6,7},{7,6},{8,9},{9,8},{10,11... | collective-permute-start | bytes 1376264 | tf_op jit(solution)/shard_map/while/body/ppermute | solution.py:279
  171.9 3.7 %collective-permute-start.1 = (bf16[64,3584]{1,0:T(8,128)(2,1)S(1)}, bf16[64,3584]{1,0:T(8,128)(2,1)S(1)}, u32[]{:S(2)}, u32[]{:S(2)}) collective-permute-start(bf16[64,3584]{1,0:T(8,128)(2,1)S(1)} %get-tuple-element.253), channel_id=1, source_target_pairs={{0,1},{1,0},{2,3},{3,2},{4,5},{5,4},{6,7},{7,6},{8,9},{9,8},{10,11... | collective-permute-start | bytes 1376264 | tf_op jit(solution)/shard_map/while/body/ppermute | solution.py:279
  177.4 77.2 %all-to-all-start = ((bf16[16,8,1792]{2,1,0:T(8,128)(2,1)}), bf16[16,8,1792]{2,1,0:T(8,128)(2,1)S(1)}, u32[]{:S(2)}, u32[]{:S(2)}) async-start(bf16[16,8,1792]{2,1,0:T(8,128)(2,1)} %bitcast.12), calls=%async_computation | async-start | bytes 917504 | tf_op jit(solution)/shard_map/all_to_all | solution.py:300
  201.4 13.6 %copy-start.1 = (bf16[1,64,3584]{2,1,0:T(8,128)(2,1)S(1)}, bf16[1,64,3584]{2,1,0:T(8,128)(2,1)}, u32[]{:S(2)}) copy-start(bf16[1,64,3584]{2,1,0:T(8,128)(2,1)} %param.16) | copy-start | bytes 1376260
  201.4 31.6 %copy-start.7 = (f32[1,64,1]{1,2,0:T(1,128)S(1)}, f32[1,64,1]{1,2,0:T(1,128)}, u32[]{:S(2)}) copy-start(f32[1,64,1]{1,2,0:T(1,128)} %param.15) | copy-start | bytes 772
  201.6 9.5 %collective-permute-start.16 = (bf16[8,3584]{1,0:T(8,128)(2,1)S(1)}, bf16[8,3584]{1,0:T(8,128)(2,1)S(1)}, u32[]{:S(2)}, u32[]{:S(2)}) collective-permute-start(bf16[8,3584]{1,0:T(8,128)(2,1)S(1)} %get-tuple-element.124), channel_id=1, source_target_pairs={{0,24},{8,0},{16,8},{24,16},{1,25},{9,1},{17,9},{25,17},{2,26},{10... | collective-permute-start | bytes 172040 | tf_op jit(solution)/shard_map/ppermute | solution.py:279
  206.1 6.4 %collective-permute-start.17 = (bf16[8,3584]{1,0:T(8,128)(2,1)S(1)}, bf16[8,3584]{1,0:T(8,128)(2,1)S(1)}, u32[]{:S(2)}, u32[]{:S(2)}) collective-permute-start(bf16[8,3584]{1,0:T(8,128)(2,1)S(1)} %get-tuple-element.125), channel_id=1, source_target_pairs={{0,16},{8,24},{16,0},{24,8},{1,17},{9,25},{17,1},{25,9},{2,18},{10... | collective-permute-start | bytes 172040 | tf_op jit(solution)/shard_map/ppermute | solution.py:279
  208.6 6.4 %collective-permute-start.18 = (bf16[8,3584]{1,0:T(8,128)(2,1)S(1)}, bf16[8,3584]{1,0:T(8,128)(2,1)S(1)}, u32[]{:S(2)}, u32[]{:S(2)}) collective-permute-start(bf16[8,3584]{1,0:T(8,128)(2,1)S(1)} %get-tuple-element.126), channel_id=1, source_target_pairs={{0,8},{8,16},{16,24},{24,0},{1,9},{9,17},{17,25},{25,1},{2,10},{10... | collective-permute-start | bytes 172040 | tf_op jit(solution)/shard_map/ppermute | solution.py:279
  216.0 35.0 %collective-permute-start.19 = (bf16[64,3584]{1,0:T(8,128)(2,1)S(1)}, bf16[64,3584]{1,0:T(8,128)(2,1)S(1)}, u32[]{:S(2)}, u32[]{:S(2)}) collective-permute-start(bf16[64,3584]{1,0:T(8,128)(2,1)S(1)} %final_b.1), channel_id=1, source_target_pairs={{0,992},{32,0},{64,32},{96,64},{128,96},{160,128},{192,160},{224,1... | collective-permute-start | bytes 1376264 | tf_op jit(solution)/shard_map/ppermute | solution.py:279
  233.1 18.0 %collective-permute-start.6 = (f32[1,64]{1,0:T(1,128)S(1)}, f32[1,64]{1,0:T(1,128)S(1)}, u32[]{:S(2)}, u32[]{:S(2)}) collective-permute-start(f32[1,64]{1,0:T(1,128)S(1)} %bitcast.34), channel_id=1, source_target_pairs={{0,32},{32,64},{64,96},{96,128},{128,160},{160,192},{192,224},{224... | collective-permute-start | bytes 776 | tf_op jit(solution)/shard_map/ppermute | solution.py:279

commit v5 on v4

--- a/solution.py
+++ b/solution.py
@@ -101,17 +101,17 @@
     out_ref[...] = total.astype(BF16)
 
 
-def expert_b_kernel(cap, c_ref, own_ref, oth_ref, *refs):
+def expert_b_kernel(cap, c_ref, both_ref, *refs):
     far, (mine_ref, send_ref), near, sems = refs[:3], refs[3:5], refs[5:8], refs[8]
     wd_ref, saved_ref, wgu_ref = near
     wd_copy, saved_copy, wgu_copy = stream(far, near, sems)
-    rows, half = own_ref.shape
+    rows, half = mine_ref.shape
     hid, width = wd_ref.shape
-    values = jnp.concatenate([joined(own_ref[...], cap), joined(oth_ref[...], cap)], axis=0)
+    values = jnp.concatenate([joined(both_ref[:rows], cap), joined(both_ref[rows:], cap)], axis=0)
     wd_copy.wait()
     dh = dot(values, wd_ref[...], ((1,), (1,)))
     r, p = iota((rows, rows), 0), iota((rows, rows), 1)
-    core = jnp.where(r < rows // 2, c_ref[0], 1 - c_ref[0])
+    core = r // (rows // 2)
     r = r % (rows // 2)
     pick = (p // (2 * cap) == r // cap) & (p % cap == r % cap) & ((p % (2 * cap)) // cap == core)
     saved_copy.wait()
@@ -130,8 +130,10 @@
             for base in (0, half)
         )
         mid = rows // 2
-        mine_ref[:, at : at + step] = parted(low[:mid], high[:mid], cap, rows)
-        send_ref[:, at : at + step] = parted(low[mid:], high[mid:], cap, rows)
+        first = parted(low[:mid], high[:mid], cap, rows)
+        second = parted(low[mid:], high[mid:], cap, rows)
+        mine_ref[:, at : at + step] = jnp.where(c_ref[0] == 0, first, second)
+        send_ref[:, at : at + step] = jnp.where(c_ref[0] == 0, second, first)
 
 
 def split_b_kernel(cap, at_ref, rows_ref, *out_refs):
@@ -197,23 +199,22 @@
     refs[-1][...] = slab(refs[:-1])
 
 
-def expert_f_kernel(own_ref, oth_ref, *refs):
+def expert_f_kernel(c_ref, both_ref, *refs):
     far, (mine_ref, send_ref), near, sems = refs[:2], refs[2:4], refs[4:6], refs[6]
     wgu_ref, wd_ref = near
     wgu_copy, wd_copy = stream(far, near, sems)
-    rows = own_ref.shape[0]
+    rows = mine_ref.shape[0]
     hid, width = wd_ref.shape
-    values = slab((own_ref, oth_ref))
     wgu_copy.wait()
-    pre = dot(values, wgu_ref[...])
+    pre = dot(both_ref[...], wgu_ref[...])
     gate = pre[:, :hid]
     hidden = (gate / (1.0 + jnp.exp(-gate)) * pre[:, hid:]).astype(BF16)
     wd_copy.wait()
     step = 512 if width % 512 == 0 else width
     for at in range(0, width, step):
         part = dot(hidden, wd_ref[:, at : at + step]).astype(BF16)
-        mine_ref[:, at : at + step] = part[:rows]
-        send_ref[:, at : at + step] = part[rows:]
+        mine_ref[:, at : at + step] = jnp.where(c_ref[0] == 0, part[:rows], part[rows:])
+        send_ref[:, at : at + step] = jnp.where(c_ref[0] == 0, part[rows:], part[:rows])
 
 
 def add_kernel(a_ref, b_ref, *out_refs):
@@ -279,6 +280,10 @@
     return lax.ppermute(block, axis, [(i, to(i)) for i in range(lax.axis_size(axis))])
 
 
+def both_cores(block):
+    return lax.all_gather(block, "c", axis=0, tiled=True)
+
+
 def swap_core(block):
     return moved(block, "c", lambda i: 1 - i)
 
@@ -343,6 +348,7 @@
         [half],
         (cot, route_b, gate_b),
         2 * many * tokens * width,
+        earlier=(route_f,),
     )
     own_b = exchange(packed, cap)
 
@@ -365,7 +371,7 @@
             kernel(expert_b_kernel, cap),
             "expert_b",
             [half] * 2,
-            (core, rows, swap_core(rows), wd, saved_pre[0, 0], wgu),
+            (core, both_cores(rows), wd, saved_pre[0, 0], wgu),
             6 * many * hid * width,
             streamed=3,
         )
@@ -384,7 +390,7 @@
     def chain_f(_, blocks):
         (own,) = call(join_kernel, "join_f", [(few, width)], blocks, few * width)
         mine, send = call(
-            expert_f_kernel, "expert_f", [(few, width)] * 2, (own, swap_core(own), wgu, wd), 6 * many * hid * width, streamed=2
+            expert_f_kernel, "expert_f", [(few, width)] * 2, (core, both_cores(own), wgu, wd), 6 * many * hid * width, streamed=2
         )
         return tuple(
             call(add_kernel, "add_f", [(block, width)] * Z_GROUPS, (mine, swap_core(send)), few * width)

time: 258 us -> 243 us (0.942)
  the two profiles are of different devices: /device:TPU:1 before, /device:TPU:145 now
where the time goes in v5:
time: 243 us; the launch traced here: 242 us
  starting transfers between devices  152 us (63%)
  waiting for transfers between devices  43 us (18%)
  blocking collectives  24.8 us (10%)
  Pallas kernels  16.5 us (7%)
  local copies, waits for them, and re-layouts  3.12 us (1%)
    ppermute x18, starting transfers between devices, moved(): lax.ppermute(block, axis, [(i, to(i)) for i in range(lax.axis_size(axis))])  116 us
    all_to_all x2, starting transfers between devices, exchange(): lax.all_to_all(blocks, ('x', 'zh'), split_axis=0, concat_axis=0, tiled=True)  36.1 us
    all_to_all x2, waiting for transfers between devices, exchange(): lax.all_to_all(blocks, ('x', 'zh'), split_axis=0, concat_axis=0, tiled=True)  24.9 us
    all_gather x2, blocking collectives, both_cores(): return lax.all_gather(block, 'c', axis=0, tiled=True)  24.8 us
    ppermute x18, waiting for transfers between devices, moved(): lax.ppermute(block, axis, [(i, to(i)) for i in range(lax.axis_size(axis))])  18.1 us
    pallas_call x12, Pallas kernels, call(): pl.pallas_call(body, out_shape=out, in_specs=[SMEM if a.ndim == 1 else VM...  16.5 us
  transfers between devices with their start and end apart: 20, of which 8 were waited for; matrix products, arithmetic and copies ran while one was open for 0% of the time, Pallas kernels for 7%

profile of v5, /device:TPU:145, one launch (start us, length us, event | category | flops | bytes accessed | tf_op | source)
XLA Modules:
  0.0 241.9 jit_solution(14549943986659348615)
XLA Ops:
  0.6 3.5 %collective-permute-start.3 = (s32[1,64]{1,0:T(1,128)}, s32[1,64]{1,0:T(1,128)S(1)}, u32[]{:S(2)}, u32[]{:S(2)}) collective-permute-start(s32[1,64]{1,0:T(1,128)} %bitcast.33), channel_id=1, source_target_pairs={{0,32},{32,64},{64,96},{96,128},{128,160},{160,192},{192,224},{224... | collective-permute-start | bytes 776 | tf_op jit(solution)/shard_map/ppermute | solution.py:280
  4.2 3.5 %collective-permute-start.2 = (bf16[64,3584]{1,0:T(8,128)(2,1)}, bf16[64,3584]{1,0:T(8,128)(2,1)S(1)}, u32[]{:S(2)}, u32[]{:S(2)}) collective-permute-start(bf16[64,3584]{1,0:T(8,128)(2,1)} %bitcast.32), channel_id=1, source_target_pairs={{0,32},{32,64},{64,96},{96,128},{128,160},{160,192},{192,224},{224... | collective-permute-start | bytes 1376264 | tf_op jit(solution)/shard_map/ppermute | solution.py:280
  7.7 0.1 pad_add_fusion.refs_0_
  7.8 0.0 collective-permute-done.3.refs_3_.refs_2_.refs_1_
  7.8 1.0 copy-done
  8.8 0.7 copy-done.2
  9.5 0.7 copy-done.4
  10.2 1.3 pack_b.1.refs_3_
  11.4 24.3 %all-to-all-start.1 = ((bf16[16,8,1792]{2,1,0:T(8,128)(2,1)}), bf16[16,8,1792]{2,1,0:T(8,128)(2,1)S(1)}, u32[]{:S(2)}, u32[]{:S(2)}) async-start(bf16[16,8,1792]{2,1,0:T(8,128)(2,1)} %bitcast.15), calls=%async_computation.1 | async-start | bytes 917504 | tf_op jit(solution)/shard_map/all_to_all | solution.py:305
  35.7 0.0 copy-start.3
  35.7 0.0 copy-start.5
  35.7 0.0 collective-permute-done.2.refs_1_.refs_0_
  35.7 0.9 pack_f.1
  36.6 3.3 %collective-permute-start.5 = (bf16[8,3584]{1,0:T(8,128)(2,1)S(1)}, bf16[8,3584]{1,0:T(8,128)(2,1)S(1)}, u32[]{:S(2)}, u32[]{:S(2)}) collective-permute-start(bf16[8,3584]{1,0:T(8,128)(2,1)S(1)} %get-tuple-element.114), channel_id=1, source_target_pairs={{0,8},{8,16},{16,24},{24,0},{1,9},{9,17},{17,25},{25,1},{2,10},{10... | collective-permute-start | bytes 172040 | tf_op jit(solution)/shard_map/ppermute | solution.py:280
  39.9 4.3 %collective-permute-start.6 = (bf16[8,3584]{1,0:T(8,128)(2,1)S(1)}, bf16[8,3584]{1,0:T(8,128)(2,1)S(1)}, u32[]{:S(2)}, u32[]{:S(2)}) collective-permute-start(bf16[8,3584]{1,0:T(8,128)(2,1)S(1)} %get-tuple-element.115), channel_id=1, source_target_pairs={{0,16},{8,24},{16,0},{24,8},{1,17},{9,25},{17,1},{25,9},{2,18},{10... | collective-permute-start | bytes 172040 | tf_op jit(solution)/shard_map/ppermute | solution.py:280
  44.2 3.1 %collective-permute-start.7 = (bf16[8,3584]{1,0:T(8,128)(2,1)S(1)}, bf16[8,3584]{1,0:T(8,128)(2,1)S(1)}, u32[]{:S(2)}, u32[]{:S(2)}) collective-permute-start(bf16[8,3584]{1,0:T(8,128)(2,1)S(1)} %get-tuple-element.116), channel_id=1, source_target_pairs={{0,24},{8,0},{16,8},{24,16},{1,25},{9,1},{17,9},{25,17},{2,26},{10... | collective-permute-start | bytes 172040 | tf_op jit(solution)/shard_map/ppermute | solution.py:280
  47.3 0.7 fusion
  48.7 0.0 collective-permute-done.5.refs_1_
  48.7 0.0 collective-permute-done.6.refs_2_
  48.7 0.7 collective-permute-done.7.refs_3_
  49.4 0.2 pairs_f.1
  49.6 21.4 %collective-permute-start.10 = (bf16[16,3584]{1,0:T(8,128)(2,1)S(1)}, bf16[16,3584]{1,0:T(8,128)(2,1)S(1)}, u32[]{:S(2)}, u32[]{:S(2)}) collective-permute-start(bf16[16,3584]{1,0:T(8,128)(2,1)S(1)} %get-tuple-element.118), channel_id=1, source_target_pairs={{0,4},{2,6},{4,0},{6,2},{1,5},{3,7},{5,1},{7,3},{8,12},{10,14},{12... | collective-permute-start | bytes 344072 | tf_op jit(solution)/shard_map/ppermute | solution.py:280
  71.1 2.7 %collective-permute-start.9 = (bf16[16,3584]{1,0:T(8,128)(2,1)S(1)}, bf16[16,3584]{1,0:T(8,128)(2,1)S(1)}, u32[]{:S(2)}, u32[]{:S(2)}) collective-permute-start(bf16[16,3584]{1,0:T(8,128)(2,1)S(1)} %get-tuple-element.118), channel_id=1, source_target_pairs={{0,6},{2,4},{4,2},{6,0},{1,7},{3,5},{5,3},{7,1},{8,14},{10,12},{12... | collective-permute-start | bytes 344072 | tf_op jit(solution)/shard_map/ppermute | solution.py:280
  73.7 1.9 collective-permute-start.8
  75.7 2.3 all-to-all-done.1
  78.0 31.4 %while.27 = (s32[]{:T(128)}, bf16[128,1792]{1,0:T(8,128)(2,1)S(1)}, s32[]{:T(128)}, bf16[1,1,128,512]{3,2,1,0:T(8,128)(2,1)S(1)}, s32[1]{0:T(128)}, /*index=5*/b...) while((s32[]{:T(128)}, bf16[128,1792]{1,0:T(8,128)(2,1)S(1)}, s32[]{:T(128)}, ...), condition=%wide.region_4.0_spmd, body=%wide.region_3.0_spmd.sunk | while | flops 705560576 | bytes 12058753 | solution.py:380
  78.0 21.8 %all_gather.9.refs_1_ = bf16[256,1792]{1,0:T(8,128)(2,1)S(1)} all-gather(bf16[128,1792]{1,0:T(8,128)(2,1)S(1)} %get-tuple-element.319), channel_id=1, replica_groups=mesh['pp'=32,'x'=4,'zh'=4,'c'=2] {'c'}, dimensions={0}, use_global_device_ids=true | all-gather | bytes 1376256 | tf_op jit(solution)/shard_map/while/body/all_gather | solution.py:284
  99.8 5.7 %expert_b.1 = (bf16[128,1792]{1,0:T(8,128)(2,1)S(1)}, bf16[128,1792]{1,0:T(8,128)(2,1)S(1)}) custom-call(s32[1]{0:T(128)} %get-tuple-element.330.refs_0_, bf16[256,1792]{1,0:T(8,128)(2,1)S(1)} %all_gather.9.refs_1_, bf16[256,3584]{1,0:T(8,128)(2,1)} %get-tuple-element.331.refs_2_, bf16[128,512]{1,0:T(8,128)(2,1)S(1)} %bitcast.29, ...), custom_call_target="tpu_custom_call" | custom-call | flops 704643072 | bytes 7471108 | tf_op jit(solution)/shard_map/while/body/expert_b/pallas_call | solution.py:264
  105.5 2.3 collective-permute-start.1
  107.8 1.4 collective-permute-done.1
  109.2 0.1 add_convert_fusion.2
  109.4 1.0 split_b.1
  110.3 39.0 %collective-permute-start.11 = (bf16[16,3584]{1,0:T(8,128)(2,1)S(1)}, bf16[16,3584]{1,0:T(8,128)(2,1)S(1)}, u32[]{:S(2)}, u32[]{:S(2)}) collective-permute-start(bf16[16,3584]{1,0:T(8,128)(2,1)S(1)} %get-tuple-element.125), channel_id=1, source_target_pairs={{0,2},{2,0},{4,6},{6,4},{1,3},{3,1},{5,7},{7,5},{8,10},{10,8},{12,... | collective-permute-start | bytes 344072 | tf_op jit(solution)/shard_map/ppermute | solution.py:280
  149.3 1.9 collective-permute-start.12
  151.2 0.0 collective-permute-done.10
  151.2 11.8 %collective-permute-start.13 = (bf16[16,3584]{1,0:T(8,128)(2,1)S(1)}, bf16[16,3584]{1,0:T(8,128)(2,1)S(1)}, u32[]{:S(2)}, u32[]{:S(2)}) collective-permute-start(bf16[16,3584]{1,0:T(8,128)(2,1)S(1)} %get-tuple-element.127), channel_id=1, source_target_pairs={{0,4},{2,6},{4,0},{6,2},{1,5},{3,7},{5,1},{7,3},{8,12},{10,14},{12... | collective-permute-start | bytes 344072 | tf_op jit(solution)/shard_map/ppermute | solution.py:280
  163.1 0.0 collective-permute-done.8
  163.1 0.0 collective-permute-done.9
  163.1 10.1 %while.26 = (s32[]{:T(128)}, bf16[16,3584]{1,0:T(8,128)(2,1)S(1)}, bf16[16,3584]{1,0:T(8,128)(2,1)S(1)}, bf16[16,3584]{1,0:T(8,128)(2,1)S(1)}, bf16[16,3584]{1,0...) while((s32[]{:T(128)}, bf16[16,3584]{1,0:T(8,128)(2,1)S(1)}, ...), condition=%wide.region_2.0_spmd, body=%wide.region_1.0_spmd.sunk | while | flops 705101824 | bytes 12845201 | solution.py:399
  163.1 3.0 %all_gather.8.refs_1_ = bf16[128,3584]{1,0:T(8,128)(2,1)S(1)} all-gather(bf16[64,3584]{1,0:T(8,128)(2,1)S(1)} %join_f.1), channel_id=1, replica_groups=mesh['pp'=32,'x'=4,'zh'=4,'c'=2] {'c'}, dimensions={0}, use_global_device_ids=true | all-gather | bytes 1376256 | tf_op jit(solution)/shard_map/while/body/all_gather | solution.py:284
  166.2 3.1 %expert_f.1 = (bf16[64,3584]{1,0:T(8,128)(2,1)S(1)}, bf16[64,3584]{1,0:T(8,128)(2,1)S(1)}) custom-call(s32[1]{0:T(128)} %get-tuple-element.306.refs_0_, bf16[128,3584]{1,0:T(8,128)(2,1)S(1)} %all_gather.8.refs_1_, bf16[3584,512]{1,0:T(8,128)(2,1)} %get-tuple-element.307.refs_2_, bf16[256,3584]{1,0:T(8,128)(2,1)} %get-tuple-element.308.refs_3_), custom_call_target="tpu_custom_call" | custom-call | flops 704643072 | bytes 7340036 | tf_op jit(solution)/shard_map/while/body/expert_f/pallas_call | solution.py:264
  169.3 2.3 collective-permute-start
  171.6 1.4 collective-permute-done.refs_1_
  173.0 0.1 add_f.1
  173.1 1.7 spread_f.1
  174.8 11.8 %all-to-all-start = ((bf16[16,8,1792]{2,1,0:T(8,128)(2,1)}), bf16[16,8,1792]{2,1,0:T(8,128)(2,1)S(1)}, u32[]{:S(2)}, u32[]{:S(2)}) async-start(bf16[16,8,1792]{2,1,0:T(8,128)(2,1)} %bitcast.12), calls=%async_computation | async-start | bytes 917504 | tf_op jit(solution)/shard_map/all_to_all | solution.py:305
  186.7 0.0 collective-permute-done.12.refs_2_
  186.7 0.0 collective-permute-done.13.refs_3_
  186.7 0.0 copy-start.1
  186.7 0.0 copy-start.6
  186.7 0.2 merge_b.1
  186.9 4.5 %collective-permute-start.14 = (bf16[8,3584]{1,0:T(8,128)(2,1)S(1)}, bf16[8,3584]{1,0:T(8,128)(2,1)S(1)}, u32[]{:S(2)}, u32[]{:S(2)}) collective-permute-start(bf16[8,3584]{1,0:T(8,128)(2,1)S(1)} %get-tuple-element.129), channel_id=1, source_target_pairs={{0,24},{8,0},{16,8},{24,16},{1,25},{9,1},{17,9},{25,17},{2,26},{10... | collective-permute-start | bytes 172040 | tf_op jit(solution)/shard_map/ppermute | solution.py:280
  191.4 2.5 %collective-permute-start.15 = (bf16[8,3584]{1,0:T(8,128)(2,1)S(1)}, bf16[8,3584]{1,0:T(8,128)(2,1)S(1)}, u32[]{:S(2)}, u32[]{:S(2)}) collective-permute-start(bf16[8,3584]{1,0:T(8,128)(2,1)S(1)} %get-tuple-element.130), channel_id=1, source_target_pairs={{0,16},{8,24},{16,0},{24,8},{1,17},{9,25},{17,1},{25,9},{2,18},{10... | collective-permute-start | bytes 172040 | tf_op jit(solution)/shard_map/ppermute | solution.py:280
  193.9 2.5 %collective-permute-start.16 = (bf16[8,3584]{1,0:T(8,128)(2,1)S(1)}, bf16[8,3584]{1,0:T(8,128)(2,1)S(1)}, u32[]{:S(2)}, u32[]{:S(2)}) collective-permute-start(bf16[8,3584]{1,0:T(8,128)(2,1)S(1)} %get-tuple-element.131), channel_id=1, source_target_pairs={{0,8},{8,16},{16,24},{24,0},{1,9},{9,17},{17,25},{25,1},{2,10},{10... | collective-permute-start | bytes 172040 | tf_op jit(solution)/shard_map/ppermute | solution.py:280
  196.4 0.0 collective-permute-done.14.refs_4_
  196.4 1.4 collective-permute-done.15.refs_5_
  197.9 2.4 %collective-permute-done.16.refs_6_ = bf16[8,3584]{1,0:T(8,128)(2,1)S(1)} collective-permute-done((bf16[8,3584]{1,0:T(8,128)(2,1)S(1)}, bf16[8,3584]{1,0:T(8,128)(2,1)S(1)}, u32[]{:S(2)}, u32[]{:S(2)}) %collective-permute-start.16) | collective-permute-done | bytes 57376 | tf_op jit(solution)/shard_map/ppermute | solution.py:280
  200.3 1.0 final_b.1
  201.3 1.9 collective-permute-start.17
  203.3 3.4 %collective-permute-start.4 = (f32[1,64]{1,0:T(1,128)S(1)}, f32[1,64]{1,0:T(1,128)S(1)}, u32[]{:S(2)}, u32[]{:S(2)}) collective-permute-start(f32[1,64]{1,0:T(1,128)S(1)} %bitcast.34), channel_id=1, source_target_pairs={{0,32},{32,64},{64,96},{96,128},{128,160},{160,192},{192,224},{224... | collective-permute-start | bytes 776 | tf_op jit(solution)/shard_map/ppermute | solution.py:280
  206.6 10.6 %collective-permute-done.4.refs_2_ = f32[1,64]{1,0:T(1,128)S(1)} collective-permute-done((f32[1,64]{1,0:T(1,128)S(1)}, f32[1,64]{1,0:T(1,128)S(1)}, u32[]{:S(2)}, u32[]{:S(2)}) %collective-permute-start.4) | collective-permute-done | bytes 288 | tf_op jit(solution)/shard_map/ppermute | solution.py:280
  217.3 22.6 %all-to-all-done = bf16[16,8,1792]{2,1,0:T(8,128)(2,1)S(1)} async-done(((bf16[16,8,1792]{2,1,0:T(8,128)(2,1)}), bf16[16,8,1792]{2,1,0:T(8,128)(2,1)S(1)}, u32[]{:S(2)}, u32[]{:S(2)}) %all-to-all-start) | async-done | bytes 458784 | tf_op jit(solution)/shard_map/all_to_all | solution.py:305
  239.9 1.3 final_f.1
  241.2 0.8 copy.34
  (10 shorter events, 0.1 us)
Async XLA Ops:
  0.6 7.2 %collective-permute-start.3 = (s32[1,64]{1,0:T(1,128)}, s32[1,64]{1,0:T(1,128)S(1)}, u32[]{:S(2)}, u32[]{:S(2)}) collective-permute-start(s32[1,64]{1,0:T(1,128)} %bitcast.33), channel_id=1, source_target_pairs={{0,32},{32,64},{64,96},{96,128},{128,160},{160,192},{192,224},{224... | collective-permute-start | bytes 776 | tf_op jit(solution)/shard_map/ppermute | solution.py:280
  4.2 31.5 %collective-permute-start.2 = (bf16[64,3584]{1,0:T(8,128)(2,1)}, bf16[64,3584]{1,0:T(8,128)(2,1)S(1)}, u32[]{:S(2)}, u32[]{:S(2)}) collective-permute-start(bf16[64,3584]{1,0:T(8,128)(2,1)} %bitcast.32), channel_id=1, source_target_pairs={{0,32},{32,64},{64,96},{96,128},{128,160},{160,192},{192,224},{224... | collective-permute-start | bytes 1376264 | tf_op jit(solution)/shard_map/ppermute | solution.py:280
  7.8 1.0 copy-start
  8.8 0.7 copy-start.2
  9.5 0.7 copy-start.4
  11.4 66.5 %all-to-all-start.1 = ((bf16[16,8,1792]{2,1,0:T(8,128)(2,1)}), bf16[16,8,1792]{2,1,0:T(8,128)(2,1)S(1)}, u32[]{:S(2)}, u32[]{:S(2)}) async-start(bf16[16,8,1792]{2,1,0:T(8,128)(2,1)} %bitcast.15), calls=%async_computation.1 | async-start | bytes 917504 | tf_op jit(solution)/shard_map/all_to_all | solution.py:305
  35.7 11.6 %copy-start.3 = (s32[1,64,1]{1,2,0:T(1,128)S(1)}, s32[1,64,1]{1,2,0:T(1,128)}, u32[]{:S(2)}) copy-start(s32[1,64,1]{1,2,0:T(1,128)} %param.17) | copy-start | bytes 772
  35.7 42.3 %copy-start.5 = (bf16[1,1,128,512]{3,2,1,0:T(8,128)(2,1)S(1)}, bf16[1,1,128,512]{3,2,1,0:T(8,128)(2,1)}, u32[]{:S(2)}) copy-start(bf16[1,1,128,512]{3,2,1,0:T(8,128)(2,1)} %param.19) | copy-start | bytes 393220
  36.6 12.1 %collective-permute-start.5 = (bf16[8,3584]{1,0:T(8,128)(2,1)S(1)}, bf16[8,3584]{1,0:T(8,128)(2,1)S(1)}, u32[]{:S(2)}, u32[]{:S(2)}) collective-permute-start(bf16[8,3584]{1,0:T(8,128)(2,1)S(1)} %get-tuple-element.114), channel_id=1, source_target_pairs={{0,8},{8,16},{16,24},{24,0},{1,9},{9,17},{17,25},{25,1},{2,10},{10... | collective-permute-start | bytes 172040 | tf_op jit(solution)/shard_map/ppermute | solution.py:280
  39.9 8.8 %collective-permute-start.6 = (bf16[8,3584]{1,0:T(8,128)(2,1)S(1)}, bf16[8,3584]{1,0:T(8,128)(2,1)S(1)}, u32[]{:S(2)}, u32[]{:S(2)}) collective-permute-start(bf16[8,3584]{1,0:T(8,128)(2,1)S(1)} %get-tuple-element.115), channel_id=1, source_target_pairs={{0,16},{8,24},{16,0},{24,8},{1,17},{9,25},{17,1},{25,9},{2,18},{10... | collective-permute-start | bytes 172040 | tf_op jit(solution)/shard_map/ppermute | solution.py:280
  44.2 5.2 %collective-permute-start.7 = (bf16[8,3584]{1,0:T(8,128)(2,1)S(1)}, bf16[8,3584]{1,0:T(8,128)(2,1)S(1)}, u32[]{:S(2)}, u32[]{:S(2)}) collective-permute-start(bf16[8,3584]{1,0:T(8,128)(2,1)S(1)} %get-tuple-element.116), channel_id=1, source_target_pairs={{0,24},{8,0},{16,8},{24,16},{1,25},{9,1},{17,9},{25,17},{2,26},{10... | collective-permute-start | bytes 172040 | tf_op jit(solution)/shard_map/ppermute | solution.py:280
  49.6 101.6 %collective-permute-start.10 = (bf16[16,3584]{1,0:T(8,128)(2,1)S(1)}, bf16[16,3584]{1,0:T(8,128)(2,1)S(1)}, u32[]{:S(2)}, u32[]{:S(2)}) collective-permute-start(bf16[16,3584]{1,0:T(8,128)(2,1)S(1)} %get-tuple-element.118), channel_id=1, source_target_pairs={{0,4},{2,6},{4,0},{6,2},{1,5},{3,7},{5,1},{7,3},{8,12},{10,14},{12... | collective-permute-start | bytes 344072 | tf_op jit(solution)/shard_map/ppermute | solution.py:280
  71.1 92.0 %collective-permute-start.9 = (bf16[16,3584]{1,0:T(8,128)(2,1)S(1)}, bf16[16,3584]{1,0:T(8,128)(2,1)S(1)}, u32[]{:S(2)}, u32[]{:S(2)}) collective-permute-start(bf16[16,3584]{1,0:T(8,128)(2,1)S(1)} %get-tuple-element.118), channel_id=1, source_target_pairs={{0,6},{2,4},{4,2},{6,0},{1,7},{3,5},{5,3},{7,1},{8,14},{10,12},{12... | collective-permute-start | bytes 344072 | tf_op jit(solution)/shard_map/ppermute | solution.py:280
  73.7 89.3 %collective-permute-start.8 = (bf16[16,3584]{1,0:T(8,128)(2,1)S(1)}, bf16[16,3584]{1,0:T(8,128)(2,1)S(1)}, u32[]{:S(2)}, u32[]{:S(2)}) collective-permute-start(bf16[16,3584]{1,0:T(8,128)(2,1)S(1)} %get-tuple-element.281), channel_id=1, source_target_pairs={{0,2},{2,0},{4,6},{6,4},{1,3},{3,1},{5,7},{7,5},{8,10},{10,8},{12,... | collective-permute-start | bytes 344072 | tf_op jit(solution)/shard_map/ppermute | solution.py:280
  105.5 3.7 %collective-permute-start.1 = (bf16[128,1792]{1,0:T(8,128)(2,1)S(1)}, bf16[128,1792]{1,0:T(8,128)(2,1)S(1)}, u32[]{:S(2)}, u32[]{:S(2)}) collective-permute-start(bf16[128,1792]{1,0:T(8,128)(2,1)S(1)} %get-tuple-element.278), channel_id=1, source_target_pairs={{0,1},{1,0},{2,3},{3,2},{4,5},{5,4},{6,7},{7,6},{8,9},{9,8},{10,11... | collective-permute-start | bytes 1376264 | tf_op jit(solution)/shard_map/while/body/ppermute | solution.py:280
  110.3 76.3 %collective-permute-start.11 = (bf16[16,3584]{1,0:T(8,128)(2,1)S(1)}, bf16[16,3584]{1,0:T(8,128)(2,1)S(1)}, u32[]{:S(2)}, u32[]{:S(2)}) collective-permute-start(bf16[16,3584]{1,0:T(8,128)(2,1)S(1)} %get-tuple-element.125), channel_id=1, source_target_pairs={{0,2},{2,0},{4,6},{6,4},{1,3},{3,1},{5,7},{7,5},{8,10},{10,8},{12,... | collective-permute-start | bytes 344072 | tf_op jit(solution)/shard_map/ppermute | solution.py:280
  149.3 37.4 %collective-permute-start.12 = (bf16[16,3584]{1,0:T(8,128)(2,1)S(1)}, bf16[16,3584]{1,0:T(8,128)(2,1)S(1)}, u32[]{:S(2)}, u32[]{:S(2)}) collective-permute-start(bf16[16,3584]{1,0:T(8,128)(2,1)S(1)} %get-tuple-element.126), channel_id=1, source_target_pairs={{0,6},{2,4},{4,2},{6,0},{1,7},{3,5},{5,3},{7,1},{8,14},{10,12},{12... | collective-permute-start | bytes 344072 | tf_op jit(solution)/shard_map/ppermute | solution.py:280
  151.2 35.5 %collective-permute-start.13 = (bf16[16,3584]{1,0:T(8,128)(2,1)S(1)}, bf16[16,3584]{1,0:T(8,128)(2,1)S(1)}, u32[]{:S(2)}, u32[]{:S(2)}) collective-permute-start(bf16[16,3584]{1,0:T(8,128)(2,1)S(1)} %get-tuple-element.127), channel_id=1, source_target_pairs={{0,4},{2,6},{4,0},{6,2},{1,5},{3,7},{5,1},{7,3},{8,12},{10,14},{12... | collective-permute-start | bytes 344072 | tf_op jit(solution)/shard_map/ppermute | solution.py:280
  169.3 3.7 %collective-permute-start = (bf16[64,3584]{1,0:T(8,128)(2,1)S(1)}, bf16[64,3584]{1,0:T(8,128)(2,1)S(1)}, u32[]{:S(2)}, u32[]{:S(2)}) collective-permute-start(bf16[64,3584]{1,0:T(8,128)(2,1)S(1)} %get-tuple-element.266), channel_id=1, source_target_pairs={{0,1},{1,0},{2,3},{3,2},{4,5},{5,4},{6,7},{7,6},{8,9},{9,8},{10,11... | collective-permute-start | bytes 1376264 | tf_op jit(solution)/shard_map/while/body/ppermute | solution.py:280
  174.8 65.0 %all-to-all-start = ((bf16[16,8,1792]{2,1,0:T(8,128)(2,1)}), bf16[16,8,1792]{2,1,0:T(8,128)(2,1)S(1)}, u32[]{:S(2)}, u32[]{:S(2)}) async-start(bf16[16,8,1792]{2,1,0:T(8,128)(2,1)} %bitcast.12), calls=%async_computation | async-start | bytes 917504 | tf_op jit(solution)/shard_map/all_to_all | solution.py:305
  186.7 13.6 %copy-start.1 = (bf16[1,64,3584]{2,1,0:T(8,128)(2,1)S(1)}, bf16[1,64,3584]{2,1,0:T(8,128)(2,1)}, u32[]{:S(2)}) copy-start(bf16[1,64,3584]{2,1,0:T(8,128)(2,1)} %param.16) | copy-start | bytes 1376260
  186.7 16.5 %copy-start.6 = (f32[1,64,1]{1,2,0:T(1,128)S(1)}, f32[1,64,1]{1,2,0:T(1,128)}, u32[]{:S(2)}) copy-start(f32[1,64,1]{1,2,0:T(1,128)} %param.15) | copy-start | bytes 772
  186.9 9.5 %collective-permute-start.14 = (bf16[8,3584]{1,0:T(8,128)(2,1)S(1)}, bf16[8,3584]{1,0:T(8,128)(2,1)S(1)}, u32[]{:S(2)}, u32[]{:S(2)}) collective-permute-start(bf16[8,3584]{1,0:T(8,128)(2,1)S(1)} %get-tuple-element.129), channel_id=1, source_target_pairs={{0,24},{8,0},{16,8},{24,16},{1,25},{9,1},{17,9},{25,17},{2,26},{10... | collective-permute-start | bytes 172040 | tf_op jit(solution)/shard_map/ppermute | solution.py:280
  191.4 6.4 %collective-permute-start.15 = (bf16[8,3584]{1,0:T(8,128)(2,1)S(1)}, bf16[8,3584]{1,0:T(8,128)(2,1)S(1)}, u32[]{:S(2)}, u32[]{:S(2)}) collective-permute-start(bf16[8,3584]{1,0:T(8,128)(2,1)S(1)} %get-tuple-element.130), channel_id=1, source_target_pairs={{0,16},{8,24},{16,0},{24,8},{1,17},{9,25},{17,1},{25,9},{2,18},{10... | collective-permute-start | bytes 172040 | tf_op jit(solution)/shard_map/ppermute | solution.py:280
  193.9 6.4 %collective-permute-start.16 = (bf16[8,3584]{1,0:T(8,128)(2,1)S(1)}, bf16[8,3584]{1,0:T(8,128)(2,1)S(1)}, u32[]{:S(2)}, u32[]{:S(2)}) collective-permute-start(bf16[8,3584]{1,0:T(8,128)(2,1)S(1)} %get-tuple-element.131), channel_id=1, source_target_pairs={{0,8},{8,16},{16,24},{24,0},{1,9},{9,17},{17,25},{25,1},{2,10},{10... | collective-permute-start | bytes 172040 | tf_op jit(solution)/shard_map/ppermute | solution.py:280
  201.3 39.8 %collective-permute-start.17 = (bf16[64,3584]{1,0:T(8,128)(2,1)S(1)}, bf16[64,3584]{1,0:T(8,128)(2,1)S(1)}, u32[]{:S(2)}, u32[]{:S(2)}) collective-permute-start(bf16[64,3584]{1,0:T(8,128)(2,1)S(1)} %final_b.1), channel_id=1, source_target_pairs={{0,992},{32,0},{64,32},{96,64},{128,96},{160,128},{192,160},{224,1... | collective-permute-start | bytes 1376264 | tf_op jit(solution)/shard_map/ppermute | solution.py:280
  203.3 14.0 %collective-permute-start.4 = (f32[1,64]{1,0:T(1,128)S(1)}, f32[1,64]{1,0:T(1,128)S(1)}, u32[]{:S(2)}, u32[]{:S(2)}) collective-permute-start(f32[1,64]{1,0:T(1,128)S(1)} %bitcast.34), channel_id=1, source_target_pairs={{0,32},{32,64},{64,96},{96,128},{128,160},{160,192},{192,224},{224... | collective-permute-start | bytes 776 | tf_op jit(solution)/shard_map/ppermute | solution.py:280

commit v6 on v5

--- a/solution.py
+++ b/solution.py
@@ -172,9 +172,9 @@
     out_ref[...] = (cot_ref[...].astype(F32) + total).astype(BF16)
 
 
-def pack_f_kernel(experts, cap, at_ref, x_ref, route_ref, *out_refs):
+def pack_f_kernel(experts, cap, at_ref, x_ref, meta_ref, *out_refs):
     tokens = x_ref.shape[0]
-    route = route_ref[...]
+    route = meta_ref[0:1, :].astype(jnp.int32)
     slot = slots_of(route, experts)
     count = len(out_refs)
     m = iota((count * 2 * cap, tokens), 0)
@@ -235,12 +235,13 @@
     out_ref[...] = total.astype(BF16)
 
 
-def final_f_kernel(experts, cap, x_ref, route_ref, gate_ref, back_ref, out_ref):
+def final_f_kernel(experts, cap, x_ref, meta_ref, back_ref, out_ref):
     tokens = x_ref.shape[0]
     rows, half = back_ref.shape
-    route = route_ref[...]
+    meta = meta_ref[...]
+    route = meta[0:1, :].astype(jnp.int32)
     slot = column(slots_of(route, experts))
-    gate = column(gate_ref[...])
+    gate = column(meta[1:2, :])
     m = iota((tokens, rows), 1)
     table = (m // (4 * cap) == column(route)) & (m % cap == slot)
     low = (m % (2 * cap)) // cap == 0
@@ -337,8 +338,10 @@
 
     route_b, gate_b = bwd_route.reshape(1, tokens), bwd_gate.reshape(1, tokens)
     x = shift(fwd_in[0], 1)
-    route_f = shift(fwd_route.reshape(1, tokens), 1)
-    gate_f = shift(fwd_gate.reshape(1, tokens), 1)
+    meta = jnp.concatenate(
+        [fwd_route.reshape(1, tokens).astype(F32), fwd_gate.reshape(1, tokens)], axis=0
+    )
+    meta = shift(meta, 1)
     core = at[2:]
     rounds = jnp.minimum(jnp.sum((bwd_route < experts).astype(jnp.int32)), 1)
 
@@ -348,7 +351,6 @@
         [half],
         (cot, route_b, gate_b),
         2 * many * tokens * width,
-        earlier=(route_f,),
     )
     own_b = exchange(packed, cap)
 
@@ -356,7 +358,7 @@
         kernel(pack_f_kernel, experts, cap),
         "pack_f",
         [(2 * cap, width)] * (block // cap),
-        (at, x, route_f),
+        (at, x, meta),
         4 * block * tokens * width,
         earlier=(packed,),
     )
@@ -364,7 +366,8 @@
     here, away = call(
         kernel(pairs_kernel, cap), "pairs_f", [(block, width)] * 2, chunks, 4 * block * block * width
     )
-    blocks_f = (here, partner(here), mirror(away), opposite(away))
+    from_mirror = mirror(away)
+    blocks_f = (here, partner(here), from_mirror, partner(from_mirror))
 
     def chain_b(_, rows):
         mine, send = call(
@@ -422,7 +425,7 @@
         kernel(final_f_kernel, experts, cap),
         "final_f",
         [(tokens, width)],
-        (x, route_f, gate_f, back_f),
+        (x, meta, back_f),
         2 * many * tokens * width,
     )
     return out_f[None], out_b[None]

time: 243 us -> 254 us (1.045)
  the two profiles are of different devices: /device:TPU:145 before, /device:TPU:312 now
where the time goes in v6:
time: 254 us; the launch traced here: 253 us
  starting transfers between devices  128 us (50%)
  waiting for transfers between devices  96.3 us (38%)
  Pallas kernels  16.5 us (6%)
  blocking collectives  4.93 us (2%)
  local copies, waits for them, and re-layouts  3.1 us (1%)
    ppermute x17, waiting for transfers between devices, moved(): lax.ppermute(block, axis, [(i, to(i)) for i in range(lax.axis_size(axis))])  96.3 us
    ppermute x17, starting transfers between devices, moved(): lax.ppermute(block, axis, [(i, to(i)) for i in range(lax.axis_size(axis))])  84.5 us
    all_to_all x2, starting transfers between devices, exchange(): lax.all_to_all(blocks, ('x', 'zh'), split_axis=0, concat_axis=0, tiled=True)  43.8 us
    pallas_call x12, Pallas kernels, call(): pl.pallas_call(body, out_shape=out, in_specs=[SMEM if a.ndim == 1 else VM...  16.5 us
  transfers between devices with their start and end apart: 19, of which 7 were waited for; matrix products, arithmetic and copies ran while one was open for 0% of the time, Pallas kernels for 6%

profile of v6, /device:TPU:312, one launch (start us, length us, event | category | flops | bytes accessed | tf_op | source)
XLA Modules:
  0.0 252.9 jit_solution(1453167234311804325)
XLA Ops:
  0.6 0.7 convert_bitcast_fusion
  1.3 0.7 pad_maximum_fusion
  2.0 3.8 %collective-permute-start.3 = (f32[2,64]{1,0:T(2,128)S(1)}, f32[2,64]{1,0:T(2,128)S(1)}, u32[]{:S(2)}, u32[]{:S(2)}) collective-permute-start(f32[2,64]{1,0:T(2,128)S(1)} %pad_maximum_fusion), channel_id=1, source_target_pairs={{0,32},{32,64},{64,96},{96,128},{128,160},{160,192},{192,224},{224... | collective-permute-start | bytes 1544 | tf_op jit(solution)/shard_map/ppermute | solution.py:281
  5.8 3.8 %collective-permute-start.2 = (bf16[64,3584]{1,0:T(8,128)(2,1)}, bf16[64,3584]{1,0:T(8,128)(2,1)S(1)}, u32[]{:S(2)}, u32[]{:S(2)}) collective-permute-start(bf16[64,3584]{1,0:T(8,128)(2,1)} %bitcast.33), channel_id=1, source_target_pairs={{0,32},{32,64},{64,96},{96,128},{128,160},{160,192},{192,224},{224... | collective-permute-start | bytes 1376264 | tf_op jit(solution)/shard_map/ppermute | solution.py:281
  9.6 0.0 copy-start
  9.6 1.0 copy-done
  10.6 0.7 copy-done.2
  11.3 0.7 copy-done.4
  11.9 1.3 pack_b.1.refs_3_
  13.2 25.0 %all-to-all-start.1 = ((bf16[16,8,1792]{2,1,0:T(8,128)(2,1)}), bf16[16,8,1792]{2,1,0:T(8,128)(2,1)S(1)}, u32[]{:S(2)}, u32[]{:S(2)}) async-start(bf16[16,8,1792]{2,1,0:T(8,128)(2,1)} %bitcast.15), calls=%async_computation.1 | async-start | bytes 917504 | tf_op jit(solution)/shard_map/all_to_all | solution.py:306
  38.3 0.1 pad_add_fusion.refs_0_
  38.3 0.0 collective-permute-done.3.refs_2_.refs_1_
  38.4 0.0 collective-permute-done.2.refs_1_.refs_0_
  38.4 0.9 pack_f.1
  39.2 3.4 %collective-permute-start.4 = (bf16[8,3584]{1,0:T(8,128)(2,1)S(1)}, bf16[8,3584]{1,0:T(8,128)(2,1)S(1)}, u32[]{:S(2)}, u32[]{:S(2)}) collective-permute-start(bf16[8,3584]{1,0:T(8,128)(2,1)S(1)} %get-tuple-element.114), channel_id=1, source_target_pairs={{0,8},{8,16},{16,24},{24,0},{1,9},{9,17},{17,25},{25,1},{2,10},{10... | collective-permute-start | bytes 172040 | tf_op jit(solution)/shard_map/ppermute | solution.py:281
  42.6 4.6 %collective-permute-start.5 = (bf16[8,3584]{1,0:T(8,128)(2,1)S(1)}, bf16[8,3584]{1,0:T(8,128)(2,1)S(1)}, u32[]{:S(2)}, u32[]{:S(2)}) collective-permute-start(bf16[8,3584]{1,0:T(8,128)(2,1)S(1)} %get-tuple-element.115), channel_id=1, source_target_pairs={{0,16},{8,24},{16,0},{24,8},{1,17},{9,25},{17,1},{25,9},{2,18},{10... | collective-permute-start | bytes 172040 | tf_op jit(solution)/shard_map/ppermute | solution.py:281
  47.2 3.4 %collective-permute-start.6 = (bf16[8,3584]{1,0:T(8,128)(2,1)S(1)}, bf16[8,3584]{1,0:T(8,128)(2,1)S(1)}, u32[]{:S(2)}, u32[]{:S(2)}) collective-permute-start(bf16[8,3584]{1,0:T(8,128)(2,1)S(1)} %get-tuple-element.116), channel_id=1, source_target_pairs={{0,24},{8,0},{16,8},{24,16},{1,25},{9,1},{17,9},{25,17},{2,26},{10... | collective-permute-start | bytes 172040 | tf_op jit(solution)/shard_map/ppermute | solution.py:281
  50.6 0.0 collective-permute-done.4.refs_1_
  50.6 0.0 collective-permute-done.5.refs_2_
  50.6 2.7 %collective-permute-done.6.refs_3_ = bf16[8,3584]{1,0:T(8,128)(2,1)S(1)} collective-permute-done((bf16[8,3584]{1,0:T(8,128)(2,1)S(1)}, bf16[8,3584]{1,0:T(8,128)(2,1)S(1)}, u32[]{:S(2)}, u32[]{:S(2)}) %collective-permute-start.6) | collective-permute-done | bytes 57376 | tf_op jit(solution)/shard_map/ppermute | solution.py:281
  53.3 0.2 pairs_f.1
  53.5 12.1 %collective-permute-start.8 = (bf16[16,3584]{1,0:T(8,128)(2,1)S(1)}, bf16[16,3584]{1,0:T(8,128)(2,1)S(1)}, u32[]{:S(2)}, u32[]{:S(2)}) collective-permute-start(bf16[16,3584]{1,0:T(8,128)(2,1)S(1)} %get-tuple-element.118), channel_id=1, source_target_pairs={{0,6},{2,4},{4,2},{6,0},{1,7},{3,5},{5,3},{7,1},{8,14},{10,12},{12... | collective-permute-start | bytes 344072 | tf_op jit(solution)/shard_map/ppermute | solution.py:281
  65.6 0.6 fusion
  66.8 2.5 collective-permute-start.7
  69.3 31.1 %collective-permute-done.8 = bf16[16,3584]{1,0:T(8,128)(2,1)S(1)} collective-permute-done((bf16[16,3584]{1,0:T(8,128)(2,1)S(1)}, bf16[16,3584]{1,0:T(8,128)(2,1)S(1)}, u32[]{:S(2)}, u32[]{:S(2)}) %collective-permute-start.8) | collective-permute-done | bytes 114720 | tf_op jit(solution)/shard_map/ppermute | solution.py:281
  100.4 1.9 collective-permute-start.9
  102.3 0.0 all-to-all-done.1
  102.3 12.0 %while.27 = (s32[]{:T(128)}, bf16[128,1792]{1,0:T(8,128)(2,1)S(1)}, s32[]{:T(128)}, bf16[1,1,128,512]{3,2,1,0:T(8,128)(2,1)S(1)}, s32[1]{0:T(128)}, /*index=5*/b...) while((s32[]{:T(128)}, bf16[128,1792]{1,0:T(8,128)(2,1)S(1)}, s32[]{:T(128)}, ...), condition=%wide.region_4.0_spmd, body=%wide.region_3.0_spmd.sunk | while | flops 705560576 | bytes 12058753 | solution.py:383
  102.3 2.5 all_gather.9.refs_1_
  104.8 5.7 %expert_b.1 = (bf16[128,1792]{1,0:T(8,128)(2,1)S(1)}, bf16[128,1792]{1,0:T(8,128)(2,1)S(1)}) custom-call(s32[1]{0:T(128)} %get-tuple-element.330.refs_0_, bf16[256,1792]{1,0:T(8,128)(2,1)S(1)} %all_gather.9.refs_1_, bf16[256,3584]{1,0:T(8,128)(2,1)} %get-tuple-element.331.refs_2_, bf16[128,512]{1,0:T(8,128)(2,1)S(1)} %bitcast.29, ...), custom_call_target="tpu_custom_call" | custom-call | flops 704643072 | bytes 7471108 | tf_op jit(solution)/shard_map/while/body/expert_b/pallas_call | solution.py:265
  110.5 2.0 collective-permute-start.1
  112.6 1.7 collective-permute-done.1
  114.2 0.1 add_convert_fusion.2
  114.4 1.0 split_b.1
  115.3 12.6 %collective-permute-start.10 = (bf16[16,3584]{1,0:T(8,128)(2,1)S(1)}, bf16[16,3584]{1,0:T(8,128)(2,1)S(1)}, u32[]{:S(2)}, u32[]{:S(2)}) collective-permute-start(bf16[16,3584]{1,0:T(8,128)(2,1)S(1)} %get-tuple-element.125), channel_id=1, source_target_pairs={{0,2},{2,0},{4,6},{6,4},{1,3},{3,1},{5,7},{7,5},{8,10},{10,8},{12,... | collective-permute-start | bytes 344072 | tf_op jit(solution)/shard_map/ppermute | solution.py:281
  128.0 4.3 %collective-permute-start.11 = (bf16[16,3584]{1,0:T(8,128)(2,1)S(1)}, bf16[16,3584]{1,0:T(8,128)(2,1)S(1)}, u32[]{:S(2)}, u32[]{:S(2)}) collective-permute-start(bf16[16,3584]{1,0:T(8,128)(2,1)S(1)} %get-tuple-element.126), channel_id=1, source_target_pairs={{0,6},{2,4},{4,2},{6,0},{1,7},{3,5},{5,3},{7,1},{8,14},{10,12},{12... | collective-permute-start | bytes 344072 | tf_op jit(solution)/shard_map/ppermute | solution.py:281
  132.2 9.7 %collective-permute-start.12 = (bf16[16,3584]{1,0:T(8,128)(2,1)S(1)}, bf16[16,3584]{1,0:T(8,128)(2,1)S(1)}, u32[]{:S(2)}, u32[]{:S(2)}) collective-permute-start(bf16[16,3584]{1,0:T(8,128)(2,1)S(1)} %get-tuple-element.127), channel_id=1, source_target_pairs={{0,4},{2,6},{4,0},{6,2},{1,5},{3,7},{5,1},{7,3},{8,12},{10,14},{12... | collective-permute-start | bytes 344072 | tf_op jit(solution)/shard_map/ppermute | solution.py:281
  142.0 0.0 collective-permute-done.7
  142.0 0.0 collective-permute-done.9
  142.0 9.5 %while.26 = (s32[]{:T(128)}, bf16[16,3584]{1,0:T(8,128)(2,1)S(1)}, bf16[16,3584]{1,0:T(8,128)(2,1)S(1)}, bf16[16,3584]{1,0:T(8,128)(2,1)S(1)}, bf16[16,3584]{1,0...) while((s32[]{:T(128)}, bf16[16,3584]{1,0:T(8,128)(2,1)S(1)}, ...), condition=%wide.region_2.0_spmd, body=%wide.region_1.0_spmd.sunk | while | flops 705101824 | bytes 12845201 | solution.py:402
  142.1 2.5 all_gather.8.refs_1_
  144.5 3.1 %expert_f.1 = (bf16[64,3584]{1,0:T(8,128)(2,1)S(1)}, bf16[64,3584]{1,0:T(8,128)(2,1)S(1)}) custom-call(s32[1]{0:T(128)} %get-tuple-element.306.refs_0_, bf16[128,3584]{1,0:T(8,128)(2,1)S(1)} %all_gather.8.refs_1_, bf16[3584,512]{1,0:T(8,128)(2,1)} %get-tuple-element.307.refs_2_, bf16[256,3584]{1,0:T(8,128)(2,1)} %get-tuple-element.308.refs_3_), custom_call_target="tpu_custom_call" | custom-call | flops 704643072 | bytes 7340036 | tf_op jit(solution)/shard_map/while/body/expert_f/pallas_call | solution.py:265
  147.7 2.0 collective-permute-start
  149.7 1.7 collective-permute-done.refs_1_
  151.4 0.1 add_f.1
  151.5 1.7 spread_f.1
  153.2 18.7 %all-to-all-start = ((bf16[16,8,1792]{2,1,0:T(8,128)(2,1)}), bf16[16,8,1792]{2,1,0:T(8,128)(2,1)S(1)}, u32[]{:S(2)}, u32[]{:S(2)}) async-start(bf16[16,8,1792]{2,1,0:T(8,128)(2,1)} %bitcast.12), calls=%async_computation | async-start | bytes 917504 | tf_op jit(solution)/shard_map/all_to_all | solution.py:306
  172.0 0.0 collective-permute-done.10.refs_1_
  172.0 0.0 collective-permute-done.11.refs_2_
  172.0 0.0 collective-permute-done.12.refs_3_
  172.0 0.0 copy-start.1
  172.0 0.2 merge_b.1
  172.2 4.6 %collective-permute-start.13 = (bf16[8,3584]{1,0:T(8,128)(2,1)S(1)}, bf16[8,3584]{1,0:T(8,128)(2,1)S(1)}, u32[]{:S(2)}, u32[]{:S(2)}) collective-permute-start(bf16[8,3584]{1,0:T(8,128)(2,1)S(1)} %get-tuple-element.129), channel_id=1, source_target_pairs={{0,24},{8,0},{16,8},{24,16},{1,25},{9,1},{17,9},{25,17},{2,26},{10... | collective-permute-start | bytes 172040 | tf_op jit(solution)/shard_map/ppermute | solution.py:281
  176.8 2.8 %collective-permute-start.14 = (bf16[8,3584]{1,0:T(8,128)(2,1)S(1)}, bf16[8,3584]{1,0:T(8,128)(2,1)S(1)}, u32[]{:S(2)}, u32[]{:S(2)}) collective-permute-start(bf16[8,3584]{1,0:T(8,128)(2,1)S(1)} %get-tuple-element.130), channel_id=1, source_target_pairs={{0,16},{8,24},{16,0},{24,8},{1,17},{9,25},{17,1},{25,9},{2,18},{10... | collective-permute-start | bytes 172040 | tf_op jit(solution)/shard_map/ppermute | solution.py:281
  179.6 2.8 %collective-permute-start.15 = (bf16[8,3584]{1,0:T(8,128)(2,1)S(1)}, bf16[8,3584]{1,0:T(8,128)(2,1)S(1)}, u32[]{:S(2)}, u32[]{:S(2)}) collective-permute-start(bf16[8,3584]{1,0:T(8,128)(2,1)S(1)} %get-tuple-element.131), channel_id=1, source_target_pairs={{0,8},{8,16},{16,24},{24,0},{1,9},{9,17},{17,25},{25,1},{2,10},{10... | collective-permute-start | bytes 172040 | tf_op jit(solution)/shard_map/ppermute | solution.py:281
  182.4 0.0 collective-permute-done.13.refs_4_
  182.4 2.4 collective-permute-done.14.refs_5_
  184.7 2.1 collective-permute-done.15.refs_6_
  186.9 1.0 final_b.1
  187.9 8.3 %collective-permute-start.16 = (bf16[64,3584]{1,0:T(8,128)(2,1)S(1)}, bf16[64,3584]{1,0:T(8,128)(2,1)S(1)}, u32[]{:S(2)}, u32[]{:S(2)}) collective-permute-start(bf16[64,3584]{1,0:T(8,128)(2,1)S(1)} %final_b.1), channel_id=1, source_target_pairs={{0,992},{32,0},{64,32},{96,64},{128,96},{160,128},{192,160},{224,1... | collective-permute-start | bytes 1376264 | tf_op jit(solution)/shard_map/ppermute | solution.py:281
  196.2 54.6 %collective-permute-done.16 = bf16[64,3584]{1,0:T(8,128)(2,1)S(1)} collective-permute-done((bf16[64,3584]{1,0:T(8,128)(2,1)S(1)}, bf16[64,3584]{1,0:T(8,128)(2,1)S(1)}, u32[]{:S(2)}, u32[]{:S(2)}) %collective-permute-start.16) | collective-permute-done | bytes 458784 | tf_op jit(solution)/shard_map/ppermute | solution.py:281
  250.8 0.0 all-to-all-done
  250.8 1.3 final_f.1
  252.1 0.8 copy.34
  (8 shorter events, 0.0 us)
Async XLA Ops:
  2.0 36.4 %collective-permute-start.3 = (f32[2,64]{1,0:T(2,128)S(1)}, f32[2,64]{1,0:T(2,128)S(1)}, u32[]{:S(2)}, u32[]{:S(2)}) collective-permute-start(f32[2,64]{1,0:T(2,128)S(1)} %pad_maximum_fusion), channel_id=1, source_target_pairs={{0,32},{32,64},{64,96},{96,128},{128,160},{160,192},{192,224},{224... | collective-permute-start | bytes 1544 | tf_op jit(solution)/shard_map/ppermute | solution.py:281
  5.8 32.6 %collective-permute-start.2 = (bf16[64,3584]{1,0:T(8,128)(2,1)}, bf16[64,3584]{1,0:T(8,128)(2,1)S(1)}, u32[]{:S(2)}, u32[]{:S(2)}) collective-permute-start(bf16[64,3584]{1,0:T(8,128)(2,1)} %bitcast.33), channel_id=1, source_target_pairs={{0,32},{32,64},{64,96},{96,128},{128,160},{160,192},{192,224},{224... | collective-permute-start | bytes 1376264 | tf_op jit(solution)/shard_map/ppermute | solution.py:281
  9.6 1.0 copy-start
  10.6 0.7 copy-start.2
  11.3 0.7 copy-start.4
  13.2 89.1 %all-to-all-start.1 = ((bf16[16,8,1792]{2,1,0:T(8,128)(2,1)}), bf16[16,8,1792]{2,1,0:T(8,128)(2,1)S(1)}, u32[]{:S(2)}, u32[]{:S(2)}) async-start(bf16[16,8,1792]{2,1,0:T(8,128)(2,1)} %bitcast.15), calls=%async_computation.1 | async-start | bytes 917504 | tf_op jit(solution)/shard_map/all_to_all | solution.py:306
  38.3 27.2 %copy-start.3 = (s32[1,64,1]{1,2,0:T(1,128)S(1)}, s32[1,64,1]{1,2,0:T(1,128)}, u32[]{:S(2)}) copy-start(s32[1,64,1]{1,2,0:T(1,128)} %param.17) | copy-start | bytes 772
  38.3 63.9 %copy-start.5 = (bf16[1,1,128,512]{3,2,1,0:T(8,128)(2,1)S(1)}, bf16[1,1,128,512]{3,2,1,0:T(8,128)(2,1)}, u32[]{:S(2)}) copy-start(bf16[1,1,128,512]{3,2,1,0:T(8,128)(2,1)} %param.19) | copy-start | bytes 393220
  39.2 11.4 %collective-permute-start.4 = (bf16[8,3584]{1,0:T(8,128)(2,1)S(1)}, bf16[8,3584]{1,0:T(8,128)(2,1)S(1)}, u32[]{:S(2)}, u32[]{:S(2)}) collective-permute-start(bf16[8,3584]{1,0:T(8,128)(2,1)S(1)} %get-tuple-element.114), channel_id=1, source_target_pairs={{0,8},{8,16},{16,24},{24,0},{1,9},{9,17},{17,25},{25,1},{2,10},{10... | collective-permute-start | bytes 172040 | tf_op jit(solution)/shard_map/ppermute | solution.py:281
  42.6 8.0 %collective-permute-start.5 = (bf16[8,3584]{1,0:T(8,128)(2,1)S(1)}, bf16[8,3584]{1,0:T(8,128)(2,1)S(1)}, u32[]{:S(2)}, u32[]{:S(2)}) collective-permute-start(bf16[8,3584]{1,0:T(8,128)(2,1)S(1)} %get-tuple-element.115), channel_id=1, source_target_pairs={{0,16},{8,24},{16,0},{24,8},{1,17},{9,25},{17,1},{25,9},{2,18},{10... | collective-permute-start | bytes 172040 | tf_op jit(solution)/shard_map/ppermute | solution.py:281
  47.2 6.1 %collective-permute-start.6 = (bf16[8,3584]{1,0:T(8,128)(2,1)S(1)}, bf16[8,3584]{1,0:T(8,128)(2,1)S(1)}, u32[]{:S(2)}, u32[]{:S(2)}) collective-permute-start(bf16[8,3584]{1,0:T(8,128)(2,1)S(1)} %get-tuple-element.116), channel_id=1, source_target_pairs={{0,24},{8,0},{16,8},{24,16},{1,25},{9,1},{17,9},{25,17},{2,26},{10... | collective-permute-start | bytes 172040 | tf_op jit(solution)/shard_map/ppermute | solution.py:281
  53.5 46.9 %collective-permute-start.8 = (bf16[16,3584]{1,0:T(8,128)(2,1)S(1)}, bf16[16,3584]{1,0:T(8,128)(2,1)S(1)}, u32[]{:S(2)}, u32[]{:S(2)}) collective-permute-start(bf16[16,3584]{1,0:T(8,128)(2,1)S(1)} %get-tuple-element.118), channel_id=1, source_target_pairs={{0,6},{2,4},{4,2},{6,0},{1,7},{3,5},{5,3},{7,1},{8,14},{10,12},{12... | collective-permute-start | bytes 344072 | tf_op jit(solution)/shard_map/ppermute | solution.py:281
  66.8 75.2 %collective-permute-start.7 = (bf16[16,3584]{1,0:T(8,128)(2,1)S(1)}, bf16[16,3584]{1,0:T(8,128)(2,1)S(1)}, u32[]{:S(2)}, u32[]{:S(2)}) collective-permute-start(bf16[16,3584]{1,0:T(8,128)(2,1)S(1)} %get-tuple-element.281), channel_id=1, source_target_pairs={{0,2},{2,0},{4,6},{6,4},{1,3},{3,1},{5,7},{7,5},{8,10},{10,8},{12,... | collective-permute-start | bytes 344072 | tf_op jit(solution)/shard_map/ppermute | solution.py:281
  100.4 41.6 %collective-permute-start.9 = (bf16[16,3584]{1,0:T(8,128)(2,1)S(1)}, bf16[16,3584]{1,0:T(8,128)(2,1)S(1)}, u32[]{:S(2)}, u32[]{:S(2)}) collective-permute-start(bf16[16,3584]{1,0:T(8,128)(2,1)S(1)} %collective-permute-done.8), channel_id=1, source_target_pairs={{0,2},{2,0},{4,6},{6,4},{1,3},{3,1},{5,7},{7,5},{8,10},{10,8},{12,... | collective-permute-start | bytes 344072 | tf_op jit(solution)/shard_map/ppermute | solution.py:281
  110.5 3.7 %collective-permute-start.1 = (bf16[128,1792]{1,0:T(8,128)(2,1)S(1)}, bf16[128,1792]{1,0:T(8,128)(2,1)S(1)}, u32[]{:S(2)}, u32[]{:S(2)}) collective-permute-start(bf16[128,1792]{1,0:T(8,128)(2,1)S(1)} %get-tuple-element.278), channel_id=1, source_target_pairs={{0,1},{1,0},{2,3},{3,2},{4,5},{5,4},{6,7},{7,6},{8,9},{9,8},{10,11... | collective-permute-start | bytes 1376264 | tf_op jit(solution)/shard_map/while/body/ppermute | solution.py:281
  115.3 56.6 %collective-permute-start.10 = (bf16[16,3584]{1,0:T(8,128)(2,1)S(1)}, bf16[16,3584]{1,0:T(8,128)(2,1)S(1)}, u32[]{:S(2)}, u32[]{:S(2)}) collective-permute-start(bf16[16,3584]{1,0:T(8,128)(2,1)S(1)} %get-tuple-element.125), channel_id=1, source_target_pairs={{0,2},{2,0},{4,6},{6,4},{1,3},{3,1},{5,7},{7,5},{8,10},{10,8},{12,... | collective-permute-start | bytes 344072 | tf_op jit(solution)/shard_map/ppermute | solution.py:281
  128.0 44.0 %collective-permute-start.11 = (bf16[16,3584]{1,0:T(8,128)(2,1)S(1)}, bf16[16,3584]{1,0:T(8,128)(2,1)S(1)}, u32[]{:S(2)}, u32[]{:S(2)}) collective-permute-start(bf16[16,3584]{1,0:T(8,128)(2,1)S(1)} %get-tuple-element.126), channel_id=1, source_target_pairs={{0,6},{2,4},{4,2},{6,0},{1,7},{3,5},{5,3},{7,1},{8,14},{10,12},{12... | collective-permute-start | bytes 344072 | tf_op jit(solution)/shard_map/ppermute | solution.py:281
  132.2 39.7 %collective-permute-start.12 = (bf16[16,3584]{1,0:T(8,128)(2,1)S(1)}, bf16[16,3584]{1,0:T(8,128)(2,1)S(1)}, u32[]{:S(2)}, u32[]{:S(2)}) collective-permute-start(bf16[16,3584]{1,0:T(8,128)(2,1)S(1)} %get-tuple-element.127), channel_id=1, source_target_pairs={{0,4},{2,6},{4,0},{6,2},{1,5},{3,7},{5,1},{7,3},{8,12},{10,14},{12... | collective-permute-start | bytes 344072 | tf_op jit(solution)/shard_map/ppermute | solution.py:281
  147.7 3.7 %collective-permute-start = (bf16[64,3584]{1,0:T(8,128)(2,1)S(1)}, bf16[64,3584]{1,0:T(8,128)(2,1)S(1)}, u32[]{:S(2)}, u32[]{:S(2)}) collective-permute-start(bf16[64,3584]{1,0:T(8,128)(2,1)S(1)} %get-tuple-element.266), channel_id=1, source_target_pairs={{0,1},{1,0},{2,3},{3,2},{4,5},{5,4},{6,7},{7,6},{8,9},{9,8},{10,11... | collective-permute-start | bytes 1376264 | tf_op jit(solution)/shard_map/while/body/ppermute | solution.py:281
  153.2 97.6 %all-to-all-start = ((bf16[16,8,1792]{2,1,0:T(8,128)(2,1)}), bf16[16,8,1792]{2,1,0:T(8,128)(2,1)S(1)}, u32[]{:S(2)}, u32[]{:S(2)}) async-start(bf16[16,8,1792]{2,1,0:T(8,128)(2,1)} %bitcast.12), calls=%async_computation | async-start | bytes 917504 | tf_op jit(solution)/shard_map/all_to_all | solution.py:306
  172.0 14.9 %copy-start.1 = (bf16[1,64,3584]{2,1,0:T(8,128)(2,1)S(1)}, bf16[1,64,3584]{2,1,0:T(8,128)(2,1)}, u32[]{:S(2)}) copy-start(bf16[1,64,3584]{2,1,0:T(8,128)(2,1)} %param.16) | copy-start | bytes 1376260
  172.2 10.1 %collective-permute-start.13 = (bf16[8,3584]{1,0:T(8,128)(2,1)S(1)}, bf16[8,3584]{1,0:T(8,128)(2,1)S(1)}, u32[]{:S(2)}, u32[]{:S(2)}) collective-permute-start(bf16[8,3584]{1,0:T(8,128)(2,1)S(1)} %get-tuple-element.129), channel_id=1, source_target_pairs={{0,24},{8,0},{16,8},{24,16},{1,25},{9,1},{17,9},{25,17},{2,26},{10... | collective-permute-start | bytes 172040 | tf_op jit(solution)/shard_map/ppermute | solution.py:281
  176.8 7.9 %collective-permute-start.14 = (bf16[8,3584]{1,0:T(8,128)(2,1)S(1)}, bf16[8,3584]{1,0:T(8,128)(2,1)S(1)}, u32[]{:S(2)}, u32[]{:S(2)}) collective-permute-start(bf16[8,3584]{1,0:T(8,128)(2,1)S(1)} %get-tuple-element.130), channel_id=1, source_target_pairs={{0,16},{8,24},{16,0},{24,8},{1,17},{9,25},{17,1},{25,9},{2,18},{10... | collective-permute-start | bytes 172040 | tf_op jit(solution)/shard_map/ppermute | solution.py:281
  179.6 7.3 %collective-permute-start.15 = (bf16[8,3584]{1,0:T(8,128)(2,1)S(1)}, bf16[8,3584]{1,0:T(8,128)(2,1)S(1)}, u32[]{:S(2)}, u32[]{:S(2)}) collective-permute-start(bf16[8,3584]{1,0:T(8,128)(2,1)S(1)} %get-tuple-element.131), channel_id=1, source_target_pairs={{0,8},{8,16},{16,24},{24,0},{1,9},{9,17},{17,25},{25,1},{2,10},{10... | collective-permute-start | bytes 172040 | tf_op jit(solution)/shard_map/ppermute | solution.py:281
  187.9 62.9 %collective-permute-start.16 = (bf16[64,3584]{1,0:T(8,128)(2,1)S(1)}, bf16[64,3584]{1,0:T(8,128)(2,1)S(1)}, u32[]{:S(2)}, u32[]{:S(2)}) collective-permute-start(bf16[64,3584]{1,0:T(8,128)(2,1)S(1)} %final_b.1), channel_id=1, source_target_pairs={{0,992},{32,0},{64,32},{96,64},{128,96},{160,128},{192,160},{224,1... | collective-permute-start | bytes 1376264 | tf_op jit(solution)/shard_map/ppermute | solution.py:281

commit v7 on v6

--- a/solution.py
+++ b/solution.py
@@ -366,8 +366,7 @@
     here, away = call(
         kernel(pairs_kernel, cap), "pairs_f", [(block, width)] * 2, chunks, 4 * block * block * width
     )
-    from_mirror = mirror(away)
-    blocks_f = (here, partner(here), from_mirror, partner(from_mirror))
+    blocks_f = (here, partner(here), mirror(away), opposite(away))
 
     def chain_b(_, rows):
         mine, send = call(

time: 254 us -> 245 us (0.965)
  the two profiles are of different devices: /device:TPU:312 before, /device:TPU:144 now
where the time goes in v7:
time: 245 us; the launch traced here: 244 us
  starting transfers between devices  152 us (62%)
  waiting for transfers between devices  63.6 us (26%)
  Pallas kernels  16.5 us (7%)
  blocking collectives  4.91 us (2%)
  local copies, waits for them, and re-layouts  3.1 us (1%)
    ppermute x17, starting transfers between devices, moved(): lax.ppermute(block, axis, [(i, to(i)) for i in range(lax.axis_size(axis))])  112 us
    all_to_all x2, starting transfers between devices, exchange(): lax.all_to_all(blocks, ('x', 'zh'), split_axis=0, concat_axis=0, tiled=True)  40.8 us
    all_to_all x2, waiting for transfers between devices, exchange(): lax.all_to_all(blocks, ('x', 'zh'), split_axis=0, concat_axis=0, tiled=True)  36.9 us
    ppermute x17, waiting for transfers between devices, moved(): lax.ppermute(block, axis, [(i, to(i)) for i in range(lax.axis_size(axis))])  26.7 us
    pallas_call x12, Pallas kernels, call(): pl.pallas_call(body, out_shape=out, in_specs=[SMEM if a.ndim == 1 else VM...  16.5 us
    all_gather x2, blocking collectives, both_cores(): return lax.all_gather(block, 'c', axis=0, tiled=True)  4.91 us
  transfers between devices with their start and end apart: 19, of which 8 were waited for; matrix products, arithmetic and copies ran while one was open for 0% of the time, Pallas kernels for 6%

profile of v7, /device:TPU:144, one launch (start us, length us, event | category | flops | bytes accessed | tf_op | source)
XLA Modules:
  0.0 244.3 jit_solution(13540483084122612022)
XLA Ops:
  0.6 0.7 convert_bitcast_fusion
  1.3 0.7 pad_maximum_fusion
  2.0 3.8 %collective-permute-start.3 = (f32[2,64]{1,0:T(2,128)S(1)}, f32[2,64]{1,0:T(2,128)S(1)}, u32[]{:S(2)}, u32[]{:S(2)}) collective-permute-start(f32[2,64]{1,0:T(2,128)S(1)} %pad_maximum_fusion), channel_id=1, source_target_pairs={{0,32},{32,64},{64,96},{96,128},{128,160},{160,192},{192,224},{224... | collective-permute-start | bytes 1544 | tf_op jit(solution)/shard_map/ppermute | solution.py:281
  5.8 3.8 %collective-permute-start.2 = (bf16[64,3584]{1,0:T(8,128)(2,1)}, bf16[64,3584]{1,0:T(8,128)(2,1)S(1)}, u32[]{:S(2)}, u32[]{:S(2)}) collective-permute-start(bf16[64,3584]{1,0:T(8,128)(2,1)} %bitcast.34), channel_id=1, source_target_pairs={{0,32},{32,64},{64,96},{96,128},{128,160},{160,192},{192,224},{224... | collective-permute-start | bytes 1376264 | tf_op jit(solution)/shard_map/ppermute | solution.py:281
  9.6 0.0 copy-start
  9.6 1.0 copy-done
  10.6 0.7 copy-done.2
  11.3 0.7 copy-done.4
  11.9 1.3 pack_b.1.refs_3_
  13.2 24.3 %all-to-all-start.1 = ((bf16[16,8,1792]{2,1,0:T(8,128)(2,1)}), bf16[16,8,1792]{2,1,0:T(8,128)(2,1)S(1)}, u32[]{:S(2)}, u32[]{:S(2)}) async-start(bf16[16,8,1792]{2,1,0:T(8,128)(2,1)} %bitcast.15), calls=%async_computation.1 | async-start | bytes 917504 | tf_op jit(solution)/shard_map/all_to_all | solution.py:306
  37.5 0.1 pad_add_fusion.refs_0_
  37.6 0.0 collective-permute-done.3.refs_2_.refs_1_
  37.6 0.0 collective-permute-done.2.refs_1_.refs_0_
  37.6 0.9 pack_f.1
  38.5 3.8 %collective-permute-start.4 = (bf16[8,3584]{1,0:T(8,128)(2,1)S(1)}, bf16[8,3584]{1,0:T(8,128)(2,1)S(1)}, u32[]{:S(2)}, u32[]{:S(2)}) collective-permute-start(bf16[8,3584]{1,0:T(8,128)(2,1)S(1)} %get-tuple-element.114), channel_id=1, source_target_pairs={{0,8},{8,16},{16,24},{24,0},{1,9},{9,17},{17,25},{25,1},{2,10},{10... | collective-permute-start | bytes 172040 | tf_op jit(solution)/shard_map/ppermute | solution.py:281
  42.4 4.6 %collective-permute-start.5 = (bf16[8,3584]{1,0:T(8,128)(2,1)S(1)}, bf16[8,3584]{1,0:T(8,128)(2,1)S(1)}, u32[]{:S(2)}, u32[]{:S(2)}) collective-permute-start(bf16[8,3584]{1,0:T(8,128)(2,1)S(1)} %get-tuple-element.115), channel_id=1, source_target_pairs={{0,16},{8,24},{16,0},{24,8},{1,17},{9,25},{17,1},{25,9},{2,18},{10... | collective-permute-start | bytes 172040 | tf_op jit(solution)/shard_map/ppermute | solution.py:281
  46.9 3.4 %collective-permute-start.6 = (bf16[8,3584]{1,0:T(8,128)(2,1)S(1)}, bf16[8,3584]{1,0:T(8,128)(2,1)S(1)}, u32[]{:S(2)}, u32[]{:S(2)}) collective-permute-start(bf16[8,3584]{1,0:T(8,128)(2,1)S(1)} %get-tuple-element.116), channel_id=1, source_target_pairs={{0,24},{8,0},{16,8},{24,16},{1,25},{9,1},{17,9},{25,17},{2,26},{10... | collective-permute-start | bytes 172040 | tf_op jit(solution)/shard_map/ppermute | solution.py:281
  50.3 0.6 fusion
  51.5 0.0 collective-permute-done.4.refs_1_
  51.5 0.0 collective-permute-done.5.refs_2_
  51.5 1.5 collective-permute-done.6.refs_3_
  53.0 0.2 pairs_f.1
  53.2 22.1 %collective-permute-start.9 = (bf16[16,3584]{1,0:T(8,128)(2,1)S(1)}, bf16[16,3584]{1,0:T(8,128)(2,1)S(1)}, u32[]{:S(2)}, u32[]{:S(2)}) collective-permute-start(bf16[16,3584]{1,0:T(8,128)(2,1)S(1)} %get-tuple-element.118), channel_id=1, source_target_pairs={{0,4},{2,6},{4,0},{6,2},{1,5},{3,7},{5,1},{7,3},{8,12},{10,14},{12... | collective-permute-start | bytes 344072 | tf_op jit(solution)/shard_map/ppermute | solution.py:281
  75.3 2.1 collective-permute-start.8
  77.4 2.5 %collective-permute-start.7 = (bf16[16,3584]{1,0:T(8,128)(2,1)S(1)}, bf16[16,3584]{1,0:T(8,128)(2,1)S(1)}, u32[]{:S(2)}, u32[]{:S(2)}) collective-permute-start(bf16[16,3584]{1,0:T(8,128)(2,1)S(1)} %get-tuple-element.281), channel_id=1, source_target_pairs={{0,2},{2,0},{4,6},{6,4},{1,3},{3,1},{5,7},{7,5},{8,10},{10,8},{12,... | collective-permute-start | bytes 344072 | tf_op jit(solution)/shard_map/ppermute | solution.py:281
  79.9 21.1 %all-to-all-done.1 = bf16[16,8,1792]{2,1,0:T(8,128)(2,1)S(1)} async-done(((bf16[16,8,1792]{2,1,0:T(8,128)(2,1)}), bf16[16,8,1792]{2,1,0:T(8,128)(2,1)S(1)}, u32[]{:S(2)}, u32[]{:S(2)}) %all-to-all-start.1) | async-done | bytes 458784 | tf_op jit(solution)/shard_map/all_to_all | solution.py:306
  100.9 12.0 %while.27 = (s32[]{:T(128)}, bf16[128,1792]{1,0:T(8,128)(2,1)S(1)}, s32[]{:T(128)}, bf16[1,1,128,512]{3,2,1,0:T(8,128)(2,1)S(1)}, s32[1]{0:T(128)}, /*index=5*/b...) while((s32[]{:T(128)}, bf16[128,1792]{1,0:T(8,128)(2,1)S(1)}, s32[]{:T(128)}, ...), condition=%wide.region_4.0_spmd, body=%wide.region_3.0_spmd.sunk | while | flops 705560576 | bytes 12058753 | solution.py:382
  100.9 2.5 %all_gather.9.refs_1_ = bf16[256,1792]{1,0:T(8,128)(2,1)S(1)} all-gather(bf16[128,1792]{1,0:T(8,128)(2,1)S(1)} %get-tuple-element.319), channel_id=1, replica_groups=mesh['pp'=32,'x'=4,'zh'=4,'c'=2] {'c'}, dimensions={0}, use_global_device_ids=true | all-gather | bytes 1376256 | tf_op jit(solution)/shard_map/while/body/all_gather | solution.py:285
  103.4 5.7 %expert_b.1 = (bf16[128,1792]{1,0:T(8,128)(2,1)S(1)}, bf16[128,1792]{1,0:T(8,128)(2,1)S(1)}) custom-call(s32[1]{0:T(128)} %get-tuple-element.330.refs_0_, bf16[256,1792]{1,0:T(8,128)(2,1)S(1)} %all_gather.9.refs_1_, bf16[256,3584]{1,0:T(8,128)(2,1)} %get-tuple-element.331.refs_2_, bf16[128,512]{1,0:T(8,128)(2,1)S(1)} %bitcast.30, ...), custom_call_target="tpu_custom_call" | custom-call | flops 704643072 | bytes 7471108 | tf_op jit(solution)/shard_map/while/body/expert_b/pallas_call | solution.py:265
  109.1 2.0 collective-permute-start.1
  111.2 1.7 collective-permute-done.1
  112.8 0.1 add_convert_fusion.2
  113.0 1.0 split_b.1
  113.9 35.0 %collective-permute-start.10 = (bf16[16,3584]{1,0:T(8,128)(2,1)S(1)}, bf16[16,3584]{1,0:T(8,128)(2,1)S(1)}, u32[]{:S(2)}, u32[]{:S(2)}) collective-permute-start(bf16[16,3584]{1,0:T(8,128)(2,1)S(1)} %get-tuple-element.125), channel_id=1, source_target_pairs={{0,2},{2,0},{4,6},{6,4},{1,3},{3,1},{5,7},{7,5},{8,10},{10,8},{12,... | collective-permute-start | bytes 344072 | tf_op jit(solution)/shard_map/ppermute | solution.py:281
  148.9 1.9 collective-permute-start.11
  150.8 0.0 collective-permute-done.7
  150.9 12.1 %collective-permute-start.12 = (bf16[16,3584]{1,0:T(8,128)(2,1)S(1)}, bf16[16,3584]{1,0:T(8,128)(2,1)S(1)}, u32[]{:S(2)}, u32[]{:S(2)}) collective-permute-start(bf16[16,3584]{1,0:T(8,128)(2,1)S(1)} %get-tuple-element.127), channel_id=1, source_target_pairs={{0,4},{2,6},{4,0},{6,2},{1,5},{3,7},{5,1},{7,3},{8,12},{10,14},{12... | collective-permute-start | bytes 344072 | tf_op jit(solution)/shard_map/ppermute | solution.py:281
  162.9 0.0 collective-permute-done.9
  163.0 0.0 collective-permute-done.8
  163.0 9.5 %while.26 = (s32[]{:T(128)}, bf16[16,3584]{1,0:T(8,128)(2,1)S(1)}, bf16[16,3584]{1,0:T(8,128)(2,1)S(1)}, bf16[16,3584]{1,0:T(8,128)(2,1)S(1)}, bf16[16,3584]{1,0...) while((s32[]{:T(128)}, bf16[16,3584]{1,0:T(8,128)(2,1)S(1)}, ...), condition=%wide.region_2.0_spmd, body=%wide.region_1.0_spmd.sunk | while | flops 705101824 | bytes 12845201 | solution.py:401
  163.0 2.5 %all_gather.8.refs_1_ = bf16[128,3584]{1,0:T(8,128)(2,1)S(1)} all-gather(bf16[64,3584]{1,0:T(8,128)(2,1)S(1)} %join_f.1), channel_id=1, replica_groups=mesh['pp'=32,'x'=4,'zh'=4,'c'=2] {'c'}, dimensions={0}, use_global_device_ids=true | all-gather | bytes 1376256 | tf_op jit(solution)/shard_map/while/body/all_gather | solution.py:285
  165.5 3.1 %expert_f.1 = (bf16[64,3584]{1,0:T(8,128)(2,1)S(1)}, bf16[64,3584]{1,0:T(8,128)(2,1)S(1)}) custom-call(s32[1]{0:T(128)} %get-tuple-element.306.refs_0_, bf16[128,3584]{1,0:T(8,128)(2,1)S(1)} %all_gather.8.refs_1_, bf16[3584,512]{1,0:T(8,128)(2,1)} %get-tuple-element.307.refs_2_, bf16[256,3584]{1,0:T(8,128)(2,1)} %get-tuple-element.308.refs_3_), custom_call_target="tpu_custom_call" | custom-call | flops 704643072 | bytes 7340036 | tf_op jit(solution)/shard_map/while/body/expert_f/pallas_call | solution.py:265
  168.6 2.0 collective-permute-start
  170.7 1.7 collective-permute-done.refs_1_
  172.4 0.1 add_f.1
  172.5 1.7 spread_f.1
  174.2 16.5 %all-to-all-start = ((bf16[16,8,1792]{2,1,0:T(8,128)(2,1)}), bf16[16,8,1792]{2,1,0:T(8,128)(2,1)S(1)}, u32[]{:S(2)}, u32[]{:S(2)}) async-start(bf16[16,8,1792]{2,1,0:T(8,128)(2,1)} %bitcast.12), calls=%async_computation | async-start | bytes 917504 | tf_op jit(solution)/shard_map/all_to_all | solution.py:306
  190.7 0.0 collective-permute-done.10.refs_1_
  190.7 0.0 collective-permute-done.11.refs_2_
  190.7 0.0 collective-permute-done.12.refs_3_
  190.7 0.0 copy-start.1
  190.8 0.2 merge_b.1
  191.0 5.0 %collective-permute-start.13 = (bf16[8,3584]{1,0:T(8,128)(2,1)S(1)}, bf16[8,3584]{1,0:T(8,128)(2,1)S(1)}, u32[]{:S(2)}, u32[]{:S(2)}) collective-permute-start(bf16[8,3584]{1,0:T(8,128)(2,1)S(1)} %get-tuple-element.129), channel_id=1, source_target_pairs={{0,24},{8,0},{16,8},{24,16},{1,25},{9,1},{17,9},{25,17},{2,26},{10... | collective-permute-start | bytes 172040 | tf_op jit(solution)/shard_map/ppermute | solution.py:281
  196.0 2.8 %collective-permute-start.14 = (bf16[8,3584]{1,0:T(8,128)(2,1)S(1)}, bf16[8,3584]{1,0:T(8,128)(2,1)S(1)}, u32[]{:S(2)}, u32[]{:S(2)}) collective-permute-start(bf16[8,3584]{1,0:T(8,128)(2,1)S(1)} %get-tuple-element.130), channel_id=1, source_target_pairs={{0,16},{8,24},{16,0},{24,8},{1,17},{9,25},{17,1},{25,9},{2,18},{10... | collective-permute-start | bytes 172040 | tf_op jit(solution)/shard_map/ppermute | solution.py:281
  198.8 2.8 %collective-permute-start.15 = (bf16[8,3584]{1,0:T(8,128)(2,1)S(1)}, bf16[8,3584]{1,0:T(8,128)(2,1)S(1)}, u32[]{:S(2)}, u32[]{:S(2)}) collective-permute-start(bf16[8,3584]{1,0:T(8,128)(2,1)S(1)} %get-tuple-element.131), channel_id=1, source_target_pairs={{0,8},{8,16},{16,24},{24,0},{1,9},{9,17},{17,25},{25,1},{2,10},{10... | collective-permute-start | bytes 172040 | tf_op jit(solution)/shard_map/ppermute | solution.py:281
  201.6 0.0 collective-permute-done.13.refs_4_
  201.6 2.4 collective-permute-done.14.refs_5_
  203.9 2.1 collective-permute-done.15.refs_6_
  206.1 1.0 final_b.1
  207.1 1.9 collective-permute-start.16
  209.0 17.4 %collective-permute-done.16 = bf16[64,3584]{1,0:T(8,128)(2,1)S(1)} collective-permute-done((bf16[64,3584]{1,0:T(8,128)(2,1)S(1)}, bf16[64,3584]{1,0:T(8,128)(2,1)S(1)}, u32[]{:S(2)}, u32[]{:S(2)}) %collective-permute-start.16) | collective-permute-done | bytes 458784 | tf_op jit(solution)/shard_map/ppermute | solution.py:281
  226.4 15.8 %all-to-all-done = bf16[16,8,1792]{2,1,0:T(8,128)(2,1)S(1)} async-done(((bf16[16,8,1792]{2,1,0:T(8,128)(2,1)}), bf16[16,8,1792]{2,1,0:T(8,128)(2,1)S(1)}, u32[]{:S(2)}, u32[]{:S(2)}) %all-to-all-start) | async-done | bytes 458784 | tf_op jit(solution)/shard_map/all_to_all | solution.py:306
  242.3 1.3 final_f.1
  243.5 0.8 copy.34
  (8 shorter events, 0.0 us)
Async XLA Ops:
  2.0 35.7 %collective-permute-start.3 = (f32[2,64]{1,0:T(2,128)S(1)}, f32[2,64]{1,0:T(2,128)S(1)}, u32[]{:S(2)}, u32[]{:S(2)}) collective-permute-start(f32[2,64]{1,0:T(2,128)S(1)} %pad_maximum_fusion), channel_id=1, source_target_pairs={{0,32},{32,64},{64,96},{96,128},{128,160},{160,192},{192,224},{224... | collective-permute-start | bytes 1544 | tf_op jit(solution)/shard_map/ppermute | solution.py:281
  5.8 31.9 %collective-permute-start.2 = (bf16[64,3584]{1,0:T(8,128)(2,1)}, bf16[64,3584]{1,0:T(8,128)(2,1)S(1)}, u32[]{:S(2)}, u32[]{:S(2)}) collective-permute-start(bf16[64,3584]{1,0:T(8,128)(2,1)} %bitcast.34), channel_id=1, source_target_pairs={{0,32},{32,64},{64,96},{96,128},{128,160},{160,192},{192,224},{224... | collective-permute-start | bytes 1376264 | tf_op jit(solution)/shard_map/ppermute | solution.py:281
  9.6 1.0 copy-start
  10.6 0.7 copy-start.2
  11.3 0.7 copy-start.4
  13.2 87.7 %all-to-all-start.1 = ((bf16[16,8,1792]{2,1,0:T(8,128)(2,1)}), bf16[16,8,1792]{2,1,0:T(8,128)(2,1)S(1)}, u32[]{:S(2)}, u32[]{:S(2)}) async-start(bf16[16,8,1792]{2,1,0:T(8,128)(2,1)} %bitcast.15), calls=%async_computation.1 | async-start | bytes 917504 | tf_op jit(solution)/shard_map/all_to_all | solution.py:306
  37.6 12.7 %copy-start.3 = (s32[1,64,1]{1,2,0:T(1,128)S(1)}, s32[1,64,1]{1,2,0:T(1,128)}, u32[]{:S(2)}) copy-start(s32[1,64,1]{1,2,0:T(1,128)} %param.17) | copy-start | bytes 772
  37.6 63.3 %copy-start.5 = (bf16[1,1,128,512]{3,2,1,0:T(8,128)(2,1)S(1)}, bf16[1,1,128,512]{3,2,1,0:T(8,128)(2,1)}, u32[]{:S(2)}) copy-start(bf16[1,1,128,512]{3,2,1,0:T(8,128)(2,1)} %param.19) | copy-start | bytes 393220
  38.5 13.0 %collective-permute-start.4 = (bf16[8,3584]{1,0:T(8,128)(2,1)S(1)}, bf16[8,3584]{1,0:T(8,128)(2,1)S(1)}, u32[]{:S(2)}, u32[]{:S(2)}) collective-permute-start(bf16[8,3584]{1,0:T(8,128)(2,1)S(1)} %get-tuple-element.114), channel_id=1, source_target_pairs={{0,8},{8,16},{16,24},{24,0},{1,9},{9,17},{17,25},{25,1},{2,10},{10... | collective-permute-start | bytes 172040 | tf_op jit(solution)/shard_map/ppermute | solution.py:281
  42.4 9.2 %collective-permute-start.5 = (bf16[8,3584]{1,0:T(8,128)(2,1)S(1)}, bf16[8,3584]{1,0:T(8,128)(2,1)S(1)}, u32[]{:S(2)}, u32[]{:S(2)}) collective-permute-start(bf16[8,3584]{1,0:T(8,128)(2,1)S(1)} %get-tuple-element.115), channel_id=1, source_target_pairs={{0,16},{8,24},{16,0},{24,8},{1,17},{9,25},{17,1},{25,9},{2,18},{10... | collective-permute-start | bytes 172040 | tf_op jit(solution)/shard_map/ppermute | solution.py:281
  46.9 6.1 %collective-permute-start.6 = (bf16[8,3584]{1,0:T(8,128)(2,1)S(1)}, bf16[8,3584]{1,0:T(8,128)(2,1)S(1)}, u32[]{:S(2)}, u32[]{:S(2)}) collective-permute-start(bf16[8,3584]{1,0:T(8,128)(2,1)S(1)} %get-tuple-element.116), channel_id=1, source_target_pairs={{0,24},{8,0},{16,8},{24,16},{1,25},{9,1},{17,9},{25,17},{2,26},{10... | collective-permute-start | bytes 172040 | tf_op jit(solution)/shard_map/ppermute | solution.py:281
  53.2 109.7 %collective-permute-start.9 = (bf16[16,3584]{1,0:T(8,128)(2,1)S(1)}, bf16[16,3584]{1,0:T(8,128)(2,1)S(1)}, u32[]{:S(2)}, u32[]{:S(2)}) collective-permute-start(bf16[16,3584]{1,0:T(8,128)(2,1)S(1)} %get-tuple-element.118), channel_id=1, source_target_pairs={{0,4},{2,6},{4,0},{6,2},{1,5},{3,7},{5,1},{7,3},{8,12},{10,14},{12... | collective-permute-start | bytes 344072 | tf_op jit(solution)/shard_map/ppermute | solution.py:281
  75.3 87.6 %collective-permute-start.8 = (bf16[16,3584]{1,0:T(8,128)(2,1)S(1)}, bf16[16,3584]{1,0:T(8,128)(2,1)S(1)}, u32[]{:S(2)}, u32[]{:S(2)}) collective-permute-start(bf16[16,3584]{1,0:T(8,128)(2,1)S(1)} %get-tuple-element.118), channel_id=1, source_target_pairs={{0,6},{2,4},{4,2},{6,0},{1,7},{3,5},{5,3},{7,1},{8,14},{10,12},{12... | collective-permute-start | bytes 344072 | tf_op jit(solution)/shard_map/ppermute | solution.py:281
  77.4 73.4 %collective-permute-start.7 = (bf16[16,3584]{1,0:T(8,128)(2,1)S(1)}, bf16[16,3584]{1,0:T(8,128)(2,1)S(1)}, u32[]{:S(2)}, u32[]{:S(2)}) collective-permute-start(bf16[16,3584]{1,0:T(8,128)(2,1)S(1)} %get-tuple-element.281), channel_id=1, source_target_pairs={{0,2},{2,0},{4,6},{6,4},{1,3},{3,1},{5,7},{7,5},{8,10},{10,8},{12,... | collective-permute-start | bytes 344072 | tf_op jit(solution)/shard_map/ppermute | solution.py:281
  109.1 3.7 %collective-permute-start.1 = (bf16[128,1792]{1,0:T(8,128)(2,1)S(1)}, bf16[128,1792]{1,0:T(8,128)(2,1)S(1)}, u32[]{:S(2)}, u32[]{:S(2)}) collective-permute-start(bf16[128,1792]{1,0:T(8,128)(2,1)S(1)} %get-tuple-element.278), channel_id=1, source_target_pairs={{0,1},{1,0},{2,3},{3,2},{4,5},{5,4},{6,7},{7,6},{8,9},{9,8},{10,11... | collective-permute-start | bytes 1376264 | tf_op jit(solution)/shard_map/while/body/ppermute | solution.py:281
  113.9 76.8 %collective-permute-start.10 = (bf16[16,3584]{1,0:T(8,128)(2,1)S(1)}, bf16[16,3584]{1,0:T(8,128)(2,1)S(1)}, u32[]{:S(2)}, u32[]{:S(2)}) collective-permute-start(bf16[16,3584]{1,0:T(8,128)(2,1)S(1)} %get-tuple-element.125), channel_id=1, source_target_pairs={{0,2},{2,0},{4,6},{6,4},{1,3},{3,1},{5,7},{7,5},{8,10},{10,8},{12,... | collective-permute-start | bytes 344072 | tf_op jit(solution)/shard_map/ppermute | solution.py:281
  148.9 41.8 %collective-permute-start.11 = (bf16[16,3584]{1,0:T(8,128)(2,1)S(1)}, bf16[16,3584]{1,0:T(8,128)(2,1)S(1)}, u32[]{:S(2)}, u32[]{:S(2)}) collective-permute-start(bf16[16,3584]{1,0:T(8,128)(2,1)S(1)} %get-tuple-element.126), channel_id=1, source_target_pairs={{0,6},{2,4},{4,2},{6,0},{1,7},{3,5},{5,3},{7,1},{8,14},{10,12},{12... | collective-permute-start | bytes 344072 | tf_op jit(solution)/shard_map/ppermute | solution.py:281
  150.9 39.9 %collective-permute-start.12 = (bf16[16,3584]{1,0:T(8,128)(2,1)S(1)}, bf16[16,3584]{1,0:T(8,128)(2,1)S(1)}, u32[]{:S(2)}, u32[]{:S(2)}) collective-permute-start(bf16[16,3584]{1,0:T(8,128)(2,1)S(1)} %get-tuple-element.127), channel_id=1, source_target_pairs={{0,4},{2,6},{4,0},{6,2},{1,5},{3,7},{5,1},{7,3},{8,12},{10,14},{12... | collective-permute-start | bytes 344072 | tf_op jit(solution)/shard_map/ppermute | solution.py:281
  168.6 3.7 %collective-permute-start = (bf16[64,3584]{1,0:T(8,128)(2,1)S(1)}, bf16[64,3584]{1,0:T(8,128)(2,1)S(1)}, u32[]{:S(2)}, u32[]{:S(2)}) collective-permute-start(bf16[64,3584]{1,0:T(8,128)(2,1)S(1)} %get-tuple-element.266), channel_id=1, source_target_pairs={{0,1},{1,0},{2,3},{3,2},{4,5},{5,4},{6,7},{7,6},{8,9},{9,8},{10,11... | collective-permute-start | bytes 1376264 | tf_op jit(solution)/shard_map/while/body/ppermute | solution.py:281
  174.2 68.1 %all-to-all-start = ((bf16[16,8,1792]{2,1,0:T(8,128)(2,1)}), bf16[16,8,1792]{2,1,0:T(8,128)(2,1)S(1)}, u32[]{:S(2)}, u32[]{:S(2)}) async-start(bf16[16,8,1792]{2,1,0:T(8,128)(2,1)} %bitcast.12), calls=%async_computation | async-start | bytes 917504 | tf_op jit(solution)/shard_map/all_to_all | solution.py:306
  190.7 15.3 %copy-start.1 = (bf16[1,64,3584]{2,1,0:T(8,128)(2,1)S(1)}, bf16[1,64,3584]{2,1,0:T(8,128)(2,1)}, u32[]{:S(2)}) copy-start(bf16[1,64,3584]{2,1,0:T(8,128)(2,1)} %param.16) | copy-start | bytes 1376260
  191.0 10.6 %collective-permute-start.13 = (bf16[8,3584]{1,0:T(8,128)(2,1)S(1)}, bf16[8,3584]{1,0:T(8,128)(2,1)S(1)}, u32[]{:S(2)}, u32[]{:S(2)}) collective-permute-start(bf16[8,3584]{1,0:T(8,128)(2,1)S(1)} %get-tuple-element.129), channel_id=1, source_target_pairs={{0,24},{8,0},{16,8},{24,16},{1,25},{9,1},{17,9},{25,17},{2,26},{10... | collective-permute-start | bytes 172040 | tf_op jit(solution)/shard_map/ppermute | solution.py:281
  196.0 7.9 %collective-permute-start.14 = (bf16[8,3584]{1,0:T(8,128)(2,1)S(1)}, bf16[8,3584]{1,0:T(8,128)(2,1)S(1)}, u32[]{:S(2)}, u32[]{:S(2)}) collective-permute-start(bf16[8,3584]{1,0:T(8,128)(2,1)S(1)} %get-tuple-element.130), channel_id=1, source_target_pairs={{0,16},{8,24},{16,0},{24,8},{1,17},{9,25},{17,1},{25,9},{2,18},{10... | collective-permute-start | bytes 172040 | tf_op jit(solution)/shard_map/ppermute | solution.py:281
  198.8 7.3 %collective-permute-start.15 = (bf16[8,3584]{1,0:T(8,128)(2,1)S(1)}, bf16[8,3584]{1,0:T(8,128)(2,1)S(1)}, u32[]{:S(2)}, u32[]{:S(2)}) collective-permute-start(bf16[8,3584]{1,0:T(8,128)(2,1)S(1)} %get-tuple-element.131), channel_id=1, source_target_pairs={{0,8},{8,16},{16,24},{24,0},{1,9},{9,17},{17,25},{25,1},{2,10},{10... | collective-permute-start | bytes 172040 | tf_op jit(solution)/shard_map/ppermute | solution.py:281
  207.1 19.4 %collective-permute-start.16 = (bf16[64,3584]{1,0:T(8,128)(2,1)S(1)}, bf16[64,3584]{1,0:T(8,128)(2,1)S(1)}, u32[]{:S(2)}, u32[]{:S(2)}) collective-permute-start(bf16[64,3584]{1,0:T(8,128)(2,1)S(1)} %final_b.1), channel_id=1, source_target_pairs={{0,992},{32,0},{64,32},{96,64},{128,96},{160,128},{192,160},{224,1... | collective-permute-start | bytes 1376264 | tf_op jit(solution)/shard_map/ppermute | solution.py:281
